TPU v7x, 256 devices: a whole 4x4x8 slice. The times are simulated.
256 devices in a mesh: section: 32 (over z, y_lo, core), dp: 8 (over x, y_hi).
Axes of the slice: x: 4, y: 4 (y_hi: 2, y_lo: 2; y = y_hi * 2 + y_lo), z: 8, core: 2. Of those that a mesh axis runs over, the one named last changes fastest.
Arguments:
- handoff: bfloat16 [32, 2048, 4096], P('section', 'dp'), may hold values from -6 to 6
- grad_back: bfloat16 [32, 2048, 4096], P('section', 'dp'), may hold values from -0.75 to 0.75
- w_in: bfloat16 [32, 4096, 512], P('section', 'dp'), may hold values from -0.09375 to 0.09375
- w_out: bfloat16 [32, 4096, 512], P('section', 'dp'), may hold values from -0.25 to 0.25
Outputs:
- layer_out: bfloat16 [32, 2048, 4096], P('section', 'dp')
- shadow_out: bfloat16 [32, 2048, 4096], P('section', 'dp')
- input_grad: bfloat16 [32, 2048, 4096], P('section', 'dp')
- grad_w_in: float32 [32, 4096, 512], P('section', 'dp')
- grad_w_out: float32 [32, 4096, 512], P('section', 'dp')
All inputs are finite; a program needn't handle non-finite values.
Results may differ from a plain program's by a relative error of at most 0.015.
Values may be sent and summed in bfloat16 or wider, within the bound.
No kernel may reach another device: no remote copies, remote signals or barrier semaphores. Data moves between devices by JAX's collectives and lax.ppermute only.
A program may use at most 128 MiB of HBM per device.

v0:
```python
import jax
import jax.numpy as jnp
from jax import lax
from jax.sharding import PartitionSpec as P

INV_ROOT_TWO = 0.7071067811865476
INV_ROOT_TWO_PI = 0.3989422804014327


def from_behind(array, axis, by):
    devices = lax.axis_size(axis)
    return lax.ppermute(array, axis, [(i, (i + by) % devices) for i in range(devices)])


def gelu_pair(preact):
    normal_cdf = 0.5 * (1.0 + lax.erf(preact * INV_ROOT_TWO))
    density = jnp.exp(-0.5 * preact * preact) * INV_ROOT_TWO_PI
    return (preact * normal_cdf, normal_cdf + preact * density)


def apply_layer(inputs, weight_in, weight_out):
    preact = jnp.dot(inputs, weight_in, preferred_element_type=jnp.float32)
    activated, unused_slope = gelu_pair(preact)
    hidden = activated.astype(jnp.bfloat16)
    branch = lax.dot_general(
        hidden, weight_out, (((1,), (1,)), ((), ())), preferred_element_type=jnp.float32
    )
    output = (inputs.astype(jnp.float32) + branch).astype(jnp.bfloat16)
    return (preact, hidden, output)


def contract_tokens(left, right):
    return lax.dot_general(
        left, right, (((0,), (0,)), ((), ())), preferred_element_type=jnp.float32
    )


def on_device(handoff, grad_back, w_in, w_out):
    inputs = from_behind(handoff, "section", 1)[0]
    upstream = from_behind(grad_back, "section", -1)[0]
    full_in, full_out = (
        lax.all_gather(w_in, "dp", axis=1, tiled=True),
        lax.all_gather(w_out, "dp", axis=1, tiled=True),
    )
    weight_in = full_in[0]
    weight_out = full_out[0]
    preact, hidden, output = apply_layer(inputs, weight_in, weight_out)
    moved_in, moved_out = from_behind((w_in, w_out), "section", -1)
    next_in, next_out = (
        lax.all_gather(moved_in, "dp", axis=1, tiled=True),
        lax.all_gather(moved_out, "dp", axis=1, tiled=True),
    )
    shadow = apply_layer(output, next_in[0], next_out[0])[2]
    dhidden = jnp.dot(upstream, weight_out, preferred_element_type=jnp.float32)
    unused_value, slope = gelu_pair(preact)
    dpre = (dhidden * slope).astype(jnp.bfloat16)
    back = lax.dot_general(
        dpre, weight_in, (((1,), (1,)), ((), ())), preferred_element_type=jnp.float32
    )
    input_grad = (upstream.astype(jnp.float32) + back).astype(jnp.bfloat16)
    hidden_width = weight_in.shape[1]
    summed = lax.psum_scatter(
        jnp.concatenate(
            [contract_tokens(inputs, dpre), contract_tokens(upstream, hidden)], axis=1
        ).astype(jnp.bfloat16),
        "dp",
        scatter_dimension=0,
        tiled=True,
    ).astype(jnp.float32)
    grad_in = summed[:, :hidden_width]
    grad_out = summed[:, hidden_width:]
    return (output[None], shadow[None], input_grad[None], grad_in[None], grad_out[None])


def solution(mesh):
    in_specs = (
        P("section", "dp", None),
        P("section", "dp", None),
        P("section", "dp", None),
        P("section", "dp", None),
    )
    out_specs = (
        P("section", "dp", None),
        P("section", "dp", None),
        P("section", "dp", None),
        P("section", "dp", None),
        P("section", "dp", None),
    )
    return jax.shard_map(
        on_device, mesh=mesh, in_specs=in_specs, out_specs=out_specs, check_vma=False
    )
```

profile of v0, /device:TPU:1, one launch (start us, length us, event | category | flops | bytes accessed | tf_op | source)
XLA Modules:
  0.0 484.0 jit_solution(10092098057953482137)
XLA Ops:
  7.2 0.0 all-gather.5.cloned.1.call-start
  7.2 0.7 all-gather.5.cloned.1.call-update
  7.9 0.0 all-gather.7.cloned.1.call-start
  7.9 0.7 all-gather.7.cloned.1.call-update
  8.6 0.0 all-gather.9.cloned.1.call-start
  8.7 3.3 collective-permute-start.1
  12.0 6.5 %collective-permute-done.1 = bf16[1,512,512]{2,1,0:T(8,128)(2,1)S(1)} collective-permute-done((bf16[1,512,512]{2,1,0:T(8,128)(2,1)}, bf16[1,512,512]{2,1,0:T(8,128)(2,1)S(1)}, u32[]{:S(2)}, u32[]{:S(2)}) %collective-permute-start.1) | collective-permute-done | bytes 524320 | tf_op jit(solution)/shard_map/ppermute | solution.py:12
  18.5 0.0 copy-start.2
  18.5 0.8 copy-done.2
  19.3 0.0 all-gather.9.cloned.1.call-update
  19.4 0.0 all-gather.11.cloned.1.call-start
  19.4 5.1 %collective-permute-start.2 = (bf16[1,512,512]{2,1,0:T(8,128)(2,1)}, bf16[1,512,512]{2,1,0:T(8,128)(2,1)S(1)}, u32[]{:S(2)}, u32[]{:S(2)}) collective-permute-start(bf16[1,512,512]{2,1,0:T(8,128)(2,1)} %param.7), channel_id=1, source_target_pairs={{0,248},{8,0},{16,8},{24,16},{32,24},{40,32},{48,40},{56,48},{64,5... | collective-permute-start | bytes 1572872 | tf_op jit(solution)/shard_map/ppermute | solution.py:12
  24.5 3.8 collective-permute-done.2
  28.3 0.0 copy-start.3
  28.3 0.8 copy-done.3
  29.1 0.0 all-gather.11.cloned.1.call-update
  29.1 0.0 reduce-scatter.2.cloned.1.call-start
  29.2 0.1 collective-permute-start
  29.3 7.5 %collective-permute-start.3 = (bf16[1,256,4096]{2,1,0:T(8,128)(2,1)}, bf16[1,256,4096]{2,1,0:T(8,128)(2,1)}, u32[]{:S(2)}, u32[]{:S(2)}) collective-permute-start(bf16[1,256,4096]{2,1,0:T(8,128)(2,1)} %param.5), channel_id=1, source_target_pairs={{0,248},{8,0},{16,8},{24,16},{32,24},{40,32},{48,40},{56,48},{64,5... | collective-permute-start | bytes 6291464 | tf_op jit(solution)/shard_map/ppermute | solution.py:12
  36.7 43.3 %collective-permute-done = bf16[1,256,4096]{2,1,0:T(8,128)(2,1)S(1)} collective-permute-done((bf16[1,256,4096]{2,1,0:T(8,128)(2,1)}, bf16[1,256,4096]{2,1,0:T(8,128)(2,1)S(1)}, u32[]{:S(2)}, u32[]{:S(2)}) %collective-permute-start) | collective-permute-done | bytes 2097184 | tf_op jit(solution)/shard_map/ppermute | solution.py:12
  80.0 37.1 %all-gather.5.cloned.1.call-done = bf16[1,4096,512]{2,1,0:T(8,128)(2,1)} async-done(((bf16[1,512,512]{2,1,0:T(8,128)(2,1)}), bf16[1,4096,512]{2,1,0:T(8,128)(2,1)}) %all-gather.5.cloned.1.call-update) | async-done | bytes 4194320 | tf_op jit(solution)/shard_map/all_gather | solution.py:42
  117.2 3.4 fusion.12
  120.6 0.0 collective-permute-done.3
  120.6 75.1 %all-gather.7.cloned.1.call-done = bf16[1,4096,512]{2,1,0:T(8,128)(2,1)} async-done(((bf16[1,512,512]{2,1,0:T(8,128)(2,1)}), bf16[1,4096,512]{2,1,0:T(8,128)(2,1)}) %all-gather.7.cloned.1.call-update) | async-done | bytes 4194320 | tf_op jit(solution)/shard_map/all_gather | solution.py:43
  195.6 4.1 fusion.25
  199.8 3.2 fusion
  203.0 4.9 %fusion.1 = bf16[4096,512]{0,1:T(8,128)(2,1)} fusion(bf16[1,256,4096]{2,1,0:T(8,128)(2,1)} %collective-permute-done.3, f32[256,512]{1,0:T(8,128)S(1)} %fusion.12), kind=kOutput, calls=%fused_computation.4 | convolution fusion | flops 1076494336 | bytes 6815744 | tf_op jit(solution)/shard_map/dot_general | solution.py:33
  207.9 8.3 %pad_maximum_fusion = bf16[4096,1024]{0,1:T(8,128)(2,1)} fusion(bf16[4096,512]{0,1:T(8,128)(2,1)} %fusion.1, bf16[4096,512]{0,1:T(8,128)(2,1)} %fusion), kind=kLoop, calls=%fused_computation | loop fusion | flops 16777216 | bytes 16777216 | tf_op jit(solution)/shard_map/concatenate | solution.py:63
  216.1 0.0 reduce-scatter.2.cloned.1.call-update
  216.2 0.0 copy-start.1
  216.2 3.6 fusion.8
  219.8 0.0 copy-done.1
  219.8 0.0 copy-start
  219.8 5.9 %fusion.15 = bf16[1,256,4096]{2,1,0:T(8,128)(2,1)} fusion(bf16[1,256,4096]{2,1,0:T(8,128)(2,1)} %collective-permute-done.3, bf16[256,512]{1,0:T(8,128)(2,1)S(1)} %fusion.25, bf16[1,4096,512]{2,1,0:T(8,128)(2,1)S(1)} %copy-done.1), kind=kOutput, calls=%fused_computation.21 | convolution fusion | flops 1076887552 | bytes 8650752 | tf_op jit(solution)/shard_map/dot_general | solution.py:57
  225.7 0.0 copy-done
  225.7 1.9 fusion.48
  227.7 45.8 %all-gather.9.cloned.1.call-done = bf16[1,4096,512]{2,1,0:T(8,128)(2,1)} async-done(((bf16[1,512,512]{2,1,0:T(8,128)(2,1)}), bf16[1,4096,512]{2,1,0:T(8,128)(2,1)}) %all-gather.9.cloned.1.call-update) | async-done | bytes 4194320 | tf_op jit(solution)/shard_map/all_gather | solution.py:50
  273.5 77.7 %all-gather.11.cloned.1.call-done = bf16[1,4096,512]{2,1,0:T(8,128)(2,1)} async-done(((bf16[1,512,512]{2,1,0:T(8,128)(2,1)}), bf16[1,4096,512]{2,1,0:T(8,128)(2,1)}) %all-gather.11.cloned.1.call-update) | async-done | bytes 4194320 | tf_op jit(solution)/shard_map/all_gather | solution.py:51
  351.2 9.6 %fusion.14 = bf16[1,256,4096]{2,1,0:T(8,128)(2,1)} fusion(bf16[1,4096,512]{2,1,0:T(8,128)(2,1)} %all-gather.11.cloned.1.call-done, bf16[1,4096,512]{2,1,0:T(8,128)(2,1)} %all-gather.9.cloned.1.call-done, f32[256,4096]{1,0:T(8,128)} %copy-done, bf16[1,256,4096]{2,1,0:T(8,128)(2,1)S(1)} %collective-permute-done), kind=kOutput, calls=%fused_computation.20 | convolution fusion | flops 2157576192 | bytes 16777216 | tf_op jit(solution)/shard_map/dot_general | solution.py:25
  360.8 112.4 %reduce-scatter.2.cloned.1.call-done = bf16[512,1024]{0,1:T(8,128)(2,1)} async-done(((bf16[4096,1024]{0,1:T(8,128)(2,1)}), bf16[512,1024]{0,1:T(8,128)(2,1)}) %reduce-scatter.2.cloned.1.call-update) | async-done | bytes 1048592 | tf_op jit(solution)/shard_map/reduce_scatter | solution.py:62
  473.2 1.5 convert_element_type.40
  474.7 0.2 slice_bitcast_fusion
  474.9 1.3 copy.10
  476.2 1.3 copy.9
Async XLA Ops:
  7.2 110.0 %all-gather.5.cloned.1.call-start = ((), (), s32[]{:S(2)}) async-start(), calls=%async_computation.1 | async-start | bytes 4718592 | tf_op jit(solution)/shard_map/all_gather | solution.py:42
  7.9 187.7 %all-gather.7.cloned.1.call-start = ((), (), s32[]{:S(2)}) async-start(), calls=%async_computation.2 | async-start | bytes 4718592 | tf_op jit(solution)/shard_map/all_gather | solution.py:43
  8.6 264.8 %all-gather.9.cloned.1.call-start = ((), (), s32[]{:S(2)}) async-start(), calls=%async_computation.3 | async-start | bytes 4718592 | tf_op jit(solution)/shard_map/all_gather | solution.py:50
  8.7 9.8 %collective-permute-start.1 = (bf16[1,512,512]{2,1,0:T(8,128)(2,1)}, bf16[1,512,512]{2,1,0:T(8,128)(2,1)S(1)}, u32[]{:S(2)}, u32[]{:S(2)}) collective-permute-start(bf16[1,512,512]{2,1,0:T(8,128)(2,1)} %param.6), channel_id=1, source_target_pairs={{0,248},{8,0},{16,8},{24,16},{32,24},{40,32},{48,40},{56,48},{64,5... | collective-permute-start | bytes 1572872 | tf_op jit(solution)/shard_map/ppermute | solution.py:12
  18.5 0.8 copy-start.2
  19.4 331.8 %all-gather.11.cloned.1.call-start = ((), (), s32[]{:S(2)}) async-start(), calls=%async_computation.4 | async-start | bytes 4718592 | tf_op jit(solution)/shard_map/all_gather | solution.py:51
  19.4 8.9 %collective-permute-start.2 = (bf16[1,512,512]{2,1,0:T(8,128)(2,1)}, bf16[1,512,512]{2,1,0:T(8,128)(2,1)S(1)}, u32[]{:S(2)}, u32[]{:S(2)}) collective-permute-start(bf16[1,512,512]{2,1,0:T(8,128)(2,1)} %param.7), channel_id=1, source_target_pairs={{0,248},{8,0},{16,8},{24,16},{32,24},{40,32},{48,40},{56,48},{64,5... | collective-permute-start | bytes 1572872 | tf_op jit(solution)/shard_map/ppermute | solution.py:12
  28.3 0.8 copy-start.3
  29.1 444.1 %reduce-scatter.2.cloned.1.call-start = ((), (), s32[]{:S(2)}) async-start(), calls=%async_computation.5 | async-start | bytes 9437184 | tf_op jit(solution)/shard_map/reduce_scatter | solution.py:62
  29.2 50.9 %collective-permute-start = (bf16[1,256,4096]{2,1,0:T(8,128)(2,1)}, bf16[1,256,4096]{2,1,0:T(8,128)(2,1)S(1)}, u32[]{:S(2)}, u32[]{:S(2)}) collective-permute-start(bf16[1,256,4096]{2,1,0:T(8,128)(2,1)} %param.4), channel_id=1, source_target_pairs={{0,8},{8,16},{16,24},{24,32},{32,40},{40,48},{48,56},{56,64},{64,7... | collective-permute-start | bytes 6291464 | tf_op jit(solution)/shard_map/ppermute | solution.py:12
  29.3 91.3 %collective-permute-start.3 = (bf16[1,256,4096]{2,1,0:T(8,128)(2,1)}, bf16[1,256,4096]{2,1,0:T(8,128)(2,1)}, u32[]{:S(2)}, u32[]{:S(2)}) collective-permute-start(bf16[1,256,4096]{2,1,0:T(8,128)(2,1)} %param.5), channel_id=1, source_target_pairs={{0,248},{8,0},{16,8},{24,16},{32,24},{40,32},{48,40},{56,48},{64,5... | collective-permute-start | bytes 6291464 | tf_op jit(solution)/shard_map/ppermute | solution.py:12
  216.2 3.7 copy-start.1
  219.8 5.9 %copy-start = (f32[256,4096]{1,0:T(8,128)}, f32[256,4096]{1,0:T(8,128)S(1)}, u32[]{:S(2)}) copy-start(f32[256,4096]{1,0:T(8,128)S(1)} %fusion.8) | copy-start | bytes 12582916
Sparse Core Ops, SparseCore 0:
  10.6 106.4 all-gather.4
  119.8 75.8 all-gather.6
  198.8 74.6 all-gather.8
  276.5 74.6 all-gather.10
  355.2 117.9 reduce-scatter.1
where the time goes:
time: 484 us
  waiting for transfers between devices  403 us (83%)
  matrix products  34.8 us (7%)
  starting transfers between devices  16.2 us (3%)
  between operations  13.9 us (3%)
  other arithmetic  11.7 us (2%)
    reduce_scatter x1, waiting for transfers between devices, on_device(): lax.psum_scatter(jnp.concatenate([contract_tokens(inputs, dpre), contract...  112 us
    all_gather x1, waiting for transfers between devices, on_device(): lax.all_gather(moved_out, 'dp', axis=1, tiled=True)  77.7 us
    all_gather x1, waiting for transfers between devices, on_device(): lax.all_gather(w_out, 'dp', axis=1, tiled=True)  75.1 us
    ppermute x4, waiting for transfers between devices, from_behind(): lax.ppermute(array, axis, [(i, (i + by) % devices) for i in range(devices)])  53.6 us
    all_gather x1, waiting for transfers between devices, on_device(): lax.all_gather(moved_in, 'dp', axis=1, tiled=True)  45.8 us
    all_gather x1, waiting for transfers between devices, on_device(): lax.all_gather(w_in, 'dp', axis=1, tiled=True)  37.1 us
    ppermute x4, starting transfers between devices, from_behind(): lax.ppermute(array, axis, [(i, (i + by) % devices) for i in range(devices)])  16 us
    dot_general x2, matrix products, apply_layer(): lax.dot_general(hidden, weight_out, (((1,), (1,)), ((), ())), preferred_e...  13.3 us
  transfers between devices with their start and end apart: 9, of which 8 were waited for; matrix products, arithmetic and copies ran while one was open for 9% of the time, Pallas kernels for 0%

commit v1 on v0

v1 whole, which is shorter than its diff:
```python
import jax
import jax.numpy as jnp
from jax import lax
from jax.experimental import pallas as pl
from jax.experimental.pallas import tpu as pltpu
from jax.sharding import PartitionSpec as P

INV_ROOT_TWO = 0.7071067811865476
INV_ROOT_TWO_PI = 0.3989422804014327
X_SIZE = 4
Y_SIZE = 2
F32 = jnp.float32
BF16 = jnp.bfloat16


def over_section(array, by):
    devices = lax.axis_size("section")
    return lax.ppermute(
        array, "section", [(i, (i + by) % devices) for i in range(devices)]
    )


def over_x(array, by):
    pairs = []
    for x in range(X_SIZE):
        for y in range(Y_SIZE):
            pairs.append((x * Y_SIZE + y, ((x + by) % X_SIZE) * Y_SIZE + y))
    return lax.ppermute(array, "dp", pairs)


def swap_y(array):
    return lax.ppermute(array, "dp", [(i, i ^ 1) for i in range(X_SIZE * Y_SIZE)])


def gelu_pair(preact):
    normal_cdf = 0.5 * (1.0 + lax.erf(preact * INV_ROOT_TWO))
    density = jnp.exp(-0.5 * preact * preact) * INV_ROOT_TWO_PI
    return (preact * normal_cdf, normal_cdf + preact * density)


def times(left, right):
    return jnp.dot(left, right, preferred_element_type=F32)


def times_transposed(left, right):
    return lax.dot_general(
        left, right, (((1,), (1,)), ((), ())), preferred_element_type=F32
    )


def weight_views(refs):
    own, partner, behind, behind_partner, ahead, ahead_partner, far_in, far_out = refs
    views = []
    for ref in (own, partner, behind, behind_partner, ahead, ahead_partner):
        half = ref.shape[0] // 2
        views.append((ref.at[pl.ds(0, half)], ref.at[pl.ds(half, half)]))
    half = far_in.shape[0] // 2
    for part in range(2):
        rows = pl.ds(part * half, half)
        views.append((far_in.at[rows], far_out.at[rows]))
    return views


def columns_of(starts, block, width):
    return pl.ds(pl.multiple_of(starts[block], width), width)


def hidden_kernel(starts, inputs, upstream, *rest):
    views, packed = weight_views(rest[:8]), rest[8]
    rows, width = views[0][0].shape
    preact = dhidden = None
    for block, (up, down) in enumerate(views):
        columns = columns_of(starts, block, rows)
        first = times(inputs[:, columns], up[...])
        second = times(upstream[:, columns], down[...])
        preact = first if preact is None else preact + first
        dhidden = second if dhidden is None else dhidden + second
    activated, slope = gelu_pair(preact)
    packed[:, :width] = activated.astype(BF16)
    packed[:, width:] = (dhidden * slope).astype(BF16)


def outputs_kernel(starts, inputs, upstream, packed, *rest):
    views, (layer_out, input_grad) = weight_views(rest[:8]), rest[8:]
    rows, width = views[0][0].shape
    for block, (up, down) in enumerate(views):
        columns = columns_of(starts, block, rows)
        branch = times_transposed(packed[:, :width], down[...])
        layer_out[:, columns] = (inputs[:, columns].astype(F32) + branch).astype(BF16)
        back = times_transposed(packed[:, width:], up[...])
        input_grad[:, columns] = (upstream[:, columns].astype(F32) + back).astype(BF16)


def shadow_kernel(starts, inputs, *rest):
    views, shadow = weight_views(rest[:8]), rest[8]
    rows, width = views[0][0].shape
    preact = None
    for block, (up, down) in enumerate(views):
        first = times(inputs[:, columns_of(starts, block, rows)], up[...])
        preact = first if preact is None else preact + first
    hidden = gelu_pair(preact)[0].astype(BF16)
    for block, (up, down) in enumerate(views):
        columns = columns_of(starts, block, rows)
        branch = times_transposed(hidden, down[...])
        shadow[:, columns] = (inputs[:, columns].astype(F32) + branch).astype(BF16)


def local_call(kernel, outs, starts, *arrays, flops):
    in_specs = [pl.BlockSpec(memory_space=pltpu.SMEM)]
    in_specs += [pl.BlockSpec(memory_space=pltpu.VMEM)] * len(arrays)
    moved = sum(a.size * a.dtype.itemsize for a in arrays)
    return pl.pallas_call(
        kernel,
        out_shape=outs,
        in_specs=in_specs,
        out_specs=jax.tree.map(lambda o: pl.BlockSpec(memory_space=pltpu.VMEM), outs),
        compiler_params=pltpu.CompilerParams(vmem_limit_bytes=40 * 2**20),
        cost_estimate=pl.CostEstimate(
            flops=flops, bytes_accessed=moved, transcendentals=0
        ),
    )(starts, *arrays)


def contract_tokens(left, right):
    return lax.dot_general(
        left, right, (((0,), (0,)), ((), ())), preferred_element_type=F32
    )


def on_device(handoff, grad_back, w_in, w_out):
    position = lax.axis_index("dp")
    x, y = position // Y_SIZE, position % Y_SIZE
    rows, width = w_in.shape[1:]
    tokens, features = handoff.shape[1:]
    starts = jnp.stack(
        [
            (lax.rem(x + by, X_SIZE) * Y_SIZE + (y + j) % Y_SIZE) * rows
            for by in (0, 3, 1, 2)
            for j in range(Y_SIZE)
        ]
    ).astype(jnp.int32)

    inputs = over_section(handoff[0], 1)
    upstream = over_section(grad_back[0], -1)
    own = jnp.concatenate([w_in[0], w_out[0]], axis=0)
    partner = swap_y(own)
    behind, ahead = over_x(own, 1), over_x(own, -1)
    behind_partner, ahead_partner = over_x(partner, 1), over_x(partner, -1)
    far_in = over_x(jnp.concatenate([behind[:rows], behind_partner[:rows]]), 1)
    far_out = over_x(jnp.concatenate([ahead[rows:], ahead_partner[rows:]]), -1)
    weights = (
        own,
        partner,
        behind,
        behind_partner,
        ahead,
        ahead_partner,
        far_in,
        far_out,
    )
    matmul = 2 * tokens * features * width

    packed = local_call(
        hidden_kernel,
        jax.ShapeDtypeStruct((tokens, 2 * width), BF16),
        starts,
        inputs,
        upstream,
        *weights,
        flops=2 * matmul,
    )
    activations = jax.ShapeDtypeStruct((tokens, features), BF16)
    layer_out, input_grad = local_call(
        outputs_kernel,
        (activations, activations),
        starts,
        inputs,
        upstream,
        packed,
        *weights,
        flops=2 * matmul,
    )
    arrived = over_section(layer_out, 1)
    shadow_back = local_call(
        shadow_kernel, activations, starts, arrived, *weights, flops=2 * matmul
    )
    shadow = over_section(shadow_back, -1)

    wide = Y_SIZE * rows
    cut = lambda array, by: lax.dynamic_slice_in_dim(
        array, lax.rem(x + by, X_SIZE) * wide, wide, axis=1
    )
    pieces, hiddens = [], [packed]
    for by in range(X_SIZE):
        piece = jnp.concatenate([cut(inputs, by), cut(upstream, by)], axis=0)
        pieces.append(piece if by == 0 else over_x(piece, by))
        if by:
            hiddens.append(over_x(packed, by))
    left_in = jnp.concatenate([p[:tokens] for p in pieces])
    left_out = jnp.concatenate([p[tokens:] for p in pieces])
    right = jnp.concatenate(hiddens)
    part = jnp.concatenate(
        [
            contract_tokens(left_in, right[:, width:]),
            contract_tokens(left_out, right[:, :width]),
        ],
        axis=1,
    )
    mine = lax.dynamic_slice_in_dim(part, y * rows, rows, axis=0)
    theirs = lax.dynamic_slice_in_dim(part, (1 - y) * rows, rows, axis=0)
    summed = mine + swap_y(theirs.astype(BF16)).astype(F32)
    return (
        layer_out[None],
        shadow[None],
        input_grad[None],
        summed[None, :, :width],
        summed[None, :, width:],
    )


def solution(mesh):
    spec = P("section", "dp", None)
    return jax.shard_map(
        on_device,
        mesh=mesh,
        in_specs=(spec,) * 4,
        out_specs=(spec,) * 5,
        check_vma=False,
    )
```

time: 484 us -> 259 us (0.54)
  waiting for transfers between devices: 403 us -> 149 us
  starting transfers between devices: 16.2 us -> 59.1 us
  matrix products: 34.8 us -> 2.57 us
  local copies, waits for them, and re-layouts: 4.38 us -> 21.3 us
  Pallas kernels: 0 us -> 15.8 us
  between operations: 13.9 us -> 0.96 us
    all_gather x4 -> x0, waiting for transfers between devices: 236 us -> none  [the longest x1 77.7 us: on_device(): lax.all_gather(moved_out, 'dp', axis=1, tiled=True)]
    reduce_scatter x1 -> x0, waiting for transfers between devices: 112 us -> none  [on_device(): lax.psum_scatter(jnp.concatenate([contract_tokens(inputs, dpre), contract...]
    ppermute x4 -> x18, waiting for transfers between devices: 53.6 us -> 149 us  [the longest x2 84.9 us: swap_y(): lax.ppermute(array, 'dp', [(i, i ^ 1) for i in range(X_SIZE * Y_SIZE)])]
    ppermute x4 -> x18, starting transfers between devices: 16 us -> 59.1 us  [the longest x4 32.6 us: over_section(): lax.ppermute(array, 'section', [(i, (i + by) % devices) for i in range(de...]
    dot_general x5 -> x0, matrix products: 26.7 us -> none  [the longest x2 13.3 us: apply_layer(): lax.dot_general(hidden, weight_out, (((1,), (1,)), ((), ())), preferred_e...]
    pallas_call x0 -> x3, Pallas kernels: none -> 15.8 us  [local_call(): pl.pallas_call(kernel, out_shape=outs, in_specs=in_specs, out_specs=jax.t...]
    unnamed x10 -> x45, local copies, waits for them, and re-layouts: 4.21 us -> 13.7 us
    dot_general x2, matrix products: 8.09 us -> 2.57 us  [contract_tokens(): lax.dot_general(left, right, (((0,), (0,)), ((), ())), preferred_element_...]
  transfers between devices with their start and end apart: 9 -> 18, of which waited for: 8 -> 7; matrix products, arithmetic and copies ran while one was open for 9% -> 8% of each run, Pallas kernels for 0% -> 4%
where the time goes in v1:
time: 259 us; the launch traced here: 258 us
  waiting for transfers between devices  149 us (58%)
  starting transfers between devices  59.1 us (23%)
  local copies, waits for them, and re-layouts  21.3 us (8%)
  Pallas kernels  15.8 us (6%)
  other arithmetic  9 us (3%)
    ppermute x2, waiting for transfers between devices, swap_y(): lax.ppermute(array, 'dp', [(i, i ^ 1) for i in range(X_SIZE * Y_SIZE)])  84.9 us
    ppermute x12, waiting for transfers between devices, over_x(): return lax.ppermute(array, 'dp', pairs)  64.2 us
    ppermute x4, starting transfers between devices, over_section(): lax.ppermute(array, 'section', [(i, (i + by) % devices) for i in range(de...  32.6 us
    ppermute x12, starting transfers between devices, over_x(): return lax.ppermute(array, 'dp', pairs)  18.3 us
    pallas_call x3, Pallas kernels, local_call(): pl.pallas_call(kernel, out_shape=outs, in_specs=in_specs, out_specs=jax.t...  15.8 us
    unnamed x45, local copies, waits for them, and re-layouts  13.7 us
    ppermute x2, starting transfers between devices, swap_y(): lax.ppermute(array, 'dp', [(i, i ^ 1) for i in range(X_SIZE * Y_SIZE)])  8.12 us
  transfers between devices with their start and end apart: 18, of which 7 were waited for; matrix products, arithmetic and copies ran while one was open for 8% of the time, Pallas kernels for 4%

profile of v1, /device:TPU:1, one launch (start us, length us, event | category | flops | bytes accessed | tf_op | source)
XLA Modules:
  0.0 257.9 jit_solution(2489480455848985011)
XLA Ops:
  0.6 1.3 pad_maximum_fusion.1.rest_0_
  1.9 3.8 %collective-permute-start.2 = (bf16[1024,512]{1,0:T(8,128)(2,1)S(1)}, bf16[1024,512]{1,0:T(8,128)(2,1)S(1)}, u32[]{:S(2)}, u32[]{:S(2)}) collective-permute-start(bf16[1024,512]{1,0:T(8,128)(2,1)S(1)} %pad_maximum_fusion.1.rest_0_), channel_id=1, source_target_pairs={{0,1},{1,0},{2,3},{3,2},{4,5},{5,4},{6,7},{7,6},{8,9},{9,8},{10,11... | collective-permute-start | bytes 3145736 | tf_op jit(solution)/shard_map/ppermute | solution.py:32
  5.7 1.2 collective-permute-start.3
  6.9 1.2 collective-permute-start.1
  8.2 0.5 collective-permute-start
  8.7 1.5 collective-permute-start.5
  10.2 39.9 %collective-permute-done.2.rest_1_ = bf16[1024,512]{1,0:T(8,128)(2,1)S(1)} collective-permute-done((bf16[1024,512]{1,0:T(8,128)(2,1)S(1)}, bf16[1024,512]{1,0:T(8,128)(2,1)S(1)}, u32[]{:S(2)}, u32[]{:S(2)}) %collective-permute-start.2) | collective-permute-done | bytes 1048608 | tf_op jit(solution)/shard_map/ppermute | solution.py:32
  50.0 2.0 collective-permute-start.4
  52.0 1.4 collective-permute-start.6
  53.4 1.0 copy-done.12
  54.5 0.9 copy-done.3
  55.4 16.4 %collective-permute-done.4.rest_3_ = bf16[1024,512]{1,0:T(8,128)(2,1)S(1)} collective-permute-done((bf16[1024,512]{1,0:T(8,128)(2,1)S(1)}, bf16[1024,512]{1,0:T(8,128)(2,1)S(1)}, u32[]{:S(2)}, u32[]{:S(2)}) %collective-permute-start.4) | collective-permute-done | bytes 1048608 | tf_op jit(solution)/shard_map/ppermute | solution.py:28
  71.9 1.0 copy-done.6
  72.8 1.0 pad_maximum_fusion.2
  73.9 1.9 collective-permute-start.7
  75.8 1.0 copy-done.9
  76.8 1.0 pad_maximum_fusion.3
  77.9 1.6 collective-permute-start.8
  79.5 1.1 constant_dynamic-slice_fusion
  80.6 2.6 constant_dynamic-slice_fusion.7
  83.2 1.0 pad_maximum_fusion.4
  84.2 1.1 pad_maximum_fusion.5
  85.3 2.6 %collective-permute-start.12 = (bf16[512,1024]{1,0:T(8,128)(2,1)}, bf16[512,1024]{1,0:T(8,128)(2,1)}, u32[]{:S(2)}, u32[]{:S(2)}) collective-permute-start(bf16[512,1024]{1,0:T(8,128)(2,1)} %pad_maximum_fusion.5), channel_id=1, source_target_pairs={{0,4},{1,5},{2,6},{3,7},{4,0},{5,1},{6,2},{7,3},{8,12},{9,13},{10,... | collective-permute-start | bytes 3145736 | tf_op jit(solution)/shard_map/ppermute | solution.py:28
  87.9 8.1 %collective-permute-done.7.rest_6_ = bf16[1024,512]{1,0:T(8,128)(2,1)} collective-permute-done((bf16[1024,512]{1,0:T(8,128)(2,1)}, bf16[1024,512]{1,0:T(8,128)(2,1)}, u32[]{:S(2)}, u32[]{:S(2)}) %collective-permute-start.7) | collective-permute-done | bytes 1048608 | tf_op jit(solution)/shard_map/ppermute | solution.py:28
  96.0 2.8 %collective-permute-done.8.rest_7_ = bf16[1024,512]{1,0:T(8,128)(2,1)} collective-permute-done((bf16[1024,512]{1,0:T(8,128)(2,1)}, bf16[1024,512]{1,0:T(8,128)(2,1)}, u32[]{:S(2)}, u32[]{:S(2)}) %collective-permute-start.8) | collective-permute-done | bytes 1048608 | tf_op jit(solution)/shard_map/ppermute | solution.py:28
  98.8 4.6 %shard_map.83.packed = bf16[256,1024]{1,0:T(8,128)(2,1)S(1)} custom-call(s32[8]{0:T(128)S(1)} %stack.35.starts, bf16[256,4096]{1,0:T(8,128)(2,1)} %collective-permute-done.inputs, bf16[256,4096]{1,0:T(8,128)(2,1)S(1)} %collective-permute-done.1.upstream, bf16[1024,512]{1,0:T(8,128)(2,1)S(1)} %pad_maximum_fusion.1.rest_0_, bf16[1024,512]{1,0:T(8,128)(2,1)S(1)} %copy-done.13, ...), custom_call_target="tpu_custom_call" | custom-call | flops 2147483648 | bytes 12582912 | tf_op jit(solution)/shard_map/pallas_call | solution.py:112
  103.4 6.6 %shard_map.84 = (bf16[256,4096]{1,0:T(8,128)(2,1)}, bf16[256,4096]{1,0:T(8,128)(2,1)}) custom-call(s32[8]{0:T(128)S(1)} %stack.35.starts, bf16[256,4096]{1,0:T(8,128)(2,1)} %collective-permute-done.inputs, bf16[256,4096]{1,0:T(8,128)(2,1)S(1)} %collective-permute-done.1.upstream, bf16[256,1024]{1,0:T(8,128)(2,1)S(1)} %shard_map.83.packed, ...), custom_call_target="tpu_custom_call" | custom-call | flops 2147483648 | bytes 13107200 | tf_op jit(solution)/shard_map/pallas_call | solution.py:112
  110.0 30.6 %collective-permute-start.9 = (bf16[256,4096]{1,0:T(8,128)(2,1)}, bf16[256,4096]{1,0:T(8,128)(2,1)}, u32[]{:S(2)}, u32[]{:S(2)}) collective-permute-start(bf16[256,4096]{1,0:T(8,128)(2,1)} %get-tuple-element.7), channel_id=1, source_target_pairs={{0,8},{8,16},{16,24},{24,32},{32,40},{40,48},{48,56},{56,64},{64,7... | collective-permute-start | bytes 6291464 | tf_op jit(solution)/shard_map/ppermute | solution.py:18
  140.6 1.0 pad_maximum_fusion.6
  141.6 3.4 %collective-permute-start.13 = (bf16[512,1024]{1,0:T(8,128)(2,1)}, bf16[512,1024]{1,0:T(8,128)(2,1)S(1)}, u32[]{:S(2)}, u32[]{:S(2)}) collective-permute-start(bf16[512,1024]{1,0:T(8,128)(2,1)} %pad_maximum_fusion.6), channel_id=1, source_target_pairs={{0,6},{1,7},{2,0},{3,1},{4,2},{5,3},{6,4},{7,5},{8,14},{9,15},{10,... | collective-permute-start | bytes 3145736 | tf_op jit(solution)/shard_map/ppermute | solution.py:28
  145.1 1.2 collective-permute-start.15
  146.3 1.3 fusion.24
  147.5 1.6 collective-permute-start.16
  149.1 1.3 fusion.25
  150.4 29.3 %collective-permute-done.13 = bf16[512,1024]{1,0:T(8,128)(2,1)S(1)} collective-permute-done((bf16[512,1024]{1,0:T(8,128)(2,1)}, bf16[512,1024]{1,0:T(8,128)(2,1)S(1)}, u32[]{:S(2)}, u32[]{:S(2)}) %collective-permute-start.13) | collective-permute-done | bytes 1048608 | tf_op jit(solution)/shard_map/ppermute | solution.py:28
  179.8 7.7 %collective-permute-done.16 = bf16[256,1024]{1,0:T(8,128)(2,1)S(1)} collective-permute-done((bf16[256,1024]{1,0:T(8,128)(2,1)S(1)}, bf16[256,1024]{1,0:T(8,128)(2,1)S(1)}, u32[]{:S(2)}, u32[]{:S(2)}) %collective-permute-start.16) | collective-permute-done | bytes 524320 | tf_op jit(solution)/shard_map/ppermute | solution.py:28
  187.7 1.3 fusion.12
  189.8 0.8 copy-done.14
  190.7 4.6 %shard_map.85 = bf16[256,4096]{1,0:T(8,128)(2,1)S(1)} custom-call(s32[8]{0:T(128)S(1)} %stack.35.starts, bf16[256,4096]{1,0:T(8,128)(2,1)} %collective-permute-done.9.inputs, bf16[1024,512]{1,0:T(8,128)(2,1)S(1)} %pad_maximum_fusion.1.rest_0_, bf16[1024,512]{1,0:T(8,128)(2,1)S(1)} %copy-done.14, bf16[1024,512]{1,0:T(8,128)(2,1)S(1)} %copy-done.2, ...), custom_call_target="tpu_custom_call" | custom-call | flops 2147483648 | bytes 10485760 | tf_op jit(solution)/shard_map/pallas_call | solution.py:112
  195.6 1.3 fusion.4
  197.1 1.1 copy-done.18
  198.3 4.3 %collective-permute-start.17 = (bf16[512,1024]{0,1:T(8,128)(2,1)S(1)}, bf16[512,1024]{0,1:T(8,128)(2,1)}, u32[]{:S(2)}, u32[]{:S(2)}) collective-permute-start(bf16[512,1024]{0,1:T(8,128)(2,1)S(1)} %fusion.1), channel_id=1, source_target_pairs={{0,1},{1,0},{2,3},{3,2},{4,5},{5,4},{6,7},{7,6},{8,9},{9,8},{10,11... | collective-permute-start | bytes 3145736 | tf_op jit(solution)/shard_map/ppermute | solution.py:32
  202.5 45.0 %collective-permute-done.17 = bf16[512,1024]{0,1:T(8,128)(2,1)} collective-permute-done((bf16[512,1024]{0,1:T(8,128)(2,1)S(1)}, bf16[512,1024]{0,1:T(8,128)(2,1)}, u32[]{:S(2)}, u32[]{:S(2)}) %collective-permute-start.17) | collective-permute-done | bytes 1048608 | tf_op jit(solution)/shard_map/ppermute | solution.py:32
  247.6 2.2 fusion.3
  249.7 1.1 slice_bitcast_fusion
  250.9 2.5 copy.10
  253.4 1.3 copy.9
  254.7 3.1 %copy.12 = bf16[1,256,4096]{2,1,0:T(8,128)(2,1)} copy(bf16[1,256,4096]{2,1,0:T(8,128)(2,1)} %bitcast.13) | data formatting | bytes 4194304
  (58 shorter events, 1.8 us)
Async XLA Ops:
  1.9 48.1 %collective-permute-start.2 = (bf16[1024,512]{1,0:T(8,128)(2,1)S(1)}, bf16[1024,512]{1,0:T(8,128)(2,1)S(1)}, u32[]{:S(2)}, u32[]{:S(2)}) collective-permute-start(bf16[1024,512]{1,0:T(8,128)(2,1)S(1)} %pad_maximum_fusion.1.rest_0_), channel_id=1, source_target_pairs={{0,1},{1,0},{2,3},{3,2},{4,5},{5,4},{6,7},{7,6},{8,9},{9,8},{10,11... | collective-permute-start | bytes 3145736 | tf_op jit(solution)/shard_map/ppermute | solution.py:32
  5.7 46.3 %collective-permute-start.3 = (bf16[1024,512]{1,0:T(8,128)(2,1)S(1)}, bf16[1024,512]{1,0:T(8,128)(2,1)S(1)}, u32[]{:S(2)}, u32[]{:S(2)}) collective-permute-start(bf16[1024,512]{1,0:T(8,128)(2,1)S(1)} %pad_maximum_fusion.1.rest_0_), channel_id=1, source_target_pairs={{0,2},{1,3},{2,4},{3,5},{4,6},{5,7},{6,0},{7,1},{8,10},{9,11},{10,... | collective-permute-start | bytes 3145736 | tf_op jit(solution)/shard_map/ppermute | solution.py:28
  6.9 72.6 %collective-permute-start.1 = (bf16[256,4096]{1,0:T(8,128)(2,1)}, bf16[256,4096]{1,0:T(8,128)(2,1)S(1)}, u32[]{:S(2)}, u32[]{:S(2)}) collective-permute-start(bf16[256,4096]{1,0:T(8,128)(2,1)} %bitcast.9), channel_id=1, source_target_pairs={{0,248},{8,0},{16,8},{24,16},{32,24},{40,32},{48,40},{56,48},{64,5... | collective-permute-start | bytes 6291464 | tf_op jit(solution)/shard_map/ppermute | solution.py:18
  8.2 72.4 %collective-permute-start = (bf16[256,4096]{1,0:T(8,128)(2,1)}, bf16[256,4096]{1,0:T(8,128)(2,1)}, u32[]{:S(2)}, u32[]{:S(2)}) collective-permute-start(bf16[256,4096]{1,0:T(8,128)(2,1)} %bitcast.8), channel_id=1, source_target_pairs={{0,8},{8,16},{16,24},{24,32},{32,40},{40,48},{48,56},{56,64},{64,7... | collective-permute-start | bytes 6291464 | tf_op jit(solution)/shard_map/ppermute | solution.py:18
  8.7 45.7 %collective-permute-start.5 = (bf16[1024,512]{1,0:T(8,128)(2,1)S(1)}, bf16[1024,512]{1,0:T(8,128)(2,1)S(1)}, u32[]{:S(2)}, u32[]{:S(2)}) collective-permute-start(bf16[1024,512]{1,0:T(8,128)(2,1)S(1)} %pad_maximum_fusion.1.rest_0_), channel_id=1, source_target_pairs={{0,6},{1,7},{2,0},{3,1},{4,2},{5,3},{6,4},{7,5},{8,14},{9,15},{10,... | collective-permute-start | bytes 3145736 | tf_op jit(solution)/shard_map/ppermute | solution.py:28
  50.0 21.8 %collective-permute-start.4 = (bf16[1024,512]{1,0:T(8,128)(2,1)S(1)}, bf16[1024,512]{1,0:T(8,128)(2,1)S(1)}, u32[]{:S(2)}, u32[]{:S(2)}) collective-permute-start(bf16[1024,512]{1,0:T(8,128)(2,1)S(1)} %collective-permute-done.2.rest_1_), channel_id=1, source_target_pairs={{0,2},{1,3},{2,4},{3,5},{4,6},{5,7},{6,0},{7,1},{8,10},{9,11},{10,... | collective-permute-start | bytes 3145736 | tf_op jit(solution)/shard_map/ppermute | solution.py:28
  52.0 2.4 copy-start
  52.0 23.7 %collective-permute-start.6 = (bf16[1024,512]{1,0:T(8,128)(2,1)S(1)}, bf16[1024,512]{1,0:T(8,128)(2,1)S(1)}, u32[]{:S(2)}, u32[]{:S(2)}) collective-permute-start(bf16[1024,512]{1,0:T(8,128)(2,1)S(1)} %collective-permute-done.2.rest_1_), channel_id=1, source_target_pairs={{0,6},{1,7},{2,0},{3,1},{4,2},{5,3},{6,4},{7,5},{8,14},{9,15},{10,... | collective-permute-start | bytes 3145736 | tf_op jit(solution)/shard_map/ppermute | solution.py:28
  53.4 1.0 copy-start.12
  54.4 1.0 copy-start.3
  71.9 1.0 copy-start.6
  73.9 22.1 %collective-permute-start.7 = (bf16[1024,512]{1,0:T(8,128)(2,1)}, bf16[1024,512]{1,0:T(8,128)(2,1)}, u32[]{:S(2)}, u32[]{:S(2)}) collective-permute-start(bf16[1024,512]{1,0:T(8,128)(2,1)} %pad_maximum_fusion.2), channel_id=1, source_target_pairs={{0,2},{1,3},{2,4},{3,5},{4,6},{5,7},{6,0},{7,1},{8,10},{9,11},{10,... | collective-permute-start | bytes 3145736 | tf_op jit(solution)/shard_map/ppermute | solution.py:28
  75.8 1.1 copy-start.9
  77.9 20.9 %collective-permute-start.8 = (bf16[1024,512]{1,0:T(8,128)(2,1)}, bf16[1024,512]{1,0:T(8,128)(2,1)}, u32[]{:S(2)}, u32[]{:S(2)}) collective-permute-start(bf16[1024,512]{1,0:T(8,128)(2,1)} %pad_maximum_fusion.3), channel_id=1, source_target_pairs={{0,6},{1,7},{2,0},{3,1},{4,2},{5,3},{6,4},{7,5},{8,14},{9,15},{10,... | collective-permute-start | bytes 3145736 | tf_op jit(solution)/shard_map/ppermute | solution.py:28
  80.6 18.1 %copy-start.13 = (bf16[1024,512]{1,0:T(8,128)(2,1)S(1)}, bf16[1024,512]{1,0:T(8,128)(2,1)}, u32[]{:S(2)}) copy-start(bf16[1024,512]{1,0:T(8,128)(2,1)} %copy-done.12) | copy-start | bytes 3145732
  83.2 15.6 %copy-start.1 = (bf16[1024,512]{1,0:T(8,128)(2,1)S(1)}, bf16[1024,512]{1,0:T(8,128)(2,1)}, u32[]{:S(2)}) copy-start(bf16[1024,512]{1,0:T(8,128)(2,1)} %copy-done) | copy-start | bytes 3145732
  83.2 15.6 %copy-start.4 = (bf16[1024,512]{1,0:T(8,128)(2,1)S(1)}, bf16[1024,512]{1,0:T(8,128)(2,1)}, u32[]{:S(2)}) copy-start(bf16[1024,512]{1,0:T(8,128)(2,1)} %copy-done.3) | copy-start | bytes 3145732
  83.2 15.6 %copy-start.7 = (bf16[1024,512]{1,0:T(8,128)(2,1)S(1)}, bf16[1024,512]{1,0:T(8,128)(2,1)}, u32[]{:S(2)}) copy-start(bf16[1024,512]{1,0:T(8,128)(2,1)} %copy-done.6) | copy-start | bytes 3145732
  83.2 15.6 %copy-start.10 = (bf16[1024,512]{1,0:T(8,128)(2,1)S(1)}, bf16[1024,512]{1,0:T(8,128)(2,1)}, u32[]{:S(2)}) copy-start(bf16[1024,512]{1,0:T(8,128)(2,1)} %copy-done.9) | copy-start | bytes 3145732
  84.2 60.8 %collective-permute-start.11 = (bf16[512,1024]{1,0:T(8,128)(2,1)}, bf16[512,1024]{1,0:T(8,128)(2,1)}, u32[]{:S(2)}, u32[]{:S(2)}) collective-permute-start(bf16[512,1024]{1,0:T(8,128)(2,1)} %pad_maximum_fusion.4), channel_id=1, source_target_pairs={{0,2},{1,3},{2,4},{3,5},{4,6},{5,7},{6,0},{7,1},{8,10},{9,11},{10,... | collective-permute-start | bytes 3145736 | tf_op jit(solution)/shard_map/ppermute | solution.py:28
  85.3 62.2 %collective-permute-start.12 = (bf16[512,1024]{1,0:T(8,128)(2,1)}, bf16[512,1024]{1,0:T(8,128)(2,1)}, u32[]{:S(2)}, u32[]{:S(2)}) collective-permute-start(bf16[512,1024]{1,0:T(8,128)(2,1)} %pad_maximum_fusion.5), channel_id=1, source_target_pairs={{0,4},{1,5},{2,6},{3,7},{4,0},{5,1},{6,2},{7,3},{8,12},{9,13},{10,... | collective-permute-start | bytes 3145736 | tf_op jit(solution)/shard_map/ppermute | solution.py:28
  103.4 6.6 %copy-start.15 = (bf16[256,1024]{1,0:T(8,128)(2,1)}, bf16[256,1024]{1,0:T(8,128)(2,1)S(1)}, u32[]{:S(2)}) copy-start(bf16[256,1024]{1,0:T(8,128)(2,1)S(1)} %shard_map.83.packed) | copy-start | bytes 1572868
  110.0 35.1 %copy-start.16 = (bf16[256,1024]{1,0:T(8,128)(2,1)S(1)}, bf16[256,1024]{1,0:T(8,128)(2,1)}, u32[]{:S(2)}) copy-start(bf16[256,1024]{1,0:T(8,128)(2,1)} %copy-done.15) | copy-start | bytes 1572868
  110.0 79.0 %collective-permute-start.9 = (bf16[256,4096]{1,0:T(8,128)(2,1)}, bf16[256,4096]{1,0:T(8,128)(2,1)}, u32[]{:S(2)}, u32[]{:S(2)}) collective-permute-start(bf16[256,4096]{1,0:T(8,128)(2,1)} %get-tuple-element.7), channel_id=1, source_target_pairs={{0,8},{8,16},{16,24},{24,32},{32,40},{40,48},{48,56},{56,64},{64,7... | collective-permute-start | bytes 6291464 | tf_op jit(solution)/shard_map/ppermute | solution.py:18
  141.6 38.0 %collective-permute-start.13 = (bf16[512,1024]{1,0:T(8,128)(2,1)}, bf16[512,1024]{1,0:T(8,128)(2,1)S(1)}, u32[]{:S(2)}, u32[]{:S(2)}) collective-permute-start(bf16[512,1024]{1,0:T(8,128)(2,1)} %pad_maximum_fusion.6), channel_id=1, source_target_pairs={{0,6},{1,7},{2,0},{3,1},{4,2},{5,3},{6,4},{7,5},{8,14},{9,15},{10,... | collective-permute-start | bytes 3145736 | tf_op jit(solution)/shard_map/ppermute | solution.py:28
  145.1 34.7 %collective-permute-start.14 = (bf16[256,1024]{1,0:T(8,128)(2,1)S(1)}, bf16[256,1024]{1,0:T(8,128)(2,1)S(1)}, u32[]{:S(2)}, u32[]{:S(2)}) collective-permute-start(bf16[256,1024]{1,0:T(8,128)(2,1)S(1)} %copy-done.16), channel_id=1, source_target_pairs={{0,2},{1,3},{2,4},{3,5},{4,6},{5,7},{6,0},{7,1},{8,10},{9,11},{10,... | collective-permute-start | bytes 1572872 | tf_op jit(solution)/shard_map/ppermute | solution.py:28
  145.1 34.7 %collective-permute-start.15 = (bf16[256,1024]{1,0:T(8,128)(2,1)S(1)}, bf16[256,1024]{1,0:T(8,128)(2,1)S(1)}, u32[]{:S(2)}, u32[]{:S(2)}) collective-permute-start(bf16[256,1024]{1,0:T(8,128)(2,1)S(1)} %copy-done.16), channel_id=1, source_target_pairs={{0,4},{1,5},{2,6},{3,7},{4,0},{5,1},{6,2},{7,3},{8,12},{9,13},{10,... | collective-permute-start | bytes 1572872 | tf_op jit(solution)/shard_map/ppermute | solution.py:28
  147.5 39.9 %collective-permute-start.16 = (bf16[256,1024]{1,0:T(8,128)(2,1)S(1)}, bf16[256,1024]{1,0:T(8,128)(2,1)S(1)}, u32[]{:S(2)}, u32[]{:S(2)}) collective-permute-start(bf16[256,1024]{1,0:T(8,128)(2,1)S(1)} %copy-done.16), channel_id=1, source_target_pairs={{0,6},{1,7},{2,0},{3,1},{4,2},{5,3},{6,4},{7,5},{8,14},{9,15},{10,... | collective-permute-start | bytes 1572872 | tf_op jit(solution)/shard_map/ppermute | solution.py:28
  179.7 7.9 %copy-start.20 = (bf16[256,1024]{1,0:T(8,128)(2,1)S(1)}, bf16[256,1024]{1,0:T(8,128)(2,1)}, u32[]{:S(2)}) copy-start(bf16[256,1024]{1,0:T(8,128)(2,1)} %get-tuple-element.16) | copy-start | bytes 1572868
  187.6 1.4 copy-start.2
  187.7 1.5 copy-start.5
  187.7 1.8 copy-start.8
  187.7 2.1 copy-start.11
  187.7 3.0 %copy-start.14 = (bf16[1024,512]{1,0:T(8,128)(2,1)S(1)}, bf16[1024,512]{1,0:T(8,128)(2,1)}, u32[]{:S(2)}) copy-start(bf16[1024,512]{1,0:T(8,128)(2,1)} %copy-done.12) | copy-start | bytes 3145732
  189.0 7.9 %copy-start.17 = (f32[1024,512]{0,1:T(8,128)}, f32[1024,512]{0,1:T(8,128)S(1)}, u32[]{:S(2)}) copy-start(f32[1024,512]{0,1:T(8,128)S(1)} %fusion.12) | copy-start | bytes 6291460
  189.0 6.6 %copy-start.19 = (bf16[256,1024]{1,0:T(8,128)(2,1)S(1)}, bf16[256,1024]{1,0:T(8,128)(2,1)}, u32[]{:S(2)}) copy-start(bf16[256,1024]{1,0:T(8,128)(2,1)} %get-tuple-element.20) | copy-start | bytes 1572868
  195.3 59.4 %collective-permute-start.10 = (bf16[256,4096]{1,0:T(8,128)(2,1)S(1)}, bf16[256,4096]{1,0:T(8,128)(2,1)}, u32[]{:S(2)}, u32[]{:S(2)}) collective-permute-start(bf16[256,4096]{1,0:T(8,128)(2,1)S(1)} %shard_map.85), channel_id=1, source_target_pairs={{0,248},{8,0},{16,8},{24,16},{32,24},{40,32},{48,40},{56,48},{64,5... | collective-permute-start | bytes 6291464 | tf_op jit(solution)/shard_map/ppermute | solution.py:18
  196.9 1.3 copy-start.18
  198.3 49.3 %collective-permute-start.17 = (bf16[512,1024]{0,1:T(8,128)(2,1)S(1)}, bf16[512,1024]{0,1:T(8,128)(2,1)}, u32[]{:S(2)}, u32[]{:S(2)}) collective-permute-start(bf16[512,1024]{0,1:T(8,128)(2,1)S(1)} %fusion.1), channel_id=1, source_target_pairs={{0,1},{1,0},{2,3},{3,2},{4,5},{5,4},{6,7},{7,6},{8,9},{9,8},{10,11... | collective-permute-start | bytes 3145736 | tf_op jit(solution)/shard_map/ppermute | solution.py:32

commit v2 on v1

v2 whole, which is shorter than its diff:
```python
import functools

import jax
import jax.numpy as jnp
from jax import lax
from jax.experimental import pallas as pl
from jax.experimental.pallas import tpu as pltpu
from jax.sharding import PartitionSpec as P

INV_ROOT_TWO = 0.7071067811865476
INV_ROOT_TWO_PI = 0.3989422804014327
X_SIZE = 4
Y_SIZE = 2
F32 = jnp.float32
BF16 = jnp.bfloat16


def over_section(array, by):
    devices = lax.axis_size("section")
    return lax.ppermute(
        array, "section", [(i, (i + by) % devices) for i in range(devices)]
    )


def over_x(array, by):
    pairs = []
    for x in range(X_SIZE):
        for y in range(Y_SIZE):
            pairs.append((x * Y_SIZE + y, ((x + by) % X_SIZE) * Y_SIZE + y))
    return lax.ppermute(array, "dp", pairs)


def swap_y(array):
    return lax.ppermute(array, "dp", [(i, i ^ 1) for i in range(X_SIZE * Y_SIZE)])


def gelu_pair(preact):
    normal_cdf = 0.5 * (1.0 + lax.erf(preact * INV_ROOT_TWO))
    density = jnp.exp(-0.5 * preact * preact) * INV_ROOT_TWO_PI
    return (preact * normal_cdf, normal_cdf + preact * density)


def times(left, right):
    return jnp.dot(left, right, preferred_element_type=F32)


def times_transposed(left, right):
    return lax.dot_general(
        left, right, (((1,), (1,)), ((), ())), preferred_element_type=F32
    )


def contract_tokens(left, right):
    return lax.dot_general(
        left, right, (((0,), (0,)), ((), ())), preferred_element_type=F32
    )


def weight_items(refs):
    near, (far_in, far_out) = refs[:6], refs[6:]
    rows = far_in.shape[0] // 2
    items = [((ref, 0), (ref, rows)) for ref in near]
    items += [((far_in, part * rows), (far_out, part * rows)) for part in range(2)]
    return rows, items


def columns_of(starts, block, width):
    return pl.ds(pl.multiple_of(starts[block], width), width)


class Loads:
    def __init__(self, semaphores):
        self.semaphores, self.copies, self.waited = semaphores, [], set()

    def start(self, source, target):
        number = len(self.copies)
        copy = pltpu.make_async_copy(source, target, self.semaphores.at[number])
        copy.start()
        self.copies.append((copy, target))
        return number

    def get(self, number):
        copy, target = self.copies[number]
        if number not in self.waited:
            self.waited.add(number)
            copy.wait()
        return target

    def finish(self):
        for number in range(len(self.copies)):
            self.get(number)


def hidden_kernel(starts, inputs, upstream, *rest):
    (rows, items), rest = weight_items(rest[:8]), rest[8:]
    hidden, dpre, left, right, up, down, semaphores = rest
    loads, numbers = Loads(semaphores), []
    for block, ((up_ref, up_row), (down_ref, down_row)) in enumerate(items):
        columns = columns_of(starts, block, rows)
        numbers.append(
            (
                loads.start(inputs.at[:, columns], left.at[block]),
                loads.start(up_ref.at[pl.ds(up_row, rows)], up.at[block]),
                loads.start(upstream.at[:, columns], right.at[block]),
                loads.start(down_ref.at[pl.ds(down_row, rows)], down.at[block]),
            )
        )
    preact = dhidden = None
    for one, two, three, four in numbers:
        first = times(loads.get(one)[...], loads.get(two)[...])
        second = times(loads.get(three)[...], loads.get(four)[...])
        preact = first if preact is None else preact + first
        dhidden = second if dhidden is None else dhidden + second
    activated, slope = gelu_pair(preact)
    hidden[...] = activated.astype(BF16)
    dpre[...] = (dhidden * slope).astype(BF16)


def residual_kernel(which, starts, inputs, inner, *rest):
    (rows, items), rest = weight_items(rest[:8]), rest[8:]
    output, left, weight, result, semaphores = rest
    loads, numbers = Loads(semaphores), []
    for block, item in enumerate(items):
        ref, row = item[which]
        numbers.append(
            (
                loads.start(ref.at[pl.ds(row, rows)], weight.at[block]),
                loads.start(
                    inputs.at[:, columns_of(starts, block, rows)], left.at[block]
                ),
            )
        )
    for block, (one, two) in enumerate(numbers):
        branch = times_transposed(inner[...], loads.get(one)[...])
        total = loads.get(two)[...].astype(F32) + branch
        result[block] = total.astype(BF16)
        loads.start(
            result.at[block], output.at[:, columns_of(starts, block, rows)]
        )
    loads.finish()


def shadow_kernel(starts, inputs, *rest):
    (rows, items), rest = weight_items(rest[:8]), rest[8:]
    output, left, up, down, result, semaphores = rest
    loads, numbers = Loads(semaphores), []
    for block, ((ref, row), _) in enumerate(items):
        columns = columns_of(starts, block, rows)
        numbers.append(
            (
                loads.start(inputs.at[:, columns], left.at[block]),
                loads.start(ref.at[pl.ds(row, rows)], up.at[block]),
            )
        )
    downs = []
    for block, (_, (ref, row)) in enumerate(items):
        downs.append(loads.start(ref.at[pl.ds(row, rows)], down.at[block]))
    preact = None
    for one, two in numbers:
        first = times(loads.get(one)[...], loads.get(two)[...])
        preact = first if preact is None else preact + first
    hidden = gelu_pair(preact)[0].astype(BF16)
    for block, number in enumerate(downs):
        branch = times_transposed(hidden, loads.get(number)[...])
        total = left[block].astype(F32) + branch
        result[block] = total.astype(BF16)
        loads.start(
            result.at[block], output.at[:, columns_of(starts, block, rows)]
        )
    loads.finish()


def part_kernel(starts, whole, other, *rest):
    pieces, (part, lefts, rights, semaphores) = rest[:-4], rest[-4:]
    rows, width = part.shape
    count = lefts.shape[0] - 1
    joined = len(pieces) == count
    loads, numbers = Loads(semaphores), []
    numbers.append(
        (
            loads.start(whole.at[:, columns_of(starts, 0, rows)], lefts.at[0]),
            loads.start(other, rights.at[0]),
        )
    )
    for k in range(count):
        piece = pieces[k]
        if joined:
            right = piece.at[:, pl.ds(piece.shape[1] - width, width)]
        else:
            right = pieces[count + k]
        numbers.append(
            (
                loads.start(
                    piece.at[:, columns_of(starts, 1, rows)], lefts.at[k + 1]
                ),
                loads.start(right, rights.at[k + 1]),
            )
        )
    total = None
    for one, two in numbers:
        product = contract_tokens(loads.get(one)[...], loads.get(two)[...])
        total = product if total is None else total + product
    part[...] = total.astype(part.dtype)


def copy_kernel(source, target, semaphores):
    loads, count = Loads(semaphores), semaphores.shape[0]
    rows = source.shape[0] // count
    for k in range(count):
        some = pl.ds(k * rows, rows)
        loads.start(source.at[some], target.at[some])
    loads.finish()


ANY = pl.BlockSpec(memory_space=pl.ANY)
VMEM = pl.BlockSpec(memory_space=pltpu.VMEM)
SMEM = pl.BlockSpec(memory_space=pltpu.SMEM)


def local_call(kernel, outs, in_specs, out_specs, scratch, copies, *arrays):
    return pl.pallas_call(
        kernel,
        out_shape=outs,
        in_specs=in_specs,
        out_specs=out_specs,
        scratch_shapes=[*scratch, pltpu.SemaphoreType.DMA((copies,))],
        compiler_params=pltpu.CompilerParams(vmem_limit_bytes=56 * 2**20),
        cost_estimate=pl.CostEstimate(flops=1, bytes_accessed=1, transcendentals=0),
    )(*arrays)


def on_device(handoff, grad_back, w_in, w_out):
    position = lax.axis_index("dp")
    x, y = position // Y_SIZE, position % Y_SIZE
    rows, width = w_in.shape[1:]
    tokens, features = handoff.shape[1:]
    starts = jnp.stack(
        [
            (lax.rem(x + by, X_SIZE) * Y_SIZE + (y + j) % Y_SIZE) * rows
            for by in (0, 3, 1, 2)
            for j in range(Y_SIZE)
        ]
    ).astype(jnp.int32)

    own = jnp.concatenate([w_in[0], w_out[0]], axis=0)
    partner = swap_y(own)
    behind, ahead = over_x(own, 1), over_x(own, -1)
    handoff, grad_back, partner = lax.optimization_barrier(
        (handoff, grad_back, partner)
    )
    behind_partner, ahead_partner = over_x(partner, 1), over_x(partner, -1)
    inputs = over_section(handoff[0], 1)
    upstream = over_section(grad_back[0], -1)
    far_in = over_x(jnp.concatenate([behind[:rows], behind_partner[:rows]]), 1)
    far_out = over_x(jnp.concatenate([ahead[rows:], ahead_partner[rows:]]), -1)
    weights = (
        own,
        partner,
        behind,
        behind_partner,
        ahead,
        ahead_partner,
        far_in,
        far_out,
    )
    blocks = X_SIZE * Y_SIZE
    activations = jax.ShapeDtypeStruct((tokens, features), BF16)
    half = jax.ShapeDtypeStruct((tokens, width), BF16)
    token_blocks = pltpu.VMEM((blocks, tokens, rows), BF16)
    weight_blocks = pltpu.VMEM((blocks, rows, width), BF16)
    wide = Y_SIZE * rows

    def cut(array, by):
        first = lax.rem(x + by, X_SIZE) * wide
        return lax.dynamic_slice_in_dim(array, first, wide, axis=1)

    inputs_out = [cut(inputs, by) for by in range(1, X_SIZE)]
    inputs_pieces = [over_x(p, by + 1) for by, p in enumerate(inputs_out)]
    first_starts, _ = lax.optimization_barrier((starts, inputs_out))

    hidden, dpre = local_call(
        hidden_kernel,
        (half, half),
        [SMEM] + [ANY] * 10,
        (VMEM, VMEM),
        [token_blocks, token_blocks, weight_blocks, weight_blocks],
        4 * blocks,
        first_starts,
        inputs,
        upstream,
        *weights,
    )

    def residual(which, base, inner):
        return local_call(
            functools.partial(residual_kernel, which),
            activations,
            [SMEM, ANY, VMEM] + [ANY] * 8,
            ANY,
            [token_blocks, weight_blocks, token_blocks],
            3 * blocks,
            starts,
            base,
            inner,
            *weights,
        )

    layer_out = residual(1, inputs, hidden)
    arrived = over_section(layer_out, 1)
    input_grad = residual(0, upstream, dpre)

    dpre_pieces = [over_x(dpre, by) for by in range(1, X_SIZE)]
    joint_pieces = [
        over_x(jnp.concatenate([cut(upstream, by), hidden], axis=1), by)
        for by in range(1, X_SIZE)
    ]
    ours = jnp.stack([x * wide + y * rows, y * rows]).astype(jnp.int32)
    other = jnp.stack([x * wide + (1 - y) * rows, (1 - y) * rows]).astype(jnp.int32)

    def part(where, kind, *arrays):
        return local_call(
            part_kernel,
            jax.ShapeDtypeStruct((rows, width), kind),
            [SMEM] + [ANY] * len(arrays),
            VMEM,
            [
                pltpu.VMEM((X_SIZE, tokens, rows), BF16),
                pltpu.VMEM((X_SIZE, tokens, width), BF16),
            ],
            2 * X_SIZE,
            where,
            *arrays,
        )

    arrays = (inputs, dpre, *inputs_pieces, *dpre_pieces)
    theirs_in = part(other, BF16, *arrays)
    mine_in = part(ours, F32, *arrays)
    received_in = swap_y(theirs_in)

    arrived, input_grad, mine_in = lax.optimization_barrier(
        (arrived, input_grad, mine_in)
    )
    shadow_back = local_call(
        shadow_kernel,
        activations,
        [SMEM] + [ANY] * 9,
        ANY,
        [token_blocks, weight_blocks, weight_blocks, token_blocks],
        4 * blocks,
        starts,
        arrived,
        *weights,
    )
    shadow = over_section(shadow_back, -1)

    arrays = (upstream, hidden, *joint_pieces)
    theirs_out = part(other, BF16, *arrays)
    mine_out = part(ours, F32, *arrays)
    received_out = swap_y(theirs_out)
    grad_in = mine_in + received_in.astype(F32)
    shadow = local_call(copy_kernel, activations, [ANY], ANY, [], 8, shadow)
    shadow, received_out, grad_in = lax.optimization_barrier(
        (shadow, received_out, grad_in)
    )
    grad_out = mine_out + received_out.astype(F32)
    return (
        layer_out[None],
        shadow[None],
        input_grad[None],
        grad_in[None],
        grad_out[None],
    )


def solution(mesh):
    spec = P("section", "dp", None)
    return jax.shard_map(
        on_device,
        mesh=mesh,
        in_specs=(spec,) * 4,
        out_specs=(spec,) * 5,
        check_vma=False,
    )
```

time: 259 us -> 276 us (1.066)
  Pallas kernels: 15.8 us -> 106 us
  waiting for transfers between devices: 149 us -> 113 us
  starting transfers between devices: 59.1 us -> 34.9 us
  local copies, waits for them, and re-layouts: 21.3 us -> 12.6 us
    pallas_call x3 -> x9, Pallas kernels: 15.8 us -> 106 us  [local_call(): pl.pallas_call(kernel, out_shape=outs, in_specs=in_specs, out_specs=out_s...]
    ppermute x2 -> x3, waiting for transfers between devices: 84.9 us -> 19.3 us  [swap_y(): lax.ppermute(array, 'dp', [(i, i ^ 1) for i in range(X_SIZE * Y_SIZE)])]
    ppermute x4, starting transfers between devices: 32.6 us -> 5.78 us  [over_section(): lax.ppermute(array, 'section', [(i, (i + by) % devices) for i in range(de...]
    ppermute x4, waiting for transfers between devices: 0.01 us -> 17.2 us  [over_section(): lax.ppermute(array, 'section', [(i, (i + by) % devices) for i in range(de...]
    ppermute x12 -> x15, waiting for transfers between devices: 64.2 us -> 76 us  [over_x(): return lax.ppermute(array, 'dp', pairs)]
    unnamed x45 -> x44, local copies, waits for them, and re-layouts: 13.7 us -> 9.06 us
    ppermute x2 -> x3, starting transfers between devices: 8.12 us -> 9.55 us  [swap_y(): lax.ppermute(array, 'dp', [(i, i ^ 1) for i in range(X_SIZE * Y_SIZE)])]
    ppermute x12 -> x15, starting transfers between devices: 18.3 us -> 19.5 us  [over_x(): return lax.ppermute(array, 'dp', pairs)]
  transfers between devices with their start and end apart: 18 -> 22, of which waited for: 7 -> 10; matrix products, arithmetic and copies ran while one was open for 8% -> 3% of each run, Pallas kernels for 4% -> 31%
where the time goes in v2:
time: 276 us
  waiting for transfers between devices  113 us (41%)
  Pallas kernels  106 us (38%)
  starting transfers between devices  34.9 us (13%)
  local copies, waits for them, and re-layouts  12.6 us (5%)
  other arithmetic  8.26 us (3%)
    pallas_call x9, Pallas kernels, local_call(): pl.pallas_call(kernel, out_shape=outs, in_specs=in_specs, out_specs=out_s...  106 us
    ppermute x15, waiting for transfers between devices, over_x(): return lax.ppermute(array, 'dp', pairs)  76 us
    ppermute x15, starting transfers between devices, over_x(): return lax.ppermute(array, 'dp', pairs)  19.5 us
    ppermute x3, waiting for transfers between devices, swap_y(): lax.ppermute(array, 'dp', [(i, i ^ 1) for i in range(X_SIZE * Y_SIZE)])  19.3 us
    ppermute x4, waiting for transfers between devices, over_section(): lax.ppermute(array, 'section', [(i, (i + by) % devices) for i in range(de...  17.2 us
    ppermute x3, starting transfers between devices, swap_y(): lax.ppermute(array, 'dp', [(i, i ^ 1) for i in range(X_SIZE * Y_SIZE)])  9.55 us
    unnamed x44, local copies, waits for them, and re-layouts  9.06 us
    ppermute x4, starting transfers between devices, over_section(): lax.ppermute(array, 'section', [(i, (i + by) % devices) for i in range(de...  5.78 us
  transfers between devices with their start and end apart: 22, of which 10 were waited for; matrix products, arithmetic and copies ran while one was open for 3% of the time, Pallas kernels for 31%

profile of v2, /device:TPU:1, one launch (start us, length us, event | category | flops | bytes accessed | tf_op | source)
XLA Modules:
  0.0 275.6 jit_solution(16556501773408246927)
XLA Ops:
  0.6 1.3 pad_maximum_fusion.3.rest_0_
  1.9 3.8 %collective-permute-start = (bf16[1024,512]{1,0:T(8,128)(2,1)S(1)}, bf16[1024,512]{1,0:T(8,128)(2,1)S(1)}, u32[]{:S(2)}, u32[]{:S(2)}) collective-permute-start(bf16[1024,512]{1,0:T(8,128)(2,1)S(1)} %pad_maximum_fusion.3.rest_0_), channel_id=1, source_target_pairs={{0,1},{1,0},{2,3},{3,2},{4,5},{5,4},{6,7},{7,6},{8,9},{9,8},{10,11... | collective-permute-start | bytes 3145736 | tf_op jit(solution)/shard_map/ppermute | solution.py:34
  5.7 2.5 collective-permute-start.5
  8.2 19.3 %collective-permute-done.rest_1_ = bf16[1024,512]{1,0:T(8,128)(2,1)S(1)} collective-permute-done((bf16[1024,512]{1,0:T(8,128)(2,1)S(1)}, bf16[1024,512]{1,0:T(8,128)(2,1)S(1)}, u32[]{:S(2)}, u32[]{:S(2)}) %collective-permute-start) | collective-permute-done | bytes 1048608 | tf_op jit(solution)/shard_map/ppermute | solution.py:34
  27.6 3.3 %collective-permute-start.6 = (bf16[1024,512]{1,0:T(8,128)(2,1)S(1)}, bf16[1024,512]{1,0:T(8,128)(2,1)S(1)}, u32[]{:S(2)}, u32[]{:S(2)}) collective-permute-start(bf16[1024,512]{1,0:T(8,128)(2,1)S(1)} %collective-permute-done.rest_1_), channel_id=1, source_target_pairs={{0,6},{1,7},{2,0},{3,1},{4,2},{5,3},{6,4},{7,5},{8,14},{9,15},{10,... | collective-permute-start | bytes 3145736 | tf_op jit(solution)/shard_map/ppermute | solution.py:30
  30.8 3.0 %collective-permute-start.1 = (bf16[256,4096]{1,0:T(8,128)(2,1)}, bf16[256,4096]{1,0:T(8,128)(2,1)}, u32[]{:S(2)}, u32[]{:S(2)}) collective-permute-start(bf16[256,4096]{1,0:T(8,128)(2,1)} %bitcast.10), channel_id=1, source_target_pairs={{0,8},{8,16},{16,24},{24,32},{32,40},{40,48},{48,56},{56,64},{64,7... | collective-permute-start | bytes 6291464 | tf_op jit(solution)/shard_map/ppermute | solution.py:20
  34.0 0.8 copy-done.3
  34.9 0.9 copy-done.4
  35.8 16.0 %collective-permute-done.6.rest_5_ = bf16[1024,512]{1,0:T(8,128)(2,1)S(1)} collective-permute-done((bf16[1024,512]{1,0:T(8,128)(2,1)S(1)}, bf16[1024,512]{1,0:T(8,128)(2,1)S(1)}, u32[]{:S(2)}, u32[]{:S(2)}) %collective-permute-start.6) | collective-permute-done | bytes 1048608 | tf_op jit(solution)/shard_map/ppermute | solution.py:30
  51.8 1.0 copy-done.5
  52.8 1.0 pad_maximum_fusion.5
  53.8 3.5 %collective-permute-start.8 = (bf16[1024,512]{1,0:T(8,128)(2,1)}, bf16[1024,512]{1,0:T(8,128)(2,1)}, u32[]{:S(2)}, u32[]{:S(2)}) collective-permute-start(bf16[1024,512]{1,0:T(8,128)(2,1)} %pad_maximum_fusion.5), channel_id=1, source_target_pairs={{0,6},{1,7},{2,0},{3,1},{4,2},{5,3},{6,4},{7,5},{8,14},{9,15},{10,... | collective-permute-start | bytes 3145736 | tf_op jit(solution)/shard_map/ppermute | solution.py:30
  57.3 2.3 collective-permute-done.4.rest_3_
  59.6 1.0 copy-done.6
  60.7 1.0 pad_maximum_fusion.4
  61.8 0.7 stack.53.starts
  62.5 17.2 %collective-permute-done.1.inputs.whole = bf16[256,4096]{1,0:T(8,128)(2,1)} collective-permute-done((bf16[256,4096]{1,0:T(8,128)(2,1)}, bf16[256,4096]{1,0:T(8,128)(2,1)}, u32[]{:S(2)}, u32[]{:S(2)}) %collective-permute-start.1) | collective-permute-done | bytes 2097184 | tf_op jit(solution)/shard_map/ppermute | solution.py:20
  79.6 2.6 constant_dynamic-slice_fusion.3
  82.2 5.4 %collective-permute-done.7.rest_6_ = bf16[1024,512]{1,0:T(8,128)(2,1)S(1)} collective-permute-done((bf16[1024,512]{1,0:T(8,128)(2,1)}, bf16[1024,512]{1,0:T(8,128)(2,1)S(1)}, u32[]{:S(2)}, u32[]{:S(2)}) %collective-permute-start.7) | collective-permute-done | bytes 1048608 | tf_op jit(solution)/shard_map/ppermute | solution.py:30
  87.6 1.0 copy-done.8
  88.6 1.3 copy-done
  89.9 6.9 %shard_map.83 = (bf16[256,512]{1,0:T(8,128)(2,1)}, bf16[256,512]{1,0:T(8,128)(2,1)}) custom-call(s32[8]{0:T(128)} %stack.53.starts, bf16[256,4096]{1,0:T(8,128)(2,1)} %collective-permute-done.1.inputs.whole, bf16[256,4096]{1,0:T(8,128)(2,1)} %copy-done, bf16[1024,512]{1,0:T(8,128)(2,1)} %copy-done.2, bf16[1024,512]{1,0:T(8,128)(2,1)} %copy-done.7, ...), custom_call_target="tpu_custom_call" | custom-call | flops 1 | bytes 1 | tf_op jit(solution)/shard_map/pallas_call | solution.py:221
  96.8 6.1 %shard_map.84 = bf16[256,4096]{1,0:T(8,128)(2,1)} custom-call(s32[8]{0:T(128)} %stack.53.starts, bf16[256,4096]{1,0:T(8,128)(2,1)} %collective-permute-done.1.inputs.whole, bf16[256,512]{1,0:T(8,128)(2,1)} %get-tuple-element.21.inner.other, bf16[1024,512]{1,0:T(8,128)(2,1)} %copy-done.2, bf16[1024,512]{1,0:T(8,128)(2,1)} %copy-done.7, ...), custom_call_target="tpu_custom_call" | custom-call | flops 1 | bytes 1 | tf_op jit(solution)/shard_map/pallas_call | solution.py:221
  102.9 2.2 collective-permute-start.9
  105.7 3.3 %collective-permute-start.12 = (bf16[256,1024]{1,0:T(8,128)(2,1)}, bf16[256,1024]{1,0:T(8,128)(2,1)S(1)}, u32[]{:S(2)}, u32[]{:S(2)}) collective-permute-start(bf16[256,1024]{1,0:T(8,128)(2,1)} %get-tuple-element.32), channel_id=1, source_target_pairs={{0,6},{1,7},{2,0},{3,1},{4,2},{5,3},{6,4},{7,5},{8,14},{9,15},{10,... | collective-permute-start | bytes 1572872 | tf_op jit(solution)/shard_map/ppermute | solution.py:30
  109.0 4.6 %collective-permute-done.15.rest_5_ = bf16[256,512]{1,0:T(8,128)(2,1)S(1)} collective-permute-done((bf16[256,512]{1,0:T(8,128)(2,1)S(1)}, bf16[256,512]{1,0:T(8,128)(2,1)S(1)}, u32[]{:S(2)}, u32[]{:S(2)}) %collective-permute-start.15) | collective-permute-done | bytes 262176 | tf_op jit(solution)/shard_map/ppermute | solution.py:30
  113.6 4.4 %collective-permute-start.10 = (bf16[256,1024]{1,0:T(8,128)(2,1)}, bf16[256,1024]{1,0:T(8,128)(2,1)S(1)}, u32[]{:S(2)}, u32[]{:S(2)}) collective-permute-start(bf16[256,1024]{1,0:T(8,128)(2,1)} %get-tuple-element.34), channel_id=1, source_target_pairs={{0,2},{1,3},{2,4},{3,5},{4,6},{5,7},{6,0},{7,1},{8,10},{9,11},{10,... | collective-permute-start | bytes 1572872 | tf_op jit(solution)/shard_map/ppermute | solution.py:30
  119.0 6.1 %shard_map.85 = bf16[256,4096]{1,0:T(8,128)(2,1)} custom-call(s32[8]{0:T(128)} %stack.53.starts, bf16[256,4096]{1,0:T(8,128)(2,1)} %copy-done, bf16[256,512]{1,0:T(8,128)(2,1)} %get-tuple-element.22.inner.other, bf16[1024,512]{1,0:T(8,128)(2,1)} %copy-done.2, bf16[1024,512]{1,0:T(8,128)(2,1)} %copy-done.7, bf16[1024,512]{1,0:T(8,128)(2,1)} %copy-done.4, ...), custom_call_target="tpu_custom_call" | custom-call | flops 1 | bytes 1 | tf_op jit(solution)/shard_map/pallas_call | solution.py:221
  125.1 17.8 %collective-permute-done.13.rest_3_ = bf16[256,512]{1,0:T(8,128)(2,1)S(1)} collective-permute-done((bf16[256,512]{1,0:T(8,128)(2,1)S(1)}, bf16[256,512]{1,0:T(8,128)(2,1)S(1)}, u32[]{:S(2)}, u32[]{:S(2)}) %collective-permute-start.13) | collective-permute-done | bytes 262176 | tf_op jit(solution)/shard_map/ppermute | solution.py:30
  142.9 0.7 copy-done.21
  143.9 0.8 copy-done.18
  144.8 3.8 %shard_map.86 = f32[512,512]{1,0:T(8,128)} custom-call(s32[2]{0:T(128)} %pad_add_fusion.starts, bf16[256,4096]{1,0:T(8,128)(2,1)} %collective-permute-done.1.inputs.whole, bf16[256,512]{1,0:T(8,128)(2,1)} %get-tuple-element.22.inner.other, bf16[256,1024]{1,0:T(8,128)(2,1)} %copy-done.18, bf16[256,1024]{1,0:T(8,128)(2,1)} %copy-done.17, ...), custom_call_target="tpu_custom_call" | custom-call | flops 1 | bytes 1 | tf_op jit(solution)/shard_map/pallas_call | solution.py:221
  148.6 7.6 %shard_map.87 = bf16[256,4096]{1,0:T(8,128)(2,1)} custom-call(s32[8]{0:T(128)} %stack.53.starts, bf16[256,4096]{1,0:T(8,128)(2,1)} %collective-permute-done.9.inputs, bf16[1024,512]{1,0:T(8,128)(2,1)} %copy-done.2, bf16[1024,512]{1,0:T(8,128)(2,1)} %copy-done.7, bf16[1024,512]{1,0:T(8,128)(2,1)} %copy-done.4, bf16[1024,512]{1,0:T(8,128)(2,1)} %copy-done.6, ...), custom_call_target="tpu_custom_call" | custom-call | flops 1 | bytes 1 | tf_op jit(solution)/shard_map/pallas_call | solution.py:221
  157.2 1.5 pad_maximum_fusion
  159.1 0.6 collective-permute-start.18
  159.7 0.6 collective-permute-start.17
  160.9 3.6 %shard_map.90 = bf16[512,512]{1,0:T(8,128)(2,1)} custom-call(s32[2]{0:T(128)} %pad_add_fusion.1.starts, bf16[256,4096]{1,0:T(8,128)(2,1)} %collective-permute-done.1.inputs.whole, bf16[256,512]{1,0:T(8,128)(2,1)} %get-tuple-element.22.inner.other, bf16[256,1024]{1,0:T(8,128)(2,1)} %copy-done.18, bf16[256,1024]{1,0:T(8,128)(2,1)} %copy-done.17, ...), custom_call_target="tpu_custom_call" | custom-call | flops 1 | bytes 1 | tf_op jit(solution)/shard_map/pallas_call | solution.py:221
  164.6 2.7 collective-permute-start.21
  167.2 8.3 %collective-permute-done.19.rest_2_ = bf16[256,1536]{1,0:T(8,128)(2,1)S(1)} collective-permute-done((bf16[256,1536]{1,0:T(8,128)(2,1)}, bf16[256,1536]{1,0:T(8,128)(2,1)S(1)}, u32[]{:S(2)}, u32[]{:S(2)}) %collective-permute-start.19) | collective-permute-done | bytes 786464 | tf_op jit(solution)/shard_map/ppermute | solution.py:30
  175.5 2.4 collective-permute-done.18.rest_1_
  177.9 19.3 %collective-permute-done.17.rest_0_ = bf16[256,1536]{1,0:T(8,128)(2,1)S(1)} collective-permute-done((bf16[256,1536]{1,0:T(8,128)(2,1)}, bf16[256,1536]{1,0:T(8,128)(2,1)S(1)}, u32[]{:S(2)}, u32[]{:S(2)}) %collective-permute-start.17) | collective-permute-done | bytes 786464 | tf_op jit(solution)/shard_map/ppermute | solution.py:30
  197.2 0.9 copy-done.14
  198.0 3.6 %shard_map.89 = bf16[512,512]{1,0:T(8,128)(2,1)} custom-call(s32[2]{0:T(128)} %pad_add_fusion.1.starts, bf16[256,4096]{1,0:T(8,128)(2,1)} %copy-done, bf16[256,512]{1,0:T(8,128)(2,1)} %get-tuple-element.21.inner.other, bf16[256,1536]{1,0:T(8,128)(2,1)} %copy-done.14, bf16[256,1536]{1,0:T(8,128)(2,1)} %copy-done.13, bf16[256,1536]{1,0:T(8,128)(2,1)} %copy-done.12), custom_call_target="tpu_custom_call" | custom-call | flops 1 | bytes 1 | tf_op jit(solution)/shard_map/pallas_call | solution.py:221
  201.7 3.1 %collective-permute-start.20 = (bf16[512,512]{1,0:T(8,128)(2,1)}, bf16[512,512]{1,0:T(8,128)(2,1)S(1)}, u32[]{:S(2)}, u32[]{:S(2)}) collective-permute-start(bf16[512,512]{1,0:T(8,128)(2,1)} %shard_map.89), channel_id=1, source_target_pairs={{0,1},{1,0},{2,3},{3,2},{4,5},{5,4},{6,7},{7,6},{8,9},{9,8},{10,11... | collective-permute-start | bytes 1572872 | tf_op jit(solution)/shard_map/ppermute | solution.py:34
  204.8 3.8 %shard_map.91 = f32[512,512]{1,0:T(8,128)} custom-call(s32[2]{0:T(128)} %pad_add_fusion.starts, bf16[256,4096]{1,0:T(8,128)(2,1)} %copy-done, bf16[256,512]{1,0:T(8,128)(2,1)} %get-tuple-element.21.inner.other, bf16[256,1536]{1,0:T(8,128)(2,1)} %copy-done.14, bf16[256,1536]{1,0:T(8,128)(2,1)} %copy-done.13, bf16[256,1536]{1,0:T(8,128)(2,1)} %copy-done.12), custom_call_target="tpu_custom_call" | custom-call | flops 1 | bytes 1 | tf_op jit(solution)/shard_map/pallas_call | solution.py:221
  208.6 1.1 convert_add_fusion
  209.7 64.7 %shard_map.88 = bf16[256,4096]{1,0:T(8,128)(2,1)} custom-call(bf16[256,4096]{1,0:T(8,128)(2,1)} %collective-permute-done.16.source), custom_call_target="tpu_custom_call" | custom-call | flops 1 | bytes 1 | tf_op jit(solution)/shard_map/pallas_call | solution.py:221
  274.5 1.1 add_bitcast_fusion
  (64 shorter events, 4.2 us)
Async XLA Ops:
  1.9 51.9 %copy-start.2 = (bf16[1024,512]{1,0:T(8,128)(2,1)}, bf16[1024,512]{1,0:T(8,128)(2,1)S(1)}, u32[]{:S(2)}) copy-start(bf16[1024,512]{1,0:T(8,128)(2,1)S(1)} %pad_maximum_fusion.3.rest_0_) | copy-start | bytes 3145732
  1.9 25.7 %collective-permute-start = (bf16[1024,512]{1,0:T(8,128)(2,1)S(1)}, bf16[1024,512]{1,0:T(8,128)(2,1)S(1)}, u32[]{:S(2)}, u32[]{:S(2)}) collective-permute-start(bf16[1024,512]{1,0:T(8,128)(2,1)S(1)} %pad_maximum_fusion.3.rest_0_), channel_id=1, source_target_pairs={{0,1},{1,0},{2,3},{3,2},{4,5},{5,4},{6,7},{7,6},{8,9},{9,8},{10,11... | collective-permute-start | bytes 3145736 | tf_op jit(solution)/shard_map/ppermute | solution.py:34
  5.7 28.1 %collective-permute-start.5 = (bf16[1024,512]{1,0:T(8,128)(2,1)S(1)}, bf16[1024,512]{1,0:T(8,128)(2,1)S(1)}, u32[]{:S(2)}, u32[]{:S(2)}) collective-permute-start(bf16[1024,512]{1,0:T(8,128)(2,1)S(1)} %pad_maximum_fusion.3.rest_0_), channel_id=1, source_target_pairs={{0,6},{1,7},{2,0},{3,1},{4,2},{5,3},{6,4},{7,5},{8,14},{9,15},{10,... | collective-permute-start | bytes 3145736 | tf_op jit(solution)/shard_map/ppermute | solution.py:30
  8.2 25.8 %collective-permute-start.3 = (bf16[1024,512]{1,0:T(8,128)(2,1)S(1)}, bf16[1024,512]{1,0:T(8,128)(2,1)S(1)}, u32[]{:S(2)}, u32[]{:S(2)}) collective-permute-start(bf16[1024,512]{1,0:T(8,128)(2,1)S(1)} %pad_maximum_fusion.3.rest_0_), channel_id=1, source_target_pairs={{0,2},{1,3},{2,4},{3,5},{4,6},{5,7},{6,0},{7,1},{8,10},{9,11},{10,... | collective-permute-start | bytes 3145736 | tf_op jit(solution)/shard_map/ppermute | solution.py:30
  27.6 33.1 %copy-start.7 = (bf16[1024,512]{1,0:T(8,128)(2,1)}, bf16[1024,512]{1,0:T(8,128)(2,1)S(1)}, u32[]{:S(2)}) copy-start(bf16[1024,512]{1,0:T(8,128)(2,1)S(1)} %collective-permute-done.rest_1_) | copy-start | bytes 3145732
  27.6 24.2 %collective-permute-start.6 = (bf16[1024,512]{1,0:T(8,128)(2,1)S(1)}, bf16[1024,512]{1,0:T(8,128)(2,1)S(1)}, u32[]{:S(2)}, u32[]{:S(2)}) collective-permute-start(bf16[1024,512]{1,0:T(8,128)(2,1)S(1)} %collective-permute-done.rest_1_), channel_id=1, source_target_pairs={{0,6},{1,7},{2,0},{3,1},{4,2},{5,3},{6,4},{7,5},{8,14},{9,15},{10,... | collective-permute-start | bytes 3145736 | tf_op jit(solution)/shard_map/ppermute | solution.py:30
  30.8 48.8 %collective-permute-start.1 = (bf16[256,4096]{1,0:T(8,128)(2,1)}, bf16[256,4096]{1,0:T(8,128)(2,1)}, u32[]{:S(2)}, u32[]{:S(2)}) collective-permute-start(bf16[256,4096]{1,0:T(8,128)(2,1)} %bitcast.10), channel_id=1, source_target_pairs={{0,8},{8,16},{16,24},{24,32},{32,40},{40,48},{48,56},{56,64},{64,7... | collective-permute-start | bytes 6291464 | tf_op jit(solution)/shard_map/ppermute | solution.py:20
  33.9 25.8 %collective-permute-start.4 = (bf16[1024,512]{1,0:T(8,128)(2,1)S(1)}, bf16[1024,512]{1,0:T(8,128)(2,1)S(1)}, u32[]{:S(2)}, u32[]{:S(2)}) collective-permute-start(bf16[1024,512]{1,0:T(8,128)(2,1)S(1)} %collective-permute-done.rest_1_), channel_id=1, source_target_pairs={{0,2},{1,3},{2,4},{3,5},{4,6},{5,7},{6,0},{7,1},{8,10},{9,11},{10,... | collective-permute-start | bytes 3145736 | tf_op jit(solution)/shard_map/ppermute | solution.py:30
  33.9 1.0 copy-start.3
  33.9 53.7 %collective-permute-start.2 = (bf16[256,4096]{1,0:T(8,128)(2,1)}, bf16[256,4096]{1,0:T(8,128)(2,1)S(1)}, u32[]{:S(2)}, u32[]{:S(2)}) collective-permute-start(bf16[256,4096]{1,0:T(8,128)(2,1)} %bitcast.11), channel_id=1, source_target_pairs={{0,248},{8,0},{16,8},{24,16},{32,24},{40,32},{48,40},{56,48},{64,5... | collective-permute-start | bytes 6291464 | tf_op jit(solution)/shard_map/ppermute | solution.py:20
  34.8 1.0 copy-start.4
  51.8 1.0 copy-start.5
  53.8 28.4 %collective-permute-start.8 = (bf16[1024,512]{1,0:T(8,128)(2,1)}, bf16[1024,512]{1,0:T(8,128)(2,1)}, u32[]{:S(2)}, u32[]{:S(2)}) collective-permute-start(bf16[1024,512]{1,0:T(8,128)(2,1)} %pad_maximum_fusion.5), channel_id=1, source_target_pairs={{0,6},{1,7},{2,0},{3,1},{4,2},{5,3},{6,4},{7,5},{8,14},{9,15},{10,... | collective-permute-start | bytes 3145736 | tf_op jit(solution)/shard_map/ppermute | solution.py:30
  59.6 1.0 copy-start.6
  61.8 25.8 %collective-permute-start.7 = (bf16[1024,512]{1,0:T(8,128)(2,1)}, bf16[1024,512]{1,0:T(8,128)(2,1)S(1)}, u32[]{:S(2)}, u32[]{:S(2)}) collective-permute-start(bf16[1024,512]{1,0:T(8,128)(2,1)} %pad_maximum_fusion.4), channel_id=1, source_target_pairs={{0,2},{1,3},{2,4},{3,5},{4,6},{5,7},{6,0},{7,1},{8,10},{9,11},{10,... | collective-permute-start | bytes 3145736 | tf_op jit(solution)/shard_map/ppermute | solution.py:30
  87.6 1.0 copy-start.8
  88.6 1.3 copy-start
  96.8 8.4 %copy-start.15 = (bf16[256,512]{1,0:T(8,128)(2,1)S(1)}, bf16[256,512]{1,0:T(8,128)(2,1)}, u32[]{:S(2)}) copy-start(bf16[256,512]{1,0:T(8,128)(2,1)} %get-tuple-element.22.inner.other) | copy-start | bytes 786436
  102.9 45.7 %collective-permute-start.9 = (bf16[256,4096]{1,0:T(8,128)(2,1)}, bf16[256,4096]{1,0:T(8,128)(2,1)}, u32[]{:S(2)}, u32[]{:S(2)}) collective-permute-start(bf16[256,4096]{1,0:T(8,128)(2,1)} %shard_map.84), channel_id=1, source_target_pairs={{0,8},{8,16},{16,24},{24,32},{32,40},{40,48},{48,56},{56,64},{64,7... | collective-permute-start | bytes 6291464 | tf_op jit(solution)/shard_map/ppermute | solution.py:20
  105.1 8.4 %collective-permute-start.15 = (bf16[256,512]{1,0:T(8,128)(2,1)S(1)}, bf16[256,512]{1,0:T(8,128)(2,1)S(1)}, u32[]{:S(2)}, u32[]{:S(2)}) collective-permute-start(bf16[256,512]{1,0:T(8,128)(2,1)S(1)} %copy-done.15), channel_id=1, source_target_pairs={{0,6},{1,7},{2,0},{3,1},{4,2},{5,3},{6,4},{7,5},{8,14},{9,15},{10,... | collective-permute-start | bytes 786440 | tf_op jit(solution)/shard_map/ppermute | solution.py:30
  105.1 12.8 %collective-permute-start.14 = (bf16[256,512]{1,0:T(8,128)(2,1)S(1)}, bf16[256,512]{1,0:T(8,128)(2,1)S(1)}, u32[]{:S(2)}, u32[]{:S(2)}) collective-permute-start(bf16[256,512]{1,0:T(8,128)(2,1)S(1)} %copy-done.15), channel_id=1, source_target_pairs={{0,4},{1,5},{2,6},{3,7},{4,0},{5,1},{6,2},{7,3},{8,12},{9,13},{10,... | collective-permute-start | bytes 786440 | tf_op jit(solution)/shard_map/ppermute | solution.py:30
  105.7 37.2 %collective-permute-start.12 = (bf16[256,1024]{1,0:T(8,128)(2,1)}, bf16[256,1024]{1,0:T(8,128)(2,1)S(1)}, u32[]{:S(2)}, u32[]{:S(2)}) collective-permute-start(bf16[256,1024]{1,0:T(8,128)(2,1)} %get-tuple-element.32), channel_id=1, source_target_pairs={{0,6},{1,7},{2,0},{3,1},{4,2},{5,3},{6,4},{7,5},{8,14},{9,15},{10,... | collective-permute-start | bytes 1572872 | tf_op jit(solution)/shard_map/ppermute | solution.py:30
  109.0 33.9 %collective-permute-start.11 = (bf16[256,1024]{1,0:T(8,128)(2,1)}, bf16[256,1024]{1,0:T(8,128)(2,1)S(1)}, u32[]{:S(2)}, u32[]{:S(2)}) collective-permute-start(bf16[256,1024]{1,0:T(8,128)(2,1)} %get-tuple-element.33), channel_id=1, source_target_pairs={{0,4},{1,5},{2,6},{3,7},{4,0},{5,1},{6,2},{7,3},{8,12},{9,13},{10,... | collective-permute-start | bytes 1572872 | tf_op jit(solution)/shard_map/ppermute | solution.py:30
  113.6 11.5 %copy-start.19 = (bf16[256,512]{1,0:T(8,128)(2,1)}, bf16[256,512]{1,0:T(8,128)(2,1)S(1)}, u32[]{:S(2)}) copy-start(bf16[256,512]{1,0:T(8,128)(2,1)S(1)} %collective-permute-done.15.rest_5_) | copy-start | bytes 786436
  113.6 29.4 %collective-permute-start.10 = (bf16[256,1024]{1,0:T(8,128)(2,1)}, bf16[256,1024]{1,0:T(8,128)(2,1)S(1)}, u32[]{:S(2)}, u32[]{:S(2)}) collective-permute-start(bf16[256,1024]{1,0:T(8,128)(2,1)} %get-tuple-element.34), channel_id=1, source_target_pairs={{0,2},{1,3},{2,4},{3,5},{4,6},{5,7},{6,0},{7,1},{8,10},{9,11},{10,... | collective-permute-start | bytes 1572872 | tf_op jit(solution)/shard_map/ppermute | solution.py:30
  118.0 7.1 %copy-start.20 = (bf16[256,512]{1,0:T(8,128)(2,1)}, bf16[256,512]{1,0:T(8,128)(2,1)S(1)}, u32[]{:S(2)}) copy-start(bf16[256,512]{1,0:T(8,128)(2,1)S(1)} %collective-permute-done.14.rest_4_) | copy-start | bytes 786436
  118.0 24.9 %collective-permute-start.13 = (bf16[256,512]{1,0:T(8,128)(2,1)S(1)}, bf16[256,512]{1,0:T(8,128)(2,1)S(1)}, u32[]{:S(2)}, u32[]{:S(2)}) collective-permute-start(bf16[256,512]{1,0:T(8,128)(2,1)S(1)} %copy-done.15), channel_id=1, source_target_pairs={{0,2},{1,3},{2,4},{3,5},{4,6},{5,7},{6,0},{7,1},{8,10},{9,11},{10,... | collective-permute-start | bytes 786440 | tf_op jit(solution)/shard_map/ppermute | solution.py:30
  142.9 0.7 copy-start.21
  142.9 0.9 copy-start.16
  142.9 1.0 copy-start.17
  143.9 0.8 copy-start.18
  148.6 8.2 %copy-start.1 = (bf16[256,4096]{1,0:T(8,128)(2,1)S(1)}, bf16[256,4096]{1,0:T(8,128)(2,1)}, u32[]{:S(2)}) copy-start(bf16[256,4096]{1,0:T(8,128)(2,1)} %copy-done) | copy-start | bytes 6291460
  156.3 1.0 copy-start.11
  156.3 53.4 %collective-permute-start.16 = (bf16[256,4096]{1,0:T(8,128)(2,1)}, bf16[256,4096]{1,0:T(8,128)(2,1)}, u32[]{:S(2)}, u32[]{:S(2)}) collective-permute-start(bf16[256,4096]{1,0:T(8,128)(2,1)} %shard_map.87), channel_id=1, source_target_pairs={{0,248},{8,0},{16,8},{24,16},{32,24},{40,32},{48,40},{56,48},{64,5... | collective-permute-start | bytes 6291464 | tf_op jit(solution)/shard_map/ppermute | solution.py:20
  158.7 16.8 %collective-permute-start.19 = (bf16[256,1536]{1,0:T(8,128)(2,1)}, bf16[256,1536]{1,0:T(8,128)(2,1)S(1)}, u32[]{:S(2)}, u32[]{:S(2)}) collective-permute-start(bf16[256,1536]{1,0:T(8,128)(2,1)} %get-tuple-element.35), channel_id=1, source_target_pairs={{0,6},{1,7},{2,0},{3,1},{4,2},{5,3},{6,4},{7,5},{8,14},{9,15},{10,... | collective-permute-start | bytes 2359304 | tf_op jit(solution)/shard_map/ppermute | solution.py:30
  159.1 18.8 %collective-permute-start.18 = (bf16[256,1536]{1,0:T(8,128)(2,1)}, bf16[256,1536]{1,0:T(8,128)(2,1)S(1)}, u32[]{:S(2)}, u32[]{:S(2)}) collective-permute-start(bf16[256,1536]{1,0:T(8,128)(2,1)} %get-tuple-element.36), channel_id=1, source_target_pairs={{0,4},{1,5},{2,6},{3,7},{4,0},{5,1},{6,2},{7,3},{8,12},{9,13},{10,... | collective-permute-start | bytes 2359304 | tf_op jit(solution)/shard_map/ppermute | solution.py:30
  159.7 37.4 %collective-permute-start.17 = (bf16[256,1536]{1,0:T(8,128)(2,1)}, bf16[256,1536]{1,0:T(8,128)(2,1)S(1)}, u32[]{:S(2)}, u32[]{:S(2)}) collective-permute-start(bf16[256,1536]{1,0:T(8,128)(2,1)} %get-tuple-element.37), channel_id=1, source_target_pairs={{0,2},{1,3},{2,4},{3,5},{4,6},{5,7},{6,0},{7,1},{8,10},{9,11},{10,... | collective-permute-start | bytes 2359304 | tf_op jit(solution)/shard_map/ppermute | solution.py:30
  164.6 44.0 %collective-permute-start.21 = (bf16[512,512]{1,0:T(8,128)(2,1)}, bf16[512,512]{1,0:T(8,128)(2,1)S(1)}, u32[]{:S(2)}, u32[]{:S(2)}) collective-permute-start(bf16[512,512]{1,0:T(8,128)(2,1)} %shard_map.90), channel_id=1, source_target_pairs={{0,1},{1,0},{2,3},{3,2},{4,5},{5,4},{6,7},{7,6},{8,9},{9,8},{10,11... | collective-permute-start | bytes 1572872 | tf_op jit(solution)/shard_map/ppermute | solution.py:34
  175.5 21.6 %copy-start.12 = (bf16[256,1536]{1,0:T(8,128)(2,1)}, bf16[256,1536]{1,0:T(8,128)(2,1)S(1)}, u32[]{:S(2)}) copy-start(bf16[256,1536]{1,0:T(8,128)(2,1)S(1)} %collective-permute-done.19.rest_2_) | copy-start | bytes 2359300
  177.9 19.3 %copy-start.13 = (bf16[256,1536]{1,0:T(8,128)(2,1)}, bf16[256,1536]{1,0:T(8,128)(2,1)S(1)}, u32[]{:S(2)}) copy-start(bf16[256,1536]{1,0:T(8,128)(2,1)S(1)} %collective-permute-done.18.rest_1_) | copy-start | bytes 2359300
  197.2 0.9 copy-start.14
  201.7 6.9 %copy-start.9 = (f32[512,512]{1,0:T(8,128)S(1)}, f32[512,512]{1,0:T(8,128)}, u32[]{:S(2)}) copy-start(f32[512,512]{1,0:T(8,128)} %shard_map.86) | copy-start | bytes 3145732
  201.7 72.7 %collective-permute-start.20 = (bf16[512,512]{1,0:T(8,128)(2,1)}, bf16[512,512]{1,0:T(8,128)(2,1)S(1)}, u32[]{:S(2)}, u32[]{:S(2)}) collective-permute-start(bf16[512,512]{1,0:T(8,128)(2,1)} %shard_map.89), channel_id=1, source_target_pairs={{0,1},{1,0},{2,3},{3,2},{4,5},{5,4},{6,7},{7,6},{8,9},{9,8},{10,11... | collective-permute-start | bytes 1572872 | tf_op jit(solution)/shard_map/ppermute | solution.py:34
  209.7 64.7 %copy-start.10 = (f32[512,512]{1,0:T(8,128)S(1)}, f32[512,512]{1,0:T(8,128)}, u32[]{:S(2)}) copy-start(f32[512,512]{1,0:T(8,128)} %shard_map.91) | copy-start | bytes 3145732

commit v3 on v2

v3 whole, which is shorter than its diff:
```python
import jax
import jax.numpy as jnp
from jax import lax
from jax.experimental import pallas as pl
from jax.experimental.pallas import tpu as pltpu
from jax.sharding import PartitionSpec as P

INV_ROOT_TWO = 0.7071067811865476
INV_ROOT_TWO_PI = 0.3989422804014327
X_SIZE = 4
Y_SIZE = 2
F32 = jnp.float32
BF16 = jnp.bfloat16


def over_section(array, by):
    devices = lax.axis_size("section")
    return lax.ppermute(
        array, "section", [(i, (i + by) % devices) for i in range(devices)]
    )


def over_x(array, by):
    pairs = []
    for x in range(X_SIZE):
        for y in range(Y_SIZE):
            pairs.append((x * Y_SIZE + y, ((x + by) % X_SIZE) * Y_SIZE + y))
    return lax.ppermute(array, "dp", pairs)


def swap_y(array):
    return lax.ppermute(array, "dp", [(i, i ^ 1) for i in range(X_SIZE * Y_SIZE)])


def gelu_pair(preact):
    normal_cdf = 0.5 * (1.0 + lax.erf(preact * INV_ROOT_TWO))
    density = jnp.exp(-0.5 * preact * preact) * INV_ROOT_TWO_PI
    return (preact * normal_cdf, normal_cdf + preact * density)


def times(left, right):
    return jnp.dot(left, right, preferred_element_type=F32)


def times_transposed(left, right):
    return lax.dot_general(
        left, right, (((1,), (1,)), ((), ())), preferred_element_type=F32
    )


def contract_tokens(left, right):
    return lax.dot_general(
        left, right, (((0,), (0,)), ((), ())), preferred_element_type=F32
    )


def weight_items(refs):
    near, far = refs[:6], refs[6:]
    rows = far[0].shape[0]
    items = [((ref, 0), (ref, rows)) for ref in near]
    items += [((far[k], 0), (far[k + 1], 0)) for k in range(0, len(far), 2)]
    return rows, items


def columns_of(starts, block, width):
    return pl.ds(pl.multiple_of(starts[block], width), width)


class Loads:
    def __init__(self, semaphores):
        self.semaphores, self.copies, self.waited = semaphores, [], set()

    def start(self, source, target):
        number = len(self.copies)
        copy = pltpu.make_async_copy(source, target, self.semaphores.at[number])
        copy.start()
        self.copies.append((copy, target))
        return number

    def get(self, number):
        copy, target = self.copies[number]
        if number not in self.waited:
            self.waited.add(number)
            copy.wait()
        return target

    def finish(self):
        for number in range(len(self.copies)):
            self.get(number)


def first_kernel(starts, inputs, *rest):
    (rows, items), rest = weight_items(rest[:8]), rest[8:]
    partial, left, up, semaphores = rest
    loads, numbers = Loads(semaphores), []
    for block, ((ref, row), _) in enumerate(items):
        columns = columns_of(starts, block, rows)
        numbers.append(
            (
                loads.start(inputs.at[:, columns], left.at[block]),
                loads.start(ref.at[pl.ds(row, rows)], up.at[block]),
            )
        )
    total = None
    for one, two in numbers:
        product = times(loads.get(one)[...], loads.get(two)[...])
        total = product if total is None else total + product
    partial[...] = total


def layer_kernel(starts, inputs, partial, *rest):
    (rows, items), rest = weight_items(rest[:10]), rest[10:]
    hidden, slope, output, left, up, down, result, semaphores = rest
    loads, lefts, downs = Loads(semaphores), [], []
    last = len(items) - 1
    order = [last, *range(last)]
    ref, row = items[last][0]
    up_number = loads.start(ref.at[pl.ds(row, rows)], up)
    for block in order:
        columns = columns_of(starts, block, rows)
        lefts.append(loads.start(inputs.at[:, columns], left.at[block]))
        ref, row = items[block][1]
        downs.append(loads.start(ref.at[pl.ds(row, rows)], down.at[block]))
    product = times(loads.get(lefts[0])[...], loads.get(up_number)[...])
    activated, gradient = gelu_pair(partial[...] + product)
    inner = activated.astype(BF16)
    hidden[...] = inner
    slope[...] = gradient
    for block, one, two in zip(order, lefts, downs):
        branch = times_transposed(inner, loads.get(two)[...])
        total = loads.get(one)[...].astype(F32) + branch
        result[block] = total.astype(BF16)
        loads.start(
            result.at[block], output.at[:, columns_of(starts, block, rows)]
        )
    loads.finish()


def back_kernel(starts, upstream, slope, *rest):
    (rows, items), rest = weight_items(rest[:10]), rest[10:]
    dpre, output, left, up, down, result, semaphores = rest
    loads, numbers, ups = Loads(semaphores), [], []
    for block, (_, (ref, row)) in enumerate(items):
        columns = columns_of(starts, block, rows)
        numbers.append(
            (
                loads.start(upstream.at[:, columns], left.at[block]),
                loads.start(ref.at[pl.ds(row, rows)], down.at[block]),
            )
        )
    for block, ((ref, row), _) in enumerate(items):
        ups.append(loads.start(ref.at[pl.ds(row, rows)], up.at[block]))
    dhidden = None
    for one, two in numbers:
        product = times(loads.get(one)[...], loads.get(two)[...])
        dhidden = product if dhidden is None else dhidden + product
    inner = (dhidden * slope[...]).astype(BF16)
    dpre[...] = inner
    for block, number in enumerate(ups):
        back = times_transposed(inner, loads.get(number)[...])
        total = left[block].astype(F32) + back
        result[block] = total.astype(BF16)
        loads.start(
            result.at[block], output.at[:, columns_of(starts, block, rows)]
        )
    loads.finish()


def shadow_kernel(starts, inputs, *rest):
    (rows, items), rest = weight_items(rest[:10]), rest[10:]
    output, left, up, down, result, semaphores = rest
    loads, numbers = Loads(semaphores), []
    for block, ((ref, row), _) in enumerate(items):
        columns = columns_of(starts, block, rows)
        numbers.append(
            (
                loads.start(inputs.at[:, columns], left.at[block]),
                loads.start(ref.at[pl.ds(row, rows)], up.at[block]),
            )
        )
    downs = []
    for block, (_, (ref, row)) in enumerate(items):
        downs.append(loads.start(ref.at[pl.ds(row, rows)], down.at[block]))
    preact = None
    for one, two in numbers:
        first = times(loads.get(one)[...], loads.get(two)[...])
        preact = first if preact is None else preact + first
    hidden = gelu_pair(preact)[0].astype(BF16)
    for block, number in enumerate(downs):
        branch = times_transposed(hidden, loads.get(number)[...])
        total = left[block].astype(F32) + branch
        result[block] = total.astype(BF16)
        loads.start(
            result.at[block], output.at[:, columns_of(starts, block, rows)]
        )
    loads.finish()


def part_kernel(starts, whole, other, *rest):
    pieces, (part, lefts, rights, semaphores) = rest[:-4], rest[-4:]
    rows, width = part.shape
    loads, numbers = Loads(semaphores), []
    numbers.append(
        (
            loads.start(whole.at[:, columns_of(starts, 0, rows)], lefts.at[0]),
            loads.start(other, rights.at[0]),
        )
    )
    for k, piece in enumerate(pieces):
        right = piece.at[:, pl.ds(piece.shape[1] - width, width)]
        numbers.append(
            (
                loads.start(
                    piece.at[:, columns_of(starts, 1, rows)], lefts.at[k + 1]
                ),
                loads.start(right, rights.at[k + 1]),
            )
        )
    total = None
    for one, two in numbers:
        product = contract_tokens(loads.get(one)[...], loads.get(two)[...])
        total = product if total is None else total + product
    part[...] = total.astype(part.dtype)


def copy_kernel(source, target, held, semaphores):
    loads, count = Loads(semaphores), semaphores.shape[0] // 2
    rows = source.shape[0] // count
    for k in range(count):
        some = pl.ds(k * rows, rows)
        loads.start(source.at[some], held.at[some])
    for k in range(count):
        some = pl.ds(k * rows, rows)
        loads.get(k)
        loads.start(held.at[some], target.at[some])
    loads.finish()


ANY = pl.BlockSpec(memory_space=pl.ANY)
VMEM = pl.BlockSpec(memory_space=pltpu.VMEM)
SMEM = pl.BlockSpec(memory_space=pltpu.SMEM)


def local_call(kernel, outs, in_specs, out_specs, scratch, copies, *arrays):
    return pl.pallas_call(
        kernel,
        out_shape=outs,
        in_specs=in_specs,
        out_specs=out_specs,
        scratch_shapes=[*scratch, pltpu.SemaphoreType.DMA((copies,))],
        compiler_params=pltpu.CompilerParams(vmem_limit_bytes=56 * 2**20),
        cost_estimate=pl.CostEstimate(flops=1, bytes_accessed=1, transcendentals=0),
    )(*arrays)


def on_device(handoff, grad_back, w_in, w_out):
    position = lax.axis_index("dp")
    x, y = position // Y_SIZE, position % Y_SIZE
    rows, width = w_in.shape[1:]
    tokens, features = handoff.shape[1:]
    places = ((0, 0), (0, 1), (3, 0), (1, 0), (3, 1), (1, 1), (2, 0), (2, 1))
    starts = jnp.stack(
        [(lax.rem(x + i, X_SIZE) * Y_SIZE + (y + j) % Y_SIZE) * rows for i, j in places]
    ).astype(jnp.int32)

    own = jnp.concatenate([w_in[0], w_out[0]], axis=0)
    partner = swap_y(own)
    behind, ahead = over_x(own, 1), over_x(own, -1)
    handoff, partner, behind, ahead = lax.optimization_barrier(
        (handoff, partner, behind, ahead)
    )
    behind_partner, ahead_partner = over_x(partner, 1), over_x(partner, -1)
    far_in, far_out = over_x(behind[:rows], 1), over_x(ahead[rows:], -1)
    inputs = over_section(handoff[0], 1)
    far_partner_in = over_x(behind_partner[:rows], 1)
    far_partner_out = over_x(ahead_partner[rows:], -1)
    grad_back, inputs = lax.optimization_barrier((grad_back, inputs))
    upstream = over_section(grad_back[0], -1)
    weights = (own, partner, behind, ahead, behind_partner, ahead_partner)
    weights += (far_in, far_out, far_partner_in, far_partner_out)

    blocks = X_SIZE * Y_SIZE
    activations = jax.ShapeDtypeStruct((tokens, features), BF16)
    half = jax.ShapeDtypeStruct((tokens, width), BF16)
    half_wide = jax.ShapeDtypeStruct((tokens, width), F32)
    token_blocks = pltpu.VMEM((blocks, tokens, rows), BF16)
    weight_blocks = pltpu.VMEM((blocks, rows, width), BF16)
    any_weights = [ANY] * len(weights)
    wide = Y_SIZE * rows

    def cut(array, by):
        first = lax.rem(x + by, X_SIZE) * wide
        return lax.dynamic_slice_in_dim(array, first, wide, axis=1)

    partial = local_call(
        first_kernel,
        half_wide,
        [SMEM, ANY] + [ANY] * 8,
        VMEM,
        [token_blocks, weight_blocks],
        2 * blocks,
        starts,
        inputs,
        *weights[:8],
    )
    hidden, slope, layer_out = local_call(
        layer_kernel,
        (half, half_wide, activations),
        [SMEM, ANY, VMEM] + any_weights,
        (VMEM, VMEM, ANY),
        [token_blocks, pltpu.VMEM((rows, width), BF16), weight_blocks, token_blocks],
        3 * blocks + 1,
        starts,
        inputs,
        partial,
        *weights,
    )
    arrived = over_section(layer_out, 1)
    out_pieces = [
        over_x(jnp.concatenate([cut(upstream, by), hidden], axis=1), by)
        for by in range(1, X_SIZE)
    ]
    dpre, input_grad = local_call(
        back_kernel,
        (half, activations),
        [SMEM, ANY, VMEM] + any_weights,
        (VMEM, ANY),
        [token_blocks, weight_blocks, weight_blocks, token_blocks],
        4 * blocks,
        starts,
        upstream,
        slope,
        *weights,
    )
    arrived, input_grad = lax.optimization_barrier((arrived, input_grad))
    shadow_back = local_call(
        shadow_kernel,
        activations,
        [SMEM, ANY] + any_weights,
        ANY,
        [token_blocks, weight_blocks, weight_blocks, token_blocks],
        4 * blocks,
        starts,
        arrived,
        *weights,
    )
    shadow = over_section(shadow_back, -1)

    in_pieces = [
        jnp.concatenate([cut(inputs, by), dpre], axis=1) for by in range(1, X_SIZE)
    ]
    in_pieces, out_pieces, shadow_back = lax.optimization_barrier(
        (in_pieces, out_pieces, shadow_back)
    )
    in_pieces = [over_x(piece, by + 1) for by, piece in enumerate(in_pieces)]
    ours = jnp.stack([x * wide + y * rows, y * rows]).astype(jnp.int32)
    apart = (1 - y) * rows
    other = jnp.stack([x * wide + apart, apart]).astype(jnp.int32)

    def part(where, kind, *arrays):
        return local_call(
            part_kernel,
            jax.ShapeDtypeStruct((rows, width), kind),
            [SMEM] + [ANY] * len(arrays),
            VMEM,
            [
                pltpu.VMEM((X_SIZE, tokens, rows), BF16),
                pltpu.VMEM((X_SIZE, tokens, width), BF16),
            ],
            2 * X_SIZE,
            where,
            *arrays,
        )

    received_out = swap_y(part(other, BF16, upstream, hidden, *out_pieces))
    mine_out = part(ours, F32, upstream, hidden, *out_pieces)
    received_in = swap_y(part(other, BF16, inputs, dpre, *in_pieces))
    mine_in = part(ours, F32, inputs, dpre, *in_pieces)
    grad_out = mine_out + received_out.astype(F32)
    shadow = local_call(
        copy_kernel,
        activations,
        [ANY],
        ANY,
        [pltpu.VMEM((tokens, features), BF16)],
        16,
        shadow,
    )
    shadow, received_in, grad_out = lax.optimization_barrier(
        (shadow, received_in, grad_out)
    )
    grad_in = mine_in + received_in.astype(F32)
    return (
        layer_out[None],
        shadow[None],
        input_grad[None],
        grad_in[None],
        grad_out[None],
    )


def solution(mesh):
    spec = P("section", "dp", None)
    return jax.shard_map(
        on_device,
        mesh=mesh,
        in_specs=(spec,) * 4,
        out_specs=(spec,) * 5,
        check_vma=False,
    )
```

time: 276 us -> 189 us (0.68)
  Pallas kernels: 106 us -> 45.5 us
  waiting for transfers between devices: 113 us -> 91.9 us
  local copies, waits for them, and re-layouts: 12.6 us -> 5.03 us
    pallas_call x9, Pallas kernels: 106 us -> 45.5 us  [local_call(): pl.pallas_call(kernel, out_shape=outs, in_specs=in_specs, out_specs=out_s...]
    ppermute x15 -> x14, waiting for transfers between devices: 76 us -> 63.1 us  [over_x(): return lax.ppermute(array, 'dp', pairs)]
    unnamed x44 -> x30, local copies, waits for them, and re-layouts: 9.06 us -> 0.93 us
    ppermute x4, waiting for transfers between devices: 17.2 us -> 9.6 us  [over_section(): lax.ppermute(array, 'section', [(i, (i + by) % devices) for i in range(de...]
    ppermute x15 -> x14, starting transfers between devices: 19.5 us -> 19.8 us  [over_x(): return lax.ppermute(array, 'dp', pairs)]
  transfers between devices with their start and end apart: 22 -> 21, of which waited for: 10 -> 10; matrix products, arithmetic and copies ran while one was open for 3% -> 5% of each run, Pallas kernels for 31% -> 24%
where the time goes in v3:
time: 189 us
  waiting for transfers between devices  91.9 us (49%)
  Pallas kernels  45.5 us (24%)
  starting transfers between devices  37.5 us (20%)
  other arithmetic  7.84 us (4%)
  local copies, waits for them, and re-layouts  5.03 us (3%)
    ppermute x14, waiting for transfers between devices, over_x(): return lax.ppermute(array, 'dp', pairs)  63.1 us
    pallas_call x9, Pallas kernels, local_call(): pl.pallas_call(kernel, out_shape=outs, in_specs=in_specs, out_specs=out_s...  45.5 us
    ppermute x14, starting transfers between devices, over_x(): return lax.ppermute(array, 'dp', pairs)  19.8 us
    ppermute x3, waiting for transfers between devices, swap_y(): lax.ppermute(array, 'dp', [(i, i ^ 1) for i in range(X_SIZE * Y_SIZE)])  19.2 us
    ppermute x4, waiting for transfers between devices, over_section(): lax.ppermute(array, 'section', [(i, (i + by) % devices) for i in range(de...  9.6 us
    ppermute x3, starting transfers between devices, swap_y(): lax.ppermute(array, 'dp', [(i, i ^ 1) for i in range(X_SIZE * Y_SIZE)])  9.44 us
    ppermute x4, starting transfers between devices, over_section(): lax.ppermute(array, 'section', [(i, (i + by) % devices) for i in range(de...  8.27 us
  transfers between devices with their start and end apart: 21, of which 10 were waited for; matrix products, arithmetic and copies ran while one was open for 5% of the time, Pallas kernels for 24%

profile of v3, /device:TPU:1, one launch (start us, length us, event | category | flops | bytes accessed | tf_op | source)
XLA Modules:
  0.0 188.6 jit_solution(13740438405384319550)
XLA Ops:
  0.6 1.4 pad_maximum_fusion.6.rest_0_
  2.1 3.8 %collective-permute-start = (bf16[1024,512]{1,0:T(8,128)(2,1)S(1)}, bf16[1024,512]{1,0:T(8,128)(2,1)S(1)}, u32[]{:S(2)}, u32[]{:S(2)}) collective-permute-start(bf16[1024,512]{1,0:T(8,128)(2,1)S(1)} %pad_maximum_fusion.6.rest_0_), channel_id=1, source_target_pairs={{0,1},{1,0},{2,3},{3,2},{4,5},{5,4},{6,7},{7,6},{8,9},{9,8},{10,11... | collective-permute-start | bytes 3145736 | tf_op jit(solution)/shard_map/ppermute | solution.py:32
  5.9 1.2 collective-permute-start.1
  7.1 1.5 collective-permute-start.2
  8.6 19.1 %collective-permute-done.rest_1_ = bf16[1024,512]{1,0:T(8,128)(2,1)S(1)} collective-permute-done((bf16[1024,512]{1,0:T(8,128)(2,1)S(1)}, bf16[1024,512]{1,0:T(8,128)(2,1)S(1)}, u32[]{:S(2)}, u32[]{:S(2)}) %collective-permute-start) | collective-permute-done | bytes 1048608 | tf_op jit(solution)/shard_map/ppermute | solution.py:32
  27.7 3.1 %collective-permute-done.1.rest_2_ = bf16[1024,512]{1,0:T(8,128)(2,1)S(1)} collective-permute-done((bf16[1024,512]{1,0:T(8,128)(2,1)S(1)}, bf16[1024,512]{1,0:T(8,128)(2,1)S(1)}, u32[]{:S(2)}, u32[]{:S(2)}) %collective-permute-start.1) | collective-permute-done | bytes 1048608 | tf_op jit(solution)/shard_map/ppermute | solution.py:28
  30.8 2.2 %collective-permute-start.3 = (bf16[256,4096]{1,0:T(8,128)(2,1)S(1)}, bf16[256,4096]{1,0:T(8,128)(2,1)S(1)}, u32[]{:S(2)}, u32[]{:S(2)}) collective-permute-start(bf16[256,4096]{1,0:T(8,128)(2,1)S(1)} %bitcast.26), channel_id=1, source_target_pairs={{0,8},{8,16},{16,24},{24,32},{32,40},{40,48},{48,56},{56,64},{64,7... | collective-permute-start | bytes 6291464 | tf_op jit(solution)/shard_map/ppermute | solution.py:18
  33.1 1.1 collective-permute-start.4
  34.2 1.6 collective-permute-start.5
  35.9 2.7 %collective-permute-start.7 = (bf16[512,512]{1,0:T(8,128)(2,1)S(1)}, bf16[512,512]{1,0:T(8,128)(2,1)}, u32[]{:S(2)}, u32[]{:S(2)}) collective-permute-start(bf16[512,512]{1,0:T(8,128)(2,1)S(1)} %slice.13), channel_id=1, source_target_pairs={{0,6},{1,7},{2,0},{3,1},{4,2},{5,3},{6,4},{7,5},{8,14},{9,15},{10,... | collective-permute-start | bytes 1572872 | tf_op jit(solution)/shard_map/ppermute | solution.py:28
  38.7 20.5 %collective-permute-done.4.rest_4_ = bf16[1024,512]{1,0:T(8,128)(2,1)S(1)} collective-permute-done((bf16[1024,512]{1,0:T(8,128)(2,1)S(1)}, bf16[1024,512]{1,0:T(8,128)(2,1)S(1)}, u32[]{:S(2)}, u32[]{:S(2)}) %collective-permute-start.4) | collective-permute-done | bytes 1048608 | tf_op jit(solution)/shard_map/ppermute | solution.py:28
  59.2 0.9 slice.16
  60.1 0.9 slice.17
  61.0 2.7 %collective-permute-start.9 = (bf16[512,512]{1,0:T(8,128)(2,1)}, bf16[512,512]{1,0:T(8,128)(2,1)}, u32[]{:S(2)}, u32[]{:S(2)}) collective-permute-start(bf16[512,512]{1,0:T(8,128)(2,1)} %slice.17), channel_id=1, source_target_pairs={{0,6},{1,7},{2,0},{3,1},{4,2},{5,3},{6,4},{7,5},{8,14},{9,15},{10,... | collective-permute-start | bytes 1572872 | tf_op jit(solution)/shard_map/ppermute | solution.py:28
  63.7 1.6 collective-permute-start.11
  65.3 0.7 stack.53.starts
  66.0 4.6 %collective-permute-done.6.rest_6_ = bf16[512,512]{1,0:T(8,128)(2,1)} collective-permute-done((bf16[512,512]{1,0:T(8,128)(2,1)S(1)}, bf16[512,512]{1,0:T(8,128)(2,1)}, u32[]{:S(2)}, u32[]{:S(2)}) %collective-permute-start.6) | collective-permute-done | bytes 524320 | tf_op jit(solution)/shard_map/ppermute | solution.py:28
  70.5 4.5 %shard_map.83.partial = f32[256,512]{1,0:T(8,128)} custom-call(s32[8]{0:T(128)} %stack.53.starts, bf16[256,4096]{1,0:T(8,128)(2,1)} %copy-done, bf16[1024,512]{1,0:T(8,128)(2,1)} %copy-done.2, bf16[1024,512]{1,0:T(8,128)(2,1)} %copy-done.7, bf16[1024,512]{1,0:T(8,128)(2,1)} %copy-done.3, bf16[1024,512]{1,0:T(8,128)(2,1)} %copy-done.4, ...), custom_call_target="tpu_custom_call" | custom-call | flops 1 | bytes 1 | tf_op jit(solution)/shard_map/pallas_call | solution.py:245
  75.0 6.8 %collective-permute-done.8.rest_8_ = bf16[512,512]{1,0:T(8,128)(2,1)} collective-permute-done((bf16[512,512]{1,0:T(8,128)(2,1)}, bf16[512,512]{1,0:T(8,128)(2,1)}, u32[]{:S(2)}, u32[]{:S(2)}) %collective-permute-start.8) | collective-permute-done | bytes 524320 | tf_op jit(solution)/shard_map/ppermute | solution.py:28
  81.8 7.5 %shard_map.84 = (bf16[256,512]{1,0:T(8,128)(2,1)}, f32[256,512]{1,0:T(8,128)}, bf16[256,4096]{1,0:T(8,128)(2,1)}) custom-call(s32[8]{0:T(128)} %stack.53.starts, bf16[256,4096]{1,0:T(8,128)(2,1)} %copy-done, f32[256,512]{1,0:T(8,128)} %shard_map.83.partial, bf16[1024,512]{1,0:T(8,128)(2,1)} %copy-done.2, bf16[1024,512]{1,0:T(8,128)(2,1)} %copy-done.7, ...), custom_call_target="tpu_custom_call" | custom-call | flops 1 | bytes 1 | tf_op jit(solution)/shard_map/pallas_call | solution.py:245
  89.2 0.3 collective-permute-start.10
  89.6 1.5 constant_dynamic-slice_fusion
  91.1 0.2 pad_maximum_fusion.3
  91.3 0.8 collective-permute-start.13
  92.0 3.0 %collective-permute-start.14 = (bf16[256,1536]{1,0:T(8,128)(2,1)S(1)}, bf16[256,1536]{1,0:T(8,128)(2,1)}, u32[]{:S(2)}, u32[]{:S(2)}) collective-permute-start(bf16[256,1536]{1,0:T(8,128)(2,1)S(1)} %get-tuple-element.56), channel_id=1, source_target_pairs={{0,4},{1,5},{2,6},{3,7},{4,0},{5,1},{6,2},{7,3},{8,12},{9,13},{10,... | collective-permute-start | bytes 2359304 | tf_op jit(solution)/shard_map/ppermute | solution.py:28
  95.1 0.8 collective-permute-start.15
  95.8 8.5 %shard_map.85 = (bf16[256,512]{1,0:T(8,128)(2,1)}, bf16[256,4096]{1,0:T(8,128)(2,1)}) custom-call(s32[8]{0:T(128)} %stack.53.starts, bf16[256,4096]{1,0:T(8,128)(2,1)} %collective-permute-done.11.upstream.whole, f32[256,512]{1,0:T(8,128)} %get-tuple-element.34.slope, bf16[1024,512]{1,0:T(8,128)(2,1)} %copy-done.2, bf16[1024,512]{1,0:T(8,128)(2,1)} %copy-done.7, ...), custom_call_target="tpu_custom_call" | custom-call | flops 1 | bytes 1 | tf_op jit(solution)/shard_map/pallas_call | solution.py:245
  104.4 9.5 %collective-permute-done.10.inputs = bf16[256,4096]{1,0:T(8,128)(2,1)} collective-permute-done((bf16[256,4096]{1,0:T(8,128)(2,1)}, bf16[256,4096]{1,0:T(8,128)(2,1)}, u32[]{:S(2)}, u32[]{:S(2)}) %collective-permute-start.10) | collective-permute-done | bytes 2097184 | tf_op jit(solution)/shard_map/ppermute | solution.py:18
  113.9 7.7 %shard_map.86 = bf16[256,4096]{1,0:T(8,128)(2,1)} custom-call(s32[8]{0:T(128)} %stack.53.starts, bf16[256,4096]{1,0:T(8,128)(2,1)} %collective-permute-done.10.inputs, bf16[1024,512]{1,0:T(8,128)(2,1)} %copy-done.2, bf16[1024,512]{1,0:T(8,128)(2,1)} %copy-done.7, bf16[1024,512]{1,0:T(8,128)(2,1)} %copy-done.3, bf16[1024,512]{1,0:T(8,128)(2,1)} %copy-done.4, ...), custom_call_target="tpu_custom_call" | custom-call | flops 1 | bytes 1 | tf_op jit(solution)/shard_map/pallas_call | solution.py:245
  121.6 4.2 %collective-permute-start.12 = (bf16[256,4096]{1,0:T(8,128)(2,1)}, bf16[256,4096]{1,0:T(8,128)(2,1)}, u32[]{:S(2)}, u32[]{:S(2)}) collective-permute-start(bf16[256,4096]{1,0:T(8,128)(2,1)} %shard_map.86), channel_id=1, source_target_pairs={{0,248},{8,0},{16,8},{24,16},{32,24},{40,32},{48,40},{56,48},{64,5... | collective-permute-start | bytes 6291464 | tf_op jit(solution)/shard_map/ppermute | solution.py:18
  125.9 1.6 pad_maximum_fusion
  127.5 1.3 collective-permute-done.14.rest_1_
  128.8 1.8 collective-permute-start.16
  130.6 2.5 %collective-permute-start.17 = (bf16[256,1536]{1,0:T(8,128)(2,1)}, bf16[256,1536]{1,0:T(8,128)(2,1)S(1)}, u32[]{:S(2)}, u32[]{:S(2)}) collective-permute-start(bf16[256,1536]{1,0:T(8,128)(2,1)} %get-tuple-element.40), channel_id=1, source_target_pairs={{0,4},{1,5},{2,6},{3,7},{4,0},{5,1},{6,2},{7,3},{8,12},{9,13},{10,... | collective-permute-start | bytes 2359304 | tf_op jit(solution)/shard_map/ppermute | solution.py:28
  133.1 0.6 pad_add_fusion.starts
  133.7 3.6 %shard_map.90 = bf16[512,512]{1,0:T(8,128)(2,1)} custom-call(s32[2]{0:T(128)} %pad_add_fusion.starts, bf16[256,4096]{1,0:T(8,128)(2,1)} %collective-permute-done.11.upstream.whole, bf16[256,512]{1,0:T(8,128)(2,1)} %get-tuple-element.38.other, bf16[256,1536]{1,0:T(8,128)(2,1)} %copy-done.9, bf16[256,1536]{1,0:T(8,128)(2,1)} %collective-permute-done.14.rest_1_, ...), custom_call_target="tpu_custom_call" | custom-call | flops 1 | bytes 1 | tf_op jit(solution)/shard_map/pallas_call | solution.py:245
  137.4 3.1 %collective-permute-start.20 = (bf16[512,512]{1,0:T(8,128)(2,1)}, bf16[512,512]{1,0:T(8,128)(2,1)S(1)}, u32[]{:S(2)}, u32[]{:S(2)}) collective-permute-start(bf16[512,512]{1,0:T(8,128)(2,1)} %shard_map.90), channel_id=1, source_target_pairs={{0,1},{1,0},{2,3},{3,2},{4,5},{5,4},{6,7},{7,6},{8,9},{9,8},{10,11... | collective-permute-start | bytes 1572872 | tf_op jit(solution)/shard_map/ppermute | solution.py:32
  140.5 8.0 %collective-permute-done.16.rest_0_ = bf16[256,1536]{1,0:T(8,128)(2,1)S(1)} collective-permute-done((bf16[256,1536]{1,0:T(8,128)(2,1)}, bf16[256,1536]{1,0:T(8,128)(2,1)S(1)}, u32[]{:S(2)}, u32[]{:S(2)}) %collective-permute-start.16) | collective-permute-done | bytes 786464 | tf_op jit(solution)/shard_map/ppermute | solution.py:28
  148.5 18.9 %collective-permute-done.17.rest_1_ = bf16[256,1536]{1,0:T(8,128)(2,1)S(1)} collective-permute-done((bf16[256,1536]{1,0:T(8,128)(2,1)}, bf16[256,1536]{1,0:T(8,128)(2,1)S(1)}, u32[]{:S(2)}, u32[]{:S(2)}) %collective-permute-start.17) | collective-permute-done | bytes 786464 | tf_op jit(solution)/shard_map/ppermute | solution.py:28
  167.4 0.9 copy-done.11
  168.2 3.6 %shard_map.88 = bf16[512,512]{1,0:T(8,128)(2,1)} custom-call(s32[2]{0:T(128)} %pad_add_fusion.starts, bf16[256,4096]{1,0:T(8,128)(2,1)} %copy-done, bf16[256,512]{1,0:T(8,128)(2,1)} %get-tuple-element.37.other, bf16[256,1536]{1,0:T(8,128)(2,1)} %copy-done.10, bf16[256,1536]{1,0:T(8,128)(2,1)} %copy-done.11, bf16[256,1536]{1,0:T(8,128)(2,1)} %collective-permute-done.18.rest_2_), custom_call_target="tpu_custom_call" | custom-call | flops 1 | bytes 1 | tf_op jit(solution)/shard_map/pallas_call | solution.py:245
  171.8 2.5 %collective-permute-start.19 = (bf16[512,512]{1,0:T(8,128)(2,1)}, bf16[512,512]{1,0:T(8,128)(2,1)S(1)}, u32[]{:S(2)}, u32[]{:S(2)}) collective-permute-start(bf16[512,512]{1,0:T(8,128)(2,1)} %shard_map.88), channel_id=1, source_target_pairs={{0,1},{1,0},{2,3},{3,2},{4,5},{5,4},{6,7},{7,6},{8,9},{9,8},{10,11... | collective-permute-start | bytes 1572872 | tf_op jit(solution)/shard_map/ppermute | solution.py:32
  174.4 0.6 pad_add_fusion.1.starts
  175.0 3.8 %shard_map.89 = f32[512,512]{1,0:T(8,128)} custom-call(s32[2]{0:T(128)} %pad_add_fusion.1.starts, bf16[256,4096]{1,0:T(8,128)(2,1)} %collective-permute-done.11.upstream.whole, bf16[256,512]{1,0:T(8,128)(2,1)} %get-tuple-element.38.other, bf16[256,1536]{1,0:T(8,128)(2,1)} %copy-done.9, bf16[256,1536]{1,0:T(8,128)(2,1)} %collective-permute-done.14.rest_1_, ...), custom_call_target="tpu_custom_call" | custom-call | flops 1 | bytes 1 | tf_op jit(solution)/shard_map/pallas_call | solution.py:245
  178.8 2.4 %convert_add_fusion = f32[512,512]{1,0:T(8,128)} fusion(f32[512,512]{1,0:T(8,128)} %shard_map.89, bf16[512,512]{1,0:T(8,128)(2,1)S(1)} %collective-permute-done.20), kind=kLoop, calls=%fused_computation.8 | loop fusion | flops 524288 | bytes 2621440 | tf_op jit(solution)/shard_map/add | solution.py:379
  181.2 3.8 %shard_map.91 = f32[512,512]{1,0:T(8,128)} custom-call(s32[2]{0:T(128)} %pad_add_fusion.1.starts, bf16[256,4096]{1,0:T(8,128)(2,1)} %copy-done, bf16[256,512]{1,0:T(8,128)(2,1)} %get-tuple-element.37.other, bf16[256,1536]{1,0:T(8,128)(2,1)} %copy-done.10, bf16[256,1536]{1,0:T(8,128)(2,1)} %copy-done.11, bf16[256,1536]{1,0:T(8,128)(2,1)} %collective-permute-done.18.rest_2_), custom_call_target="tpu_custom_call" | custom-call | flops 1 | bytes 1 | tf_op jit(solution)/shard_map/pallas_call | solution.py:245
  185.0 2.5 %shard_map.87 = bf16[256,4096]{1,0:T(8,128)(2,1)} custom-call(bf16[256,4096]{1,0:T(8,128)(2,1)} %collective-permute-done.12.source), custom_call_target="tpu_custom_call" | custom-call | flops 1 | bytes 1 | tf_op jit(solution)/shard_map/pallas_call | solution.py:245
  187.5 1.1 add_bitcast_fusion
  (47 shorter events, 0.4 us)
Async XLA Ops:
  0.6 30.2 %copy-start.14 = (bf16[1,256,4096]{2,1,0:T(8,128)(2,1)S(1)}, bf16[1,256,4096]{2,1,0:T(8,128)(2,1)}, u32[]{:S(2)}) copy-start(bf16[1,256,4096]{2,1,0:T(8,128)(2,1)} %param.4) | copy-start | bytes 6291460
  2.1 58.9 %copy-start.2 = (bf16[1024,512]{1,0:T(8,128)(2,1)}, bf16[1024,512]{1,0:T(8,128)(2,1)S(1)}, u32[]{:S(2)}) copy-start(bf16[1024,512]{1,0:T(8,128)(2,1)S(1)} %pad_maximum_fusion.6.rest_0_) | copy-start | bytes 3145732
  2.1 25.7 %collective-permute-start = (bf16[1024,512]{1,0:T(8,128)(2,1)S(1)}, bf16[1024,512]{1,0:T(8,128)(2,1)S(1)}, u32[]{:S(2)}, u32[]{:S(2)}) collective-permute-start(bf16[1024,512]{1,0:T(8,128)(2,1)S(1)} %pad_maximum_fusion.6.rest_0_), channel_id=1, source_target_pairs={{0,1},{1,0},{2,3},{3,2},{4,5},{5,4},{6,7},{7,6},{8,9},{9,8},{10,11... | collective-permute-start | bytes 3145736 | tf_op jit(solution)/shard_map/ppermute | solution.py:32
  5.9 24.9 %collective-permute-start.1 = (bf16[1024,512]{1,0:T(8,128)(2,1)S(1)}, bf16[1024,512]{1,0:T(8,128)(2,1)S(1)}, u32[]{:S(2)}, u32[]{:S(2)}) collective-permute-start(bf16[1024,512]{1,0:T(8,128)(2,1)S(1)} %pad_maximum_fusion.6.rest_0_), channel_id=1, source_target_pairs={{0,2},{1,3},{2,4},{3,5},{4,6},{5,7},{6,0},{7,1},{8,10},{9,11},{10,... | collective-permute-start | bytes 3145736 | tf_op jit(solution)/shard_map/ppermute | solution.py:28
  7.1 23.7 %collective-permute-start.2 = (bf16[1024,512]{1,0:T(8,128)(2,1)S(1)}, bf16[1024,512]{1,0:T(8,128)(2,1)S(1)}, u32[]{:S(2)}, u32[]{:S(2)}) collective-permute-start(bf16[1024,512]{1,0:T(8,128)(2,1)S(1)} %pad_maximum_fusion.6.rest_0_), channel_id=1, source_target_pairs={{0,6},{1,7},{2,0},{3,1},{4,2},{5,3},{6,4},{7,5},{8,14},{9,15},{10,... | collective-permute-start | bytes 3145736 | tf_op jit(solution)/shard_map/ppermute | solution.py:28
  27.7 37.6 %copy-start.7 = (bf16[1024,512]{1,0:T(8,128)(2,1)}, bf16[1024,512]{1,0:T(8,128)(2,1)S(1)}, u32[]{:S(2)}) copy-start(bf16[1024,512]{1,0:T(8,128)(2,1)S(1)} %collective-permute-done.rest_1_) | copy-start | bytes 3145732
  30.8 30.2 %copy-start.3 = (bf16[1024,512]{1,0:T(8,128)(2,1)}, bf16[1024,512]{1,0:T(8,128)(2,1)S(1)}, u32[]{:S(2)}) copy-start(bf16[1024,512]{1,0:T(8,128)(2,1)S(1)} %collective-permute-done.1.rest_2_) | copy-start | bytes 3145732
  30.8 30.2 %copy-start.4 = (bf16[1024,512]{1,0:T(8,128)(2,1)}, bf16[1024,512]{1,0:T(8,128)(2,1)S(1)}, u32[]{:S(2)}) copy-start(bf16[1024,512]{1,0:T(8,128)(2,1)S(1)} %collective-permute-done.2.rest_3_) | copy-start | bytes 3145732
  30.8 32.9 %collective-permute-start.3 = (bf16[256,4096]{1,0:T(8,128)(2,1)S(1)}, bf16[256,4096]{1,0:T(8,128)(2,1)S(1)}, u32[]{:S(2)}, u32[]{:S(2)}) collective-permute-start(bf16[256,4096]{1,0:T(8,128)(2,1)S(1)} %bitcast.26), channel_id=1, source_target_pairs={{0,8},{8,16},{16,24},{24,32},{32,40},{40,48},{48,56},{56,64},{64,7... | collective-permute-start | bytes 6291464 | tf_op jit(solution)/shard_map/ppermute | solution.py:18
  33.1 26.1 %collective-permute-start.4 = (bf16[1024,512]{1,0:T(8,128)(2,1)S(1)}, bf16[1024,512]{1,0:T(8,128)(2,1)S(1)}, u32[]{:S(2)}, u32[]{:S(2)}) collective-permute-start(bf16[1024,512]{1,0:T(8,128)(2,1)S(1)} %collective-permute-done.rest_1_), channel_id=1, source_target_pairs={{0,2},{1,3},{2,4},{3,5},{4,6},{5,7},{6,0},{7,1},{8,10},{9,11},{10,... | collective-permute-start | bytes 3145736 | tf_op jit(solution)/shard_map/ppermute | solution.py:28
  34.2 25.9 %collective-permute-start.5 = (bf16[1024,512]{1,0:T(8,128)(2,1)S(1)}, bf16[1024,512]{1,0:T(8,128)(2,1)S(1)}, u32[]{:S(2)}, u32[]{:S(2)}) collective-permute-start(bf16[1024,512]{1,0:T(8,128)(2,1)S(1)} %collective-permute-done.rest_1_), channel_id=1, source_target_pairs={{0,6},{1,7},{2,0},{3,1},{4,2},{5,3},{6,4},{7,5},{8,14},{9,15},{10,... | collective-permute-start | bytes 3145736 | tf_op jit(solution)/shard_map/ppermute | solution.py:28
  35.8 34.7 %collective-permute-start.6 = (bf16[512,512]{1,0:T(8,128)(2,1)S(1)}, bf16[512,512]{1,0:T(8,128)(2,1)}, u32[]{:S(2)}, u32[]{:S(2)}) collective-permute-start(bf16[512,512]{1,0:T(8,128)(2,1)S(1)} %slice.12), channel_id=1, source_target_pairs={{0,2},{1,3},{2,4},{3,5},{4,6},{5,7},{6,0},{7,1},{8,10},{9,11},{10,... | collective-permute-start | bytes 1572872 | tf_op jit(solution)/shard_map/ppermute | solution.py:28
  35.9 34.6 %collective-permute-start.7 = (bf16[512,512]{1,0:T(8,128)(2,1)S(1)}, bf16[512,512]{1,0:T(8,128)(2,1)}, u32[]{:S(2)}, u32[]{:S(2)}) collective-permute-start(bf16[512,512]{1,0:T(8,128)(2,1)S(1)} %slice.13), channel_id=1, source_target_pairs={{0,6},{1,7},{2,0},{3,1},{4,2},{5,3},{6,4},{7,5},{8,14},{9,15},{10,... | collective-permute-start | bytes 1572872 | tf_op jit(solution)/shard_map/ppermute | solution.py:28
  59.2 4.6 %copy-start.5 = (bf16[1024,512]{1,0:T(8,128)(2,1)}, bf16[1024,512]{1,0:T(8,128)(2,1)S(1)}, u32[]{:S(2)}) copy-start(bf16[1024,512]{1,0:T(8,128)(2,1)S(1)} %collective-permute-done.4.rest_4_) | copy-start | bytes 3145732
  60.1 21.7 %collective-permute-start.8 = (bf16[512,512]{1,0:T(8,128)(2,1)}, bf16[512,512]{1,0:T(8,128)(2,1)}, u32[]{:S(2)}, u32[]{:S(2)}) collective-permute-start(bf16[512,512]{1,0:T(8,128)(2,1)} %slice.16), channel_id=1, source_target_pairs={{0,2},{1,3},{2,4},{3,5},{4,6},{5,7},{6,0},{7,1},{8,10},{9,11},{10,... | collective-permute-start | bytes 1572872 | tf_op jit(solution)/shard_map/ppermute | solution.py:28
  60.1 3.7 %copy-start.6 = (bf16[1024,512]{1,0:T(8,128)(2,1)}, bf16[1024,512]{1,0:T(8,128)(2,1)S(1)}, u32[]{:S(2)}) copy-start(bf16[1024,512]{1,0:T(8,128)(2,1)S(1)} %collective-permute-done.5.rest_5_) | copy-start | bytes 3145732
  61.0 20.8 %collective-permute-start.9 = (bf16[512,512]{1,0:T(8,128)(2,1)}, bf16[512,512]{1,0:T(8,128)(2,1)}, u32[]{:S(2)}, u32[]{:S(2)}) collective-permute-start(bf16[512,512]{1,0:T(8,128)(2,1)} %slice.17), channel_id=1, source_target_pairs={{0,6},{1,7},{2,0},{3,1},{4,2},{5,3},{6,4},{7,5},{8,14},{9,15},{10,... | collective-permute-start | bytes 1572872 | tf_op jit(solution)/shard_map/ppermute | solution.py:28
  63.7 6.8 %copy-start = (bf16[256,4096]{1,0:T(8,128)(2,1)}, bf16[256,4096]{1,0:T(8,128)(2,1)S(1)}, u32[]{:S(2)}) copy-start(bf16[256,4096]{1,0:T(8,128)(2,1)S(1)} %collective-permute-done.3.inputs.whole) | copy-start | bytes 6291460
  63.7 25.9 %collective-permute-start.11 = (bf16[256,4096]{1,0:T(8,128)(2,1)}, bf16[256,4096]{1,0:T(8,128)(2,1)}, u32[]{:S(2)}, u32[]{:S(2)}) collective-permute-start(bf16[256,4096]{1,0:T(8,128)(2,1)} %bitcast.12), channel_id=1, source_target_pairs={{0,248},{8,0},{16,8},{24,16},{32,24},{40,32},{48,40},{56,48},{64,5... | collective-permute-start | bytes 6291464 | tf_op jit(solution)/shard_map/ppermute | solution.py:18
  89.2 1.8 copy-start.12
  89.2 24.7 %collective-permute-start.10 = (bf16[256,4096]{1,0:T(8,128)(2,1)}, bf16[256,4096]{1,0:T(8,128)(2,1)}, u32[]{:S(2)}, u32[]{:S(2)}) collective-permute-start(bf16[256,4096]{1,0:T(8,128)(2,1)} %get-tuple-element.32), channel_id=1, source_target_pairs={{0,8},{8,16},{16,24},{24,32},{32,40},{40,48},{48,56},{56,64},{64,7... | collective-permute-start | bytes 6291464 | tf_op jit(solution)/shard_map/ppermute | solution.py:18
  91.3 36.2 %collective-permute-start.13 = (bf16[256,1536]{1,0:T(8,128)(2,1)S(1)}, bf16[256,1536]{1,0:T(8,128)(2,1)S(1)}, u32[]{:S(2)}, u32[]{:S(2)}) collective-permute-start(bf16[256,1536]{1,0:T(8,128)(2,1)S(1)} %get-tuple-element.57), channel_id=1, source_target_pairs={{0,2},{1,3},{2,4},{3,5},{4,6},{5,7},{6,0},{7,1},{8,10},{9,11},{10,... | collective-permute-start | bytes 2359304 | tf_op jit(solution)/shard_map/ppermute | solution.py:28
  92.0 36.8 %collective-permute-start.14 = (bf16[256,1536]{1,0:T(8,128)(2,1)S(1)}, bf16[256,1536]{1,0:T(8,128)(2,1)}, u32[]{:S(2)}, u32[]{:S(2)}) collective-permute-start(bf16[256,1536]{1,0:T(8,128)(2,1)S(1)} %get-tuple-element.56), channel_id=1, source_target_pairs={{0,4},{1,5},{2,6},{3,7},{4,0},{5,1},{6,2},{7,3},{8,12},{9,13},{10,... | collective-permute-start | bytes 2359304 | tf_op jit(solution)/shard_map/ppermute | solution.py:28
  95.1 33.8 %collective-permute-start.15 = (bf16[256,1536]{1,0:T(8,128)(2,1)S(1)}, bf16[256,1536]{1,0:T(8,128)(2,1)}, u32[]{:S(2)}, u32[]{:S(2)}) collective-permute-start(bf16[256,1536]{1,0:T(8,128)(2,1)S(1)} %get-tuple-element.55), channel_id=1, source_target_pairs={{0,6},{1,7},{2,0},{3,1},{4,2},{5,3},{6,4},{7,5},{8,14},{9,15},{10,... | collective-permute-start | bytes 2359304 | tf_op jit(solution)/shard_map/ppermute | solution.py:28
  113.9 11.9 %copy-start.1 = (bf16[256,4096]{1,0:T(8,128)(2,1)S(1)}, bf16[256,4096]{1,0:T(8,128)(2,1)}, u32[]{:S(2)}) copy-start(bf16[256,4096]{1,0:T(8,128)(2,1)} %copy-done) | copy-start | bytes 6291460
  121.6 4.4 %copy-start.13 = (bf16[256,512]{1,0:T(8,128)(2,1)S(1)}, bf16[256,512]{1,0:T(8,128)(2,1)}, u32[]{:S(2)}) copy-start(bf16[256,512]{1,0:T(8,128)(2,1)} %get-tuple-element.37.other) | copy-start | bytes 786436
  121.6 63.4 %collective-permute-start.12 = (bf16[256,4096]{1,0:T(8,128)(2,1)}, bf16[256,4096]{1,0:T(8,128)(2,1)}, u32[]{:S(2)}, u32[]{:S(2)}) collective-permute-start(bf16[256,4096]{1,0:T(8,128)(2,1)} %shard_map.86), channel_id=1, source_target_pairs={{0,248},{8,0},{16,8},{24,16},{32,24},{40,32},{48,40},{56,48},{64,5... | collective-permute-start | bytes 6291464 | tf_op jit(solution)/shard_map/ppermute | solution.py:18
  127.5 6.2 %copy-start.9 = (bf16[256,1536]{1,0:T(8,128)(2,1)}, bf16[256,1536]{1,0:T(8,128)(2,1)S(1)}, u32[]{:S(2)}) copy-start(bf16[256,1536]{1,0:T(8,128)(2,1)S(1)} %collective-permute-done.13.rest_0_) | copy-start | bytes 2359300
  128.8 19.7 %collective-permute-start.16 = (bf16[256,1536]{1,0:T(8,128)(2,1)}, bf16[256,1536]{1,0:T(8,128)(2,1)S(1)}, u32[]{:S(2)}, u32[]{:S(2)}) collective-permute-start(bf16[256,1536]{1,0:T(8,128)(2,1)} %get-tuple-element.39), channel_id=1, source_target_pairs={{0,2},{1,3},{2,4},{3,5},{4,6},{5,7},{6,0},{7,1},{8,10},{9,11},{10,... | collective-permute-start | bytes 2359304 | tf_op jit(solution)/shard_map/ppermute | solution.py:28
  130.6 36.7 %collective-permute-start.17 = (bf16[256,1536]{1,0:T(8,128)(2,1)}, bf16[256,1536]{1,0:T(8,128)(2,1)S(1)}, u32[]{:S(2)}, u32[]{:S(2)}) collective-permute-start(bf16[256,1536]{1,0:T(8,128)(2,1)} %get-tuple-element.40), channel_id=1, source_target_pairs={{0,4},{1,5},{2,6},{3,7},{4,0},{5,1},{6,2},{7,3},{8,12},{9,13},{10,... | collective-permute-start | bytes 2359304 | tf_op jit(solution)/shard_map/ppermute | solution.py:28
  133.1 34.2 %collective-permute-start.18 = (bf16[256,1536]{1,0:T(8,128)(2,1)}, bf16[256,1536]{1,0:T(8,128)(2,1)}, u32[]{:S(2)}, u32[]{:S(2)}) collective-permute-start(bf16[256,1536]{1,0:T(8,128)(2,1)} %get-tuple-element.41), channel_id=1, source_target_pairs={{0,6},{1,7},{2,0},{3,1},{4,2},{5,3},{6,4},{7,5},{8,14},{9,15},{10,... | collective-permute-start | bytes 2359304 | tf_op jit(solution)/shard_map/ppermute | solution.py:28
  137.4 41.4 %collective-permute-start.20 = (bf16[512,512]{1,0:T(8,128)(2,1)}, bf16[512,512]{1,0:T(8,128)(2,1)S(1)}, u32[]{:S(2)}, u32[]{:S(2)}) collective-permute-start(bf16[512,512]{1,0:T(8,128)(2,1)} %shard_map.90), channel_id=1, source_target_pairs={{0,1},{1,0},{2,3},{3,2},{4,5},{5,4},{6,7},{7,6},{8,9},{9,8},{10,11... | collective-permute-start | bytes 1572872 | tf_op jit(solution)/shard_map/ppermute | solution.py:32
  148.5 18.9 %copy-start.10 = (bf16[256,1536]{1,0:T(8,128)(2,1)}, bf16[256,1536]{1,0:T(8,128)(2,1)S(1)}, u32[]{:S(2)}) copy-start(bf16[256,1536]{1,0:T(8,128)(2,1)S(1)} %collective-permute-done.16.rest_0_) | copy-start | bytes 2359300
  167.3 0.9 copy-start.11
  171.8 15.6 %collective-permute-start.19 = (bf16[512,512]{1,0:T(8,128)(2,1)}, bf16[512,512]{1,0:T(8,128)(2,1)S(1)}, u32[]{:S(2)}, u32[]{:S(2)}) collective-permute-start(bf16[512,512]{1,0:T(8,128)(2,1)} %shard_map.88), channel_id=1, source_target_pairs={{0,1},{1,0},{2,3},{3,2},{4,5},{5,4},{6,7},{7,6},{8,9},{9,8},{10,11... | collective-permute-start | bytes 1572872 | tf_op jit(solution)/shard_map/ppermute | solution.py:32
  185.0 2.5 %copy-start.8 = (f32[512,512]{1,0:T(8,128)S(1)}, f32[512,512]{1,0:T(8,128)}, u32[]{:S(2)}) copy-start(f32[512,512]{1,0:T(8,128)} %shard_map.91) | copy-start | bytes 3145732

commit v4 on v3

--- a/solution.py
+++ b/solution.py
@@ -206,12 +206,13 @@
             loads.start(other, rights.at[0]),
         )
     )
-    for k, piece in enumerate(pieces):
-        right = piece.at[:, pl.ds(piece.shape[1] - width, width)]
+    count = len(pieces) // 2
+    for k, (left, right) in enumerate(zip(pieces[:count], pieces[count:])):
+        right = right.at[:, pl.ds(right.shape[1] - width, width)]
         numbers.append(
             (
                 loads.start(
-                    piece.at[:, columns_of(starts, 1, rows)], lefts.at[k + 1]
+                    left.at[:, columns_of(starts, 1, rows)], lefts.at[k + 1]
                 ),
                 loads.start(right, rights.at[k + 1]),
             )
@@ -315,7 +316,11 @@
         partial,
         *weights,
     )
-    arrived = over_section(layer_out, 1)
+    steps = range(1, X_SIZE)
+    opposite = X_SIZE // 2
+    near_inputs = {by: over_x(cut(inputs, by), by) for by in steps if by != opposite}
+    ready, near_inputs = lax.optimization_barrier((layer_out, near_inputs))
+    arrived = over_section(ready, 1)
     out_pieces = [
         over_x(jnp.concatenate([cut(upstream, by), hidden], axis=1), by)
         for by in range(1, X_SIZE)
@@ -346,13 +351,15 @@
     )
     shadow = over_section(shadow_back, -1)
 
-    in_pieces = [
-        jnp.concatenate([cut(inputs, by), dpre], axis=1) for by in range(1, X_SIZE)
+    far_send = jnp.concatenate([cut(inputs, opposite), dpre], axis=1)
+    dpre_send, far_send, out_pieces, shadow_back = lax.optimization_barrier(
+        (dpre, far_send, out_pieces, shadow_back)
+    )
+    rights = [over_x(far_send if by == opposite else dpre_send, by) for by in steps]
+    lefts = [
+        rights[opposite - 1] if by == opposite else near_inputs[by] for by in steps
     ]
-    in_pieces, out_pieces, shadow_back = lax.optimization_barrier(
-        (in_pieces, out_pieces, shadow_back)
-    )
-    in_pieces = [over_x(piece, by + 1) for by, piece in enumerate(in_pieces)]
+    in_pieces = [*lefts, *rights]
     ours = jnp.stack([x * wide + y * rows, y * rows]).astype(jnp.int32)
     apart = (1 - y) * rows
     other = jnp.stack([x * wide + apart, apart]).astype(jnp.int32)
@@ -372,11 +379,8 @@
             *arrays,
         )
 
-    received_out = swap_y(part(other, BF16, upstream, hidden, *out_pieces))
-    mine_out = part(ours, F32, upstream, hidden, *out_pieces)
-    received_in = swap_y(part(other, BF16, inputs, dpre, *in_pieces))
-    mine_in = part(ours, F32, inputs, dpre, *in_pieces)
-    grad_out = mine_out + received_out.astype(F32)
+    received_out = swap_y(part(other, BF16, upstream, hidden, *out_pieces, *out_pieces))
+    mine_out = part(ours, F32, upstream, hidden, *out_pieces, *out_pieces)
     shadow = local_call(
         copy_kernel,
         activations,
@@ -386,9 +390,11 @@
         16,
         shadow,
     )
-    shadow, received_in, grad_out = lax.optimization_barrier(
-        (shadow, received_in, grad_out)
-    )
+    in_pieces, mine_out = lax.optimization_barrier((in_pieces, mine_out))
+    received_in = swap_y(part(other, BF16, inputs, dpre, *in_pieces))
+    mine_in = part(ours, F32, inputs, dpre, *in_pieces)
+    grad_out = mine_out + received_out.astype(F32)
+    shadow, received_in = lax.optimization_barrier((shadow, received_in))
     grad_in = mine_in + received_in.astype(F32)
     return (
         layer_out[None],

time: 189 us -> 193 us (1.021); the launches traced: 189 us -> 189 us
  waiting for transfers between devices: 91.9 us -> 74 us
  starting transfers between devices: 37.5 us -> 50.1 us
  local copies, waits for them, and re-layouts: 5.03 us -> 11.9 us
    ppermute x14 -> x16, waiting for transfers between devices: 63.1 us -> 40.4 us  [over_x(): return lax.ppermute(array, 'dp', pairs)]
    ppermute x3, starting transfers between devices: 9.44 us -> 27.8 us  [swap_y(): lax.ppermute(array, 'dp', [(i, i ^ 1) for i in range(X_SIZE * Y_SIZE)])]
    ppermute x4, starting transfers between devices: 8.27 us -> 3.34 us  [over_section(): lax.ppermute(array, 'section', [(i, (i + by) % devices) for i in range(de...]
    ppermute x4, waiting for transfers between devices: 9.6 us -> 14.5 us  [over_section(): lax.ppermute(array, 'section', [(i, (i + by) % devices) for i in range(de...]
    add x1 -> x0, other arithmetic: 2.36 us -> none  [on_device(): grad_out = mine_out + received_out.astype(F32)]
    unnamed x30, local copies, waits for them, and re-layouts: 0.93 us -> 3.08 us
    ppermute x14 -> x16, starting transfers between devices: 19.8 us -> 18.9 us  [over_x(): return lax.ppermute(array, 'dp', pairs)]
  transfers between devices with their start and end apart: 21 -> 23, of which waited for: 10 -> 10; matrix products, arithmetic and copies ran while one was open for 5% -> 7% of each run, Pallas kernels for 24% -> 24%
where the time goes in v4:
time: 193 us; the launch traced here: 189 us
  waiting for transfers between devices  74 us (38%)
  starting transfers between devices  50.1 us (26%)
  Pallas kernels  45.5 us (24%)
  local copies, waits for them, and re-layouts  11.9 us (6%)
  other arithmetic  7.01 us (4%)
    pallas_call x9, Pallas kernels, local_call(): pl.pallas_call(kernel, out_shape=outs, in_specs=in_specs, out_specs=out_s...  45.5 us
    ppermute x16, waiting for transfers between devices, over_x(): return lax.ppermute(array, 'dp', pairs)  40.4 us
    ppermute x3, starting transfers between devices, swap_y(): lax.ppermute(array, 'dp', [(i, i ^ 1) for i in range(X_SIZE * Y_SIZE)])  27.8 us
    ppermute x3, waiting for transfers between devices, swap_y(): lax.ppermute(array, 'dp', [(i, i ^ 1) for i in range(X_SIZE * Y_SIZE)])  19.2 us
    ppermute x16, starting transfers between devices, over_x(): return lax.ppermute(array, 'dp', pairs)  18.9 us
    ppermute x4, waiting for transfers between devices, over_section(): lax.ppermute(array, 'section', [(i, (i + by) % devices) for i in range(de...  14.5 us
  transfers between devices with their start and end apart: 23, of which 10 were waited for; matrix products, arithmetic and copies ran while one was open for 7% of the time, Pallas kernels for 24%

profile of v4, /device:TPU:1, one launch (start us, length us, event | category | flops | bytes accessed | tf_op | source)
XLA Modules:
  0.0 189.4 jit_solution(85694634938845582)
XLA Ops:
  0.6 1.3 pad_maximum_fusion.3.rest_0_
  1.9 3.8 %collective-permute-start = (bf16[1024,512]{1,0:T(8,128)(2,1)S(1)}, bf16[1024,512]{1,0:T(8,128)(2,1)}, u32[]{:S(2)}, u32[]{:S(2)}) collective-permute-start(bf16[1024,512]{1,0:T(8,128)(2,1)S(1)} %pad_maximum_fusion.3.rest_0_), channel_id=1, source_target_pairs={{0,1},{1,0},{2,3},{3,2},{4,5},{5,4},{6,7},{7,6},{8,9},{9,8},{10,11... | collective-permute-start | bytes 3145736 | tf_op jit(solution)/shard_map/ppermute | solution.py:32
  5.7 1.2 collective-permute-start.1
  7.0 1.5 collective-permute-start.2
  8.4 19.1 %collective-permute-done.rest_1_ = bf16[1024,512]{1,0:T(8,128)(2,1)} collective-permute-done((bf16[1024,512]{1,0:T(8,128)(2,1)S(1)}, bf16[1024,512]{1,0:T(8,128)(2,1)}, u32[]{:S(2)}, u32[]{:S(2)}) %collective-permute-start) | collective-permute-done | bytes 1048608 | tf_op jit(solution)/shard_map/ppermute | solution.py:32
  27.6 3.1 %collective-permute-done.1.rest_2_ = bf16[1024,512]{1,0:T(8,128)(2,1)S(1)} collective-permute-done((bf16[1024,512]{1,0:T(8,128)(2,1)S(1)}, bf16[1024,512]{1,0:T(8,128)(2,1)S(1)}, u32[]{:S(2)}, u32[]{:S(2)}) %collective-permute-start.1) | collective-permute-done | bytes 1048608 | tf_op jit(solution)/shard_map/ppermute | solution.py:28
  30.7 2.2 %collective-permute-start.3 = (bf16[256,4096]{1,0:T(8,128)(2,1)}, bf16[256,4096]{1,0:T(8,128)(2,1)S(1)}, u32[]{:S(2)}, u32[]{:S(2)}) collective-permute-start(bf16[256,4096]{1,0:T(8,128)(2,1)} %bitcast.10), channel_id=1, source_target_pairs={{0,8},{8,16},{16,24},{24,32},{32,40},{40,48},{48,56},{56,64},{64,7... | collective-permute-start | bytes 6291464 | tf_op jit(solution)/shard_map/ppermute | solution.py:18
  32.9 1.1 collective-permute-start.4
  34.0 1.6 collective-permute-start.5
  35.6 0.8 slice.12
  36.4 0.8 slice.13
  37.3 2.7 %collective-permute-start.7 = (bf16[512,512]{1,0:T(8,128)(2,1)}, bf16[512,512]{1,0:T(8,128)(2,1)}, u32[]{:S(2)}, u32[]{:S(2)}) collective-permute-start(bf16[512,512]{1,0:T(8,128)(2,1)} %slice.13), channel_id=1, source_target_pairs={{0,6},{1,7},{2,0},{3,1},{4,2},{5,3},{6,4},{7,5},{8,14},{9,15},{10,... | collective-permute-start | bytes 1572872 | tf_op jit(solution)/shard_map/ppermute | solution.py:28
  39.9 19.4 %collective-permute-done.4.rest_4_ = bf16[1024,512]{1,0:T(8,128)(2,1)} collective-permute-done((bf16[1024,512]{1,0:T(8,128)(2,1)}, bf16[1024,512]{1,0:T(8,128)(2,1)}, u32[]{:S(2)}, u32[]{:S(2)}) %collective-permute-start.4) | collective-permute-done | bytes 1048608 | tf_op jit(solution)/shard_map/ppermute | solution.py:28
  59.3 1.9 slice.16
  61.2 1.9 slice.17
  63.1 2.7 %collective-permute-start.9 = (bf16[512,512]{1,0:T(8,128)(2,1)}, bf16[512,512]{1,0:T(8,128)(2,1)}, u32[]{:S(2)}, u32[]{:S(2)}) collective-permute-start(bf16[512,512]{1,0:T(8,128)(2,1)} %slice.17), channel_id=1, source_target_pairs={{0,6},{1,7},{2,0},{3,1},{4,2},{5,3},{6,4},{7,5},{8,14},{9,15},{10,... | collective-permute-start | bytes 1572872 | tf_op jit(solution)/shard_map/ppermute | solution.py:28
  65.8 1.3 constant_dynamic-slice_fusion.3
  67.1 3.5 %collective-permute-done.6.rest_6_ = bf16[512,512]{1,0:T(8,128)(2,1)} collective-permute-done((bf16[512,512]{1,0:T(8,128)(2,1)}, bf16[512,512]{1,0:T(8,128)(2,1)}, u32[]{:S(2)}, u32[]{:S(2)}) %collective-permute-start.6) | collective-permute-done | bytes 524320 | tf_op jit(solution)/shard_map/ppermute | solution.py:28
  70.6 1.5 collective-permute-start.11
  72.0 1.0 collective-permute-start.13
  73.7 4.5 %shard_map.83.partial = f32[256,512]{1,0:T(8,128)} custom-call(s32[8]{0:T(128)} %stack.53.starts, bf16[256,4096]{1,0:T(8,128)(2,1)} %copy-done, bf16[1024,512]{1,0:T(8,128)(2,1)} %copy-done.1, bf16[1024,512]{1,0:T(8,128)(2,1)} %collective-permute-done.rest_1_, bf16[1024,512]{1,0:T(8,128)(2,1)} %copy-done.2, bf16[1024,512]{1,0:T(8,128)(2,1)} %copy-done.3, ...), custom_call_target="tpu_custom_call" | custom-call | flops 1 | bytes 1 | tf_op jit(solution)/shard_map/pallas_call | solution.py:246
  78.2 3.6 %collective-permute-done.8.rest_8_ = bf16[512,512]{1,0:T(8,128)(2,1)} collective-permute-done((bf16[512,512]{1,0:T(8,128)(2,1)}, bf16[512,512]{1,0:T(8,128)(2,1)}, u32[]{:S(2)}, u32[]{:S(2)}) %collective-permute-start.8) | collective-permute-done | bytes 524320 | tf_op jit(solution)/shard_map/ppermute | solution.py:28
  81.8 7.5 %shard_map.84 = (bf16[256,512]{1,0:T(8,128)(2,1)}, f32[256,512]{1,0:T(8,128)}, bf16[256,4096]{1,0:T(8,128)(2,1)}) custom-call(s32[8]{0:T(128)} %stack.53.starts, bf16[256,4096]{1,0:T(8,128)(2,1)} %copy-done, f32[256,512]{1,0:T(8,128)} %shard_map.83.partial, bf16[1024,512]{1,0:T(8,128)(2,1)} %copy-done.1, bf16[1024,512]{1,0:T(8,128)(2,1)} %collective-permute-done.rest_1_, ...), custom_call_target="tpu_custom_call" | custom-call | flops 1 | bytes 1 | tf_op jit(solution)/shard_map/pallas_call | solution.py:246
  89.3 3.7 %collective-permute-done.10.rest_0_ = bf16[256,1024]{1,0:T(8,128)(2,1)} collective-permute-done((bf16[256,1024]{1,0:T(8,128)(2,1)}, bf16[256,1024]{1,0:T(8,128)(2,1)}, u32[]{:S(2)}, u32[]{:S(2)}) %collective-permute-start.10) | collective-permute-done | bytes 524320 | tf_op jit(solution)/shard_map/ppermute | solution.py:28
  93.0 4.8 %collective-permute-done.13.upstream.whole = bf16[256,4096]{1,0:T(8,128)(2,1)} collective-permute-done((bf16[256,4096]{1,0:T(8,128)(2,1)}, bf16[256,4096]{1,0:T(8,128)(2,1)}, u32[]{:S(2)}, u32[]{:S(2)}) %collective-permute-start.13) | collective-permute-done | bytes 2097184 | tf_op jit(solution)/shard_map/ppermute | solution.py:18
  97.8 1.5 constant_dynamic-slice_fusion
  99.3 1.3 pad_maximum_fusion
  100.7 2.2 %collective-permute-start.16 = (bf16[256,1536]{1,0:T(8,128)(2,1)}, bf16[256,1536]{1,0:T(8,128)(2,1)S(1)}, u32[]{:S(2)}, u32[]{:S(2)}) collective-permute-start(bf16[256,1536]{1,0:T(8,128)(2,1)} %get-tuple-element.72), channel_id=1, source_target_pairs={{0,4},{1,5},{2,6},{3,7},{4,0},{5,1},{6,2},{7,3},{8,12},{9,13},{10,... | collective-permute-start | bytes 2359304 | tf_op jit(solution)/shard_map/ppermute | solution.py:28
  102.9 0.9 collective-permute-start.17
  103.7 8.5 %shard_map.85 = (bf16[256,512]{1,0:T(8,128)(2,1)}, bf16[256,4096]{1,0:T(8,128)(2,1)}) custom-call(s32[8]{0:T(128)} %stack.53.starts, bf16[256,4096]{1,0:T(8,128)(2,1)} %collective-permute-done.13.upstream.whole, f32[256,512]{1,0:T(8,128)} %get-tuple-element.43.slope, bf16[1024,512]{1,0:T(8,128)(2,1)} %copy-done.1, ...), custom_call_target="tpu_custom_call" | custom-call | flops 1 | bytes 1 | tf_op jit(solution)/shard_map/pallas_call | solution.py:246
  112.3 9.7 %collective-permute-done.12.inputs = bf16[256,4096]{1,0:T(8,128)(2,1)S(1)} collective-permute-done((bf16[256,4096]{1,0:T(8,128)(2,1)}, bf16[256,4096]{1,0:T(8,128)(2,1)S(1)}, u32[]{:S(2)}, u32[]{:S(2)}) %collective-permute-start.12) | collective-permute-done | bytes 2097184 | tf_op jit(solution)/shard_map/ppermute | solution.py:18
  122.0 1.4 copy-done.12
  123.3 7.6 %shard_map.86 = bf16[256,4096]{1,0:T(8,128)(2,1)} custom-call(s32[8]{0:T(128)} %stack.53.starts, bf16[256,4096]{1,0:T(8,128)(2,1)} %copy-done.12, bf16[1024,512]{1,0:T(8,128)(2,1)} %copy-done.1, bf16[1024,512]{1,0:T(8,128)(2,1)} %collective-permute-done.rest_1_, bf16[1024,512]{1,0:T(8,128)(2,1)} %copy-done.2, bf16[1024,512]{1,0:T(8,128)(2,1)} %copy-done.3, ...), custom_call_target="tpu_custom_call" | custom-call | flops 1 | bytes 1 | tf_op jit(solution)/shard_map/pallas_call | solution.py:246
  131.1 0.9 pad_maximum_fusion.4
  132.0 6.0 %collective-permute-done.15.rest_0_.rest_3_ = bf16[256,1536]{1,0:T(8,128)(2,1)S(1)} collective-permute-done((bf16[256,1536]{1,0:T(8,128)(2,1)}, bf16[256,1536]{1,0:T(8,128)(2,1)S(1)}, u32[]{:S(2)}, u32[]{:S(2)}) %collective-permute-start.15) | collective-permute-done | bytes 786464 | tf_op jit(solution)/shard_map/ppermute | solution.py:28
  138.1 1.0 collective-permute-done.17.rest_2_.rest_5_
  139.1 1.0 collective-permute-start.18
  140.7 3.6 %shard_map.91 = bf16[512,512]{1,0:T(8,128)(2,1)} custom-call(s32[2]{0:T(128)} %pad_add_fusion.starts, bf16[256,4096]{1,0:T(8,128)(2,1)} %collective-permute-done.13.upstream.whole, bf16[256,512]{1,0:T(8,128)(2,1)} %get-tuple-element.48.other, bf16[256,1536]{1,0:T(8,128)(2,1)} %copy-done.4, bf16[256,1536]{1,0:T(8,128)(2,1)} %copy-done.5, ...), custom_call_target="tpu_custom_call" | custom-call | flops 1 | bytes 1 | tf_op jit(solution)/shard_map/pallas_call | solution.py:246
  144.3 20.3 %collective-permute-start.22 = (bf16[512,512]{1,0:T(8,128)(2,1)}, bf16[512,512]{1,0:T(8,128)(2,1)S(1)}, u32[]{:S(2)}, u32[]{:S(2)}) collective-permute-start(bf16[512,512]{1,0:T(8,128)(2,1)} %shard_map.91), channel_id=1, source_target_pairs={{0,1},{1,0},{2,3},{3,2},{4,5},{5,4},{6,7},{7,6},{8,9},{9,8},{10,11... | collective-permute-start | bytes 1572872 | tf_op jit(solution)/shard_map/ppermute | solution.py:32
  164.7 2.7 %collective-permute-start.20 = (bf16[256,512]{1,0:T(8,128)(2,1)S(1)}, bf16[256,512]{1,0:T(8,128)(2,1)S(1)}, u32[]{:S(2)}, u32[]{:S(2)}) collective-permute-start(bf16[256,512]{1,0:T(8,128)(2,1)S(1)} %copy-done.11), channel_id=1, source_target_pairs={{0,6},{1,7},{2,0},{3,1},{4,2},{5,3},{6,4},{7,5},{8,14},{9,15},{10,... | collective-permute-start | bytes 786440 | tf_op jit(solution)/shard_map/ppermute | solution.py:28
  167.9 3.8 %shard_map.88 = f32[512,512]{1,0:T(8,128)} custom-call(s32[2]{0:T(128)} %pad_add_fusion.1.starts, bf16[256,4096]{1,0:T(8,128)(2,1)} %collective-permute-done.13.upstream.whole, bf16[256,512]{1,0:T(8,128)(2,1)} %get-tuple-element.48.other, bf16[256,1536]{1,0:T(8,128)(2,1)} %copy-done.4, bf16[256,1536]{1,0:T(8,128)(2,1)} %copy-done.5, ...), custom_call_target="tpu_custom_call" | custom-call | flops 1 | bytes 1 | tf_op jit(solution)/shard_map/pallas_call | solution.py:246
  172.6 0.9 copy-done.7
  173.5 3.6 %shard_map.89 = bf16[512,512]{1,0:T(8,128)(2,1)} custom-call(s32[2]{0:T(128)} %pad_add_fusion.starts, bf16[256,4096]{1,0:T(8,128)(2,1)} %copy-done, bf16[256,512]{1,0:T(8,128)(2,1)} %get-tuple-element.51.other, bf16[256,1024]{1,0:T(8,128)(2,1)} %collective-permute-done.10.rest_0_, bf16[256,1536]{1,0:T(8,128)(2,1)} %copy-done.7, ...), custom_call_target="tpu_custom_call" | custom-call | flops 1 | bytes 1 | tf_op jit(solution)/shard_map/pallas_call | solution.py:246
  177.1 3.6 %collective-permute-start.21 = (bf16[512,512]{1,0:T(8,128)(2,1)}, bf16[512,512]{1,0:T(8,128)(2,1)S(1)}, u32[]{:S(2)}, u32[]{:S(2)}) collective-permute-start(bf16[512,512]{1,0:T(8,128)(2,1)} %shard_map.89), channel_id=1, source_target_pairs={{0,1},{1,0},{2,3},{3,2},{4,5},{5,4},{6,7},{7,6},{8,9},{9,8},{10,11... | collective-permute-start | bytes 1572872 | tf_op jit(solution)/shard_map/ppermute | solution.py:32
  180.8 3.8 %shard_map.90 = f32[512,512]{1,0:T(8,128)} custom-call(s32[2]{0:T(128)} %pad_add_fusion.1.starts, bf16[256,4096]{1,0:T(8,128)(2,1)} %copy-done, bf16[256,512]{1,0:T(8,128)(2,1)} %get-tuple-element.51.other, bf16[256,1024]{1,0:T(8,128)(2,1)} %collective-permute-done.10.rest_0_, bf16[256,1536]{1,0:T(8,128)(2,1)} %copy-done.7, ...), custom_call_target="tpu_custom_call" | custom-call | flops 1 | bytes 1 | tf_op jit(solution)/shard_map/pallas_call | solution.py:246
  184.6 1.1 add_bitcast_fusion
  185.7 2.5 %shard_map.87 = bf16[256,4096]{1,0:T(8,128)(2,1)} custom-call(bf16[256,4096]{1,0:T(8,128)(2,1)} %collective-permute-done.14.source), custom_call_target="tpu_custom_call" | custom-call | flops 1 | bytes 1 | tf_op jit(solution)/shard_map/pallas_call | solution.py:246
  188.2 1.1 add_bitcast_fusion.1
  (51 shorter events, 2.8 us)
Async XLA Ops:
  1.9 61.2 %copy-start.1 = (bf16[1024,512]{1,0:T(8,128)(2,1)}, bf16[1024,512]{1,0:T(8,128)(2,1)S(1)}, u32[]{:S(2)}) copy-start(bf16[1024,512]{1,0:T(8,128)(2,1)S(1)} %pad_maximum_fusion.3.rest_0_) | copy-start | bytes 3145732
  1.9 25.7 %collective-permute-start = (bf16[1024,512]{1,0:T(8,128)(2,1)S(1)}, bf16[1024,512]{1,0:T(8,128)(2,1)}, u32[]{:S(2)}, u32[]{:S(2)}) collective-permute-start(bf16[1024,512]{1,0:T(8,128)(2,1)S(1)} %pad_maximum_fusion.3.rest_0_), channel_id=1, source_target_pairs={{0,1},{1,0},{2,3},{3,2},{4,5},{5,4},{6,7},{7,6},{8,9},{9,8},{10,11... | collective-permute-start | bytes 3145736 | tf_op jit(solution)/shard_map/ppermute | solution.py:32
  5.7 24.9 %collective-permute-start.1 = (bf16[1024,512]{1,0:T(8,128)(2,1)S(1)}, bf16[1024,512]{1,0:T(8,128)(2,1)S(1)}, u32[]{:S(2)}, u32[]{:S(2)}) collective-permute-start(bf16[1024,512]{1,0:T(8,128)(2,1)S(1)} %pad_maximum_fusion.3.rest_0_), channel_id=1, source_target_pairs={{0,2},{1,3},{2,4},{3,5},{4,6},{5,7},{6,0},{7,1},{8,10},{9,11},{10,... | collective-permute-start | bytes 3145736 | tf_op jit(solution)/shard_map/ppermute | solution.py:28
  7.0 23.7 %collective-permute-start.2 = (bf16[1024,512]{1,0:T(8,128)(2,1)S(1)}, bf16[1024,512]{1,0:T(8,128)(2,1)S(1)}, u32[]{:S(2)}, u32[]{:S(2)}) collective-permute-start(bf16[1024,512]{1,0:T(8,128)(2,1)S(1)} %pad_maximum_fusion.3.rest_0_), channel_id=1, source_target_pairs={{0,6},{1,7},{2,0},{3,1},{4,2},{5,3},{6,4},{7,5},{8,14},{9,15},{10,... | collective-permute-start | bytes 3145736 | tf_op jit(solution)/shard_map/ppermute | solution.py:28
  30.7 4.9 %copy-start.2 = (bf16[1024,512]{1,0:T(8,128)(2,1)}, bf16[1024,512]{1,0:T(8,128)(2,1)S(1)}, u32[]{:S(2)}) copy-start(bf16[1024,512]{1,0:T(8,128)(2,1)S(1)} %collective-permute-done.1.rest_2_) | copy-start | bytes 3145732
  30.7 5.8 %copy-start.3 = (bf16[1024,512]{1,0:T(8,128)(2,1)}, bf16[1024,512]{1,0:T(8,128)(2,1)S(1)}, u32[]{:S(2)}) copy-start(bf16[1024,512]{1,0:T(8,128)(2,1)S(1)} %collective-permute-done.2.rest_3_) | copy-start | bytes 3145732
  30.7 35.1 %collective-permute-start.3 = (bf16[256,4096]{1,0:T(8,128)(2,1)}, bf16[256,4096]{1,0:T(8,128)(2,1)S(1)}, u32[]{:S(2)}, u32[]{:S(2)}) collective-permute-start(bf16[256,4096]{1,0:T(8,128)(2,1)} %bitcast.10), channel_id=1, source_target_pairs={{0,8},{8,16},{16,24},{24,32},{32,40},{40,48},{48,56},{56,64},{64,7... | collective-permute-start | bytes 6291464 | tf_op jit(solution)/shard_map/ppermute | solution.py:18
  32.9 26.4 %collective-permute-start.4 = (bf16[1024,512]{1,0:T(8,128)(2,1)}, bf16[1024,512]{1,0:T(8,128)(2,1)}, u32[]{:S(2)}, u32[]{:S(2)}) collective-permute-start(bf16[1024,512]{1,0:T(8,128)(2,1)} %collective-permute-done.rest_1_), channel_id=1, source_target_pairs={{0,2},{1,3},{2,4},{3,5},{4,6},{5,7},{6,0},{7,1},{8,10},{9,11},{10,... | collective-permute-start | bytes 3145736 | tf_op jit(solution)/shard_map/ppermute | solution.py:28
  34.0 27.2 %collective-permute-start.5 = (bf16[1024,512]{1,0:T(8,128)(2,1)}, bf16[1024,512]{1,0:T(8,128)(2,1)}, u32[]{:S(2)}, u32[]{:S(2)}) collective-permute-start(bf16[1024,512]{1,0:T(8,128)(2,1)} %collective-permute-done.rest_1_), channel_id=1, source_target_pairs={{0,6},{1,7},{2,0},{3,1},{4,2},{5,3},{6,4},{7,5},{8,14},{9,15},{10,... | collective-permute-start | bytes 3145736 | tf_op jit(solution)/shard_map/ppermute | solution.py:28
  36.4 34.1 %collective-permute-start.6 = (bf16[512,512]{1,0:T(8,128)(2,1)}, bf16[512,512]{1,0:T(8,128)(2,1)}, u32[]{:S(2)}, u32[]{:S(2)}) collective-permute-start(bf16[512,512]{1,0:T(8,128)(2,1)} %slice.12), channel_id=1, source_target_pairs={{0,2},{1,3},{2,4},{3,5},{4,6},{5,7},{6,0},{7,1},{8,10},{9,11},{10,... | collective-permute-start | bytes 1572872 | tf_op jit(solution)/shard_map/ppermute | solution.py:28
  37.3 34.8 %collective-permute-start.7 = (bf16[512,512]{1,0:T(8,128)(2,1)}, bf16[512,512]{1,0:T(8,128)(2,1)}, u32[]{:S(2)}, u32[]{:S(2)}) collective-permute-start(bf16[512,512]{1,0:T(8,128)(2,1)} %slice.13), channel_id=1, source_target_pairs={{0,6},{1,7},{2,0},{3,1},{4,2},{5,3},{6,4},{7,5},{8,14},{9,15},{10,... | collective-permute-start | bytes 1572872 | tf_op jit(solution)/shard_map/ppermute | solution.py:28
  61.2 20.6 %collective-permute-start.8 = (bf16[512,512]{1,0:T(8,128)(2,1)}, bf16[512,512]{1,0:T(8,128)(2,1)}, u32[]{:S(2)}, u32[]{:S(2)}) collective-permute-start(bf16[512,512]{1,0:T(8,128)(2,1)} %slice.16), channel_id=1, source_target_pairs={{0,2},{1,3},{2,4},{3,5},{4,6},{5,7},{6,0},{7,1},{8,10},{9,11},{10,... | collective-permute-start | bytes 1572872 | tf_op jit(solution)/shard_map/ppermute | solution.py:28
  63.1 18.7 %collective-permute-start.9 = (bf16[512,512]{1,0:T(8,128)(2,1)}, bf16[512,512]{1,0:T(8,128)(2,1)}, u32[]{:S(2)}, u32[]{:S(2)}) collective-permute-start(bf16[512,512]{1,0:T(8,128)(2,1)} %slice.17), channel_id=1, source_target_pairs={{0,6},{1,7},{2,0},{3,1},{4,2},{5,3},{6,4},{7,5},{8,14},{9,15},{10,... | collective-permute-start | bytes 1572872 | tf_op jit(solution)/shard_map/ppermute | solution.py:28
  65.8 7.9 %copy-start = (bf16[256,4096]{1,0:T(8,128)(2,1)}, bf16[256,4096]{1,0:T(8,128)(2,1)S(1)}, u32[]{:S(2)}) copy-start(bf16[256,4096]{1,0:T(8,128)(2,1)S(1)} %collective-permute-done.3.inputs.whole) | copy-start | bytes 6291460
  67.1 25.9 %collective-permute-start.10 = (bf16[256,1024]{1,0:T(8,128)(2,1)}, bf16[256,1024]{1,0:T(8,128)(2,1)}, u32[]{:S(2)}, u32[]{:S(2)}) collective-permute-start(bf16[256,1024]{1,0:T(8,128)(2,1)} %get-tuple-element.70), channel_id=1, source_target_pairs={{0,2},{1,3},{2,4},{3,5},{4,6},{5,7},{6,0},{7,1},{8,10},{9,11},{10,... | collective-permute-start | bytes 1572872 | tf_op jit(solution)/shard_map/ppermute | solution.py:28
  70.6 22.5 %collective-permute-start.11 = (bf16[256,1024]{1,0:T(8,128)(2,1)}, bf16[256,1024]{1,0:T(8,128)(2,1)}, u32[]{:S(2)}, u32[]{:S(2)}) collective-permute-start(bf16[256,1024]{1,0:T(8,128)(2,1)} %get-tuple-element.69), channel_id=1, source_target_pairs={{0,6},{1,7},{2,0},{3,1},{4,2},{5,3},{6,4},{7,5},{8,14},{9,15},{10,... | collective-permute-start | bytes 1572872 | tf_op jit(solution)/shard_map/ppermute | solution.py:28
  72.0 25.8 %collective-permute-start.13 = (bf16[256,4096]{1,0:T(8,128)(2,1)}, bf16[256,4096]{1,0:T(8,128)(2,1)}, u32[]{:S(2)}, u32[]{:S(2)}) collective-permute-start(bf16[256,4096]{1,0:T(8,128)(2,1)} %bitcast.12), channel_id=1, source_target_pairs={{0,248},{8,0},{16,8},{24,16},{32,24},{40,32},{48,40},{56,48},{64,5... | collective-permute-start | bytes 6291464 | tf_op jit(solution)/shard_map/ppermute | solution.py:18
  89.3 10.0 %copy-start.10 = (bf16[256,512]{1,0:T(8,128)(2,1)S(1)}, bf16[256,512]{1,0:T(8,128)(2,1)}, u32[]{:S(2)}) copy-start(bf16[256,512]{1,0:T(8,128)(2,1)} %get-tuple-element.48.other) | copy-start | bytes 786436
  93.0 28.9 %collective-permute-start.12 = (bf16[256,4096]{1,0:T(8,128)(2,1)}, bf16[256,4096]{1,0:T(8,128)(2,1)S(1)}, u32[]{:S(2)}, u32[]{:S(2)}) collective-permute-start(bf16[256,4096]{1,0:T(8,128)(2,1)} %get-tuple-element.41), channel_id=1, source_target_pairs={{0,8},{8,16},{16,24},{24,32},{32,40},{40,48},{48,56},{56,64},{64,7... | collective-permute-start | bytes 6291464 | tf_op jit(solution)/shard_map/ppermute | solution.py:18
  100.7 37.4 %collective-permute-start.15 = (bf16[256,1536]{1,0:T(8,128)(2,1)}, bf16[256,1536]{1,0:T(8,128)(2,1)S(1)}, u32[]{:S(2)}, u32[]{:S(2)}) collective-permute-start(bf16[256,1536]{1,0:T(8,128)(2,1)} %get-tuple-element.73), channel_id=1, source_target_pairs={{0,2},{1,3},{2,4},{3,5},{4,6},{5,7},{6,0},{7,1},{8,10},{9,11},{10,... | collective-permute-start | bytes 2359304 | tf_op jit(solution)/shard_map/ppermute | solution.py:28
  100.7 37.4 %collective-permute-start.16 = (bf16[256,1536]{1,0:T(8,128)(2,1)}, bf16[256,1536]{1,0:T(8,128)(2,1)S(1)}, u32[]{:S(2)}, u32[]{:S(2)}) collective-permute-start(bf16[256,1536]{1,0:T(8,128)(2,1)} %get-tuple-element.72), channel_id=1, source_target_pairs={{0,4},{1,5},{2,6},{3,7},{4,0},{5,1},{6,2},{7,3},{8,12},{9,13},{10,... | collective-permute-start | bytes 2359304 | tf_op jit(solution)/shard_map/ppermute | solution.py:28
  102.9 36.2 %collective-permute-start.17 = (bf16[256,1536]{1,0:T(8,128)(2,1)S(1)}, bf16[256,1536]{1,0:T(8,128)(2,1)S(1)}, u32[]{:S(2)}, u32[]{:S(2)}) collective-permute-start(bf16[256,1536]{1,0:T(8,128)(2,1)S(1)} %get-tuple-element.71), channel_id=1, source_target_pairs={{0,6},{1,7},{2,0},{3,1},{4,2},{5,3},{6,4},{7,5},{8,14},{9,15},{10,... | collective-permute-start | bytes 2359304 | tf_op jit(solution)/shard_map/ppermute | solution.py:28
  122.0 1.4 copy-start.12
  123.3 7.7 %copy-start.11 = (bf16[256,512]{1,0:T(8,128)(2,1)S(1)}, bf16[256,512]{1,0:T(8,128)(2,1)}, u32[]{:S(2)}) copy-start(bf16[256,512]{1,0:T(8,128)(2,1)} %get-tuple-element.51.other) | copy-start | bytes 786436
  131.0 54.7 %collective-permute-start.14 = (bf16[256,4096]{1,0:T(8,128)(2,1)}, bf16[256,4096]{1,0:T(8,128)(2,1)}, u32[]{:S(2)}, u32[]{:S(2)}) collective-permute-start(bf16[256,4096]{1,0:T(8,128)(2,1)} %shard_map.86), channel_id=1, source_target_pairs={{0,248},{8,0},{16,8},{24,16},{32,24},{40,32},{48,40},{56,48},{64,5... | collective-permute-start | bytes 6291464 | tf_op jit(solution)/shard_map/ppermute | solution.py:18
  138.1 2.6 %copy-start.4 = (bf16[256,1536]{1,0:T(8,128)(2,1)}, bf16[256,1536]{1,0:T(8,128)(2,1)S(1)}, u32[]{:S(2)}) copy-start(bf16[256,1536]{1,0:T(8,128)(2,1)S(1)} %collective-permute-done.15.rest_0_.rest_3_) | copy-start | bytes 2359300
  138.1 2.6 %copy-start.5 = (bf16[256,1536]{1,0:T(8,128)(2,1)}, bf16[256,1536]{1,0:T(8,128)(2,1)S(1)}, u32[]{:S(2)}) copy-start(bf16[256,1536]{1,0:T(8,128)(2,1)S(1)} %collective-permute-done.16.rest_1_.rest_4_) | copy-start | bytes 2359300
  139.1 1.6 copy-start.6
  139.1 32.7 %collective-permute-start.18 = (bf16[256,1536]{1,0:T(8,128)(2,1)}, bf16[256,1536]{1,0:T(8,128)(2,1)S(1)}, u32[]{:S(2)}, u32[]{:S(2)}) collective-permute-start(bf16[256,1536]{1,0:T(8,128)(2,1)} %pad_maximum_fusion.4), channel_id=1, source_target_pairs={{0,4},{1,5},{2,6},{3,7},{4,0},{5,1},{6,2},{7,3},{8,12},{9,13},{10,... | collective-permute-start | bytes 2359304 | tf_op jit(solution)/shard_map/ppermute | solution.py:28
  144.3 40.3 %collective-permute-start.22 = (bf16[512,512]{1,0:T(8,128)(2,1)}, bf16[512,512]{1,0:T(8,128)(2,1)S(1)}, u32[]{:S(2)}, u32[]{:S(2)}) collective-permute-start(bf16[512,512]{1,0:T(8,128)(2,1)} %shard_map.91), channel_id=1, source_target_pairs={{0,1},{1,0},{2,3},{3,2},{4,5},{5,4},{6,7},{7,6},{8,9},{9,8},{10,11... | collective-permute-start | bytes 1572872 | tf_op jit(solution)/shard_map/ppermute | solution.py:32
  164.7 7.1 %collective-permute-start.19 = (bf16[256,512]{1,0:T(8,128)(2,1)S(1)}, bf16[256,512]{1,0:T(8,128)(2,1)S(1)}, u32[]{:S(2)}, u32[]{:S(2)}) collective-permute-start(bf16[256,512]{1,0:T(8,128)(2,1)S(1)} %copy-done.11), channel_id=1, source_target_pairs={{0,2},{1,3},{2,4},{3,5},{4,6},{5,7},{6,0},{7,1},{8,10},{9,11},{10,... | collective-permute-start | bytes 786440 | tf_op jit(solution)/shard_map/ppermute | solution.py:28
  164.7 7.1 %collective-permute-start.20 = (bf16[256,512]{1,0:T(8,128)(2,1)S(1)}, bf16[256,512]{1,0:T(8,128)(2,1)S(1)}, u32[]{:S(2)}, u32[]{:S(2)}) collective-permute-start(bf16[256,512]{1,0:T(8,128)(2,1)S(1)} %copy-done.11), channel_id=1, source_target_pairs={{0,6},{1,7},{2,0},{3,1},{4,2},{5,3},{6,4},{7,5},{8,14},{9,15},{10,... | collective-permute-start | bytes 786440 | tf_op jit(solution)/shard_map/ppermute | solution.py:28
  171.8 0.7 copy-start.13
  171.8 0.8 copy-start.14
  172.6 0.9 copy-start.7
  177.1 7.5 %copy-start.9 = (f32[512,512]{1,0:T(8,128)S(1)}, f32[512,512]{1,0:T(8,128)}, u32[]{:S(2)}) copy-start(f32[512,512]{1,0:T(8,128)} %shard_map.88) | copy-start | bytes 3145732
  177.1 11.1 %collective-permute-start.21 = (bf16[512,512]{1,0:T(8,128)(2,1)}, bf16[512,512]{1,0:T(8,128)(2,1)S(1)}, u32[]{:S(2)}, u32[]{:S(2)}) collective-permute-start(bf16[512,512]{1,0:T(8,128)(2,1)} %shard_map.89), channel_id=1, source_target_pairs={{0,1},{1,0},{2,3},{3,2},{4,5},{5,4},{6,7},{7,6},{8,9},{9,8},{10,11... | collective-permute-start | bytes 1572872 | tf_op jit(solution)/shard_map/ppermute | solution.py:32
  185.7 2.5 %copy-start.8 = (f32[512,512]{1,0:T(8,128)S(1)}, f32[512,512]{1,0:T(8,128)}, u32[]{:S(2)}) copy-start(f32[512,512]{1,0:T(8,128)} %shard_map.90) | copy-start | bytes 3145732

commit v5 on v4

--- a/solution.py
+++ b/solution.py
@@ -275,7 +275,9 @@
     inputs = over_section(handoff[0], 1)
     far_partner_in = over_x(behind_partner[:rows], 1)
     far_partner_out = over_x(ahead_partner[rows:], -1)
-    grad_back, inputs = lax.optimization_barrier((grad_back, inputs))
+    grad_back, inputs, _ = lax.optimization_barrier(
+        (grad_back, inputs, (far_in, far_out, behind_partner, ahead_partner))
+    )
     upstream = over_section(grad_back[0], -1)
     weights = (own, partner, behind, ahead, behind_partner, ahead_partner)
     weights += (far_in, far_out, far_partner_in, far_partner_out)
@@ -319,7 +321,9 @@
     steps = range(1, X_SIZE)
     opposite = X_SIZE // 2
     near_inputs = {by: over_x(cut(inputs, by), by) for by in steps if by != opposite}
-    ready, near_inputs = lax.optimization_barrier((layer_out, near_inputs))
+    ready, near_inputs, upstream = lax.optimization_barrier(
+        (layer_out, near_inputs, upstream)
+    )
     arrived = over_section(ready, 1)
     out_pieces = [
         over_x(jnp.concatenate([cut(upstream, by), hidden], axis=1), by)

time: 193 us -> 194 us (level); the launches traced: 189 us -> 193 us
  waiting for transfers between devices: 74 us -> 91.4 us
  starting transfers between devices: 50.1 us -> 37.7 us
    ppermute x3, starting transfers between devices: 27.8 us -> 5.23 us  [swap_y(): lax.ppermute(array, 'dp', [(i, i ^ 1) for i in range(X_SIZE * Y_SIZE)])]
    ppermute x16, waiting for transfers between devices: 40.4 us -> 58.3 us  [over_x(): return lax.ppermute(array, 'dp', pairs)]
    ppermute x4, waiting for transfers between devices: 14.5 us -> 7.12 us  [over_section(): lax.ppermute(array, 'section', [(i, (i + by) % devices) for i in range(de...]
    ppermute x3, waiting for transfers between devices: 19.2 us -> 26 us  [swap_y(): lax.ppermute(array, 'dp', [(i, i ^ 1) for i in range(X_SIZE * Y_SIZE)])]
    ppermute x4, starting transfers between devices: 3.34 us -> 9.38 us  [over_section(): lax.ppermute(array, 'section', [(i, (i + by) % devices) for i in range(de...]
    ppermute x16, starting transfers between devices: 18.9 us -> 23.1 us  [over_x(): return lax.ppermute(array, 'dp', pairs)]
    unnamed x30 -> x48, local copies, waits for them, and re-layouts: 3.08 us -> 3.9 us
  transfers between devices with their start and end apart: 23 -> 23, of which waited for: 10 -> 11; matrix products, arithmetic and copies ran while one was open for 7% -> 6% of each run, Pallas kernels for 24% -> 24%
where the time goes in v5:
time: 194 us; the launch traced here: 193 us
  waiting for transfers between devices  91.4 us (47%)
  Pallas kernels  45.5 us (23%)
  starting transfers between devices  37.7 us (19%)
  local copies, waits for them, and re-layouts  11.1 us (6%)
  other arithmetic  6.84 us (4%)
    ppermute x16, waiting for transfers between devices, over_x(): return lax.ppermute(array, 'dp', pairs)  58.3 us
    pallas_call x9, Pallas kernels, local_call(): pl.pallas_call(kernel, out_shape=outs, in_specs=in_specs, out_specs=out_s...  45.5 us
    ppermute x3, waiting for transfers between devices, swap_y(): lax.ppermute(array, 'dp', [(i, i ^ 1) for i in range(X_SIZE * Y_SIZE)])  26 us
    ppermute x16, starting transfers between devices, over_x(): return lax.ppermute(array, 'dp', pairs)  23.1 us
    ppermute x4, starting transfers between devices, over_section(): lax.ppermute(array, 'section', [(i, (i + by) % devices) for i in range(de...  9.38 us
    ppermute x4, waiting for transfers between devices, over_section(): lax.ppermute(array, 'section', [(i, (i + by) % devices) for i in range(de...  7.12 us
    ppermute x3, starting transfers between devices, swap_y(): lax.ppermute(array, 'dp', [(i, i ^ 1) for i in range(X_SIZE * Y_SIZE)])  5.23 us
    unnamed x48, local copies, waits for them, and re-layouts  3.9 us
  transfers between devices with their start and end apart: 23, of which 11 were waited for; matrix products, arithmetic and copies ran while one was open for 6% of the time, Pallas kernels for 24%

profile of v5, /device:TPU:1, one launch (start us, length us, event | category | flops | bytes accessed | tf_op | source)
XLA Modules:
  0.0 193.5 jit_solution(5044137127272540622)
XLA Ops:
  0.6 1.4 pad_maximum_fusion.3.rest_0_
  2.1 3.8 %collective-permute-start = (bf16[1024,512]{1,0:T(8,128)(2,1)S(1)}, bf16[1024,512]{1,0:T(8,128)(2,1)S(1)}, u32[]{:S(2)}, u32[]{:S(2)}) collective-permute-start(bf16[1024,512]{1,0:T(8,128)(2,1)S(1)} %pad_maximum_fusion.3.rest_0_), channel_id=1, source_target_pairs={{0,1},{1,0},{2,3},{3,2},{4,5},{5,4},{6,7},{7,6},{8,9},{9,8},{10,11... | collective-permute-start | bytes 3145736 | tf_op jit(solution)/shard_map/ppermute | solution.py:32
  5.9 1.2 collective-permute-start.1
  7.1 1.5 collective-permute-start.2
  8.6 19.1 %collective-permute-done.rest_1_ = bf16[1024,512]{1,0:T(8,128)(2,1)S(1)} collective-permute-done((bf16[1024,512]{1,0:T(8,128)(2,1)S(1)}, bf16[1024,512]{1,0:T(8,128)(2,1)S(1)}, u32[]{:S(2)}, u32[]{:S(2)}) %collective-permute-start) | collective-permute-done | bytes 1048608 | tf_op jit(solution)/shard_map/ppermute | solution.py:32
  27.7 3.1 %collective-permute-done.1.rest_2_ = bf16[1024,512]{1,0:T(8,128)(2,1)S(1)} collective-permute-done((bf16[1024,512]{1,0:T(8,128)(2,1)S(1)}, bf16[1024,512]{1,0:T(8,128)(2,1)S(1)}, u32[]{:S(2)}, u32[]{:S(2)}) %collective-permute-start.1) | collective-permute-done | bytes 1048608 | tf_op jit(solution)/shard_map/ppermute | solution.py:28
  30.8 2.2 %collective-permute-start.3 = (bf16[256,4096]{1,0:T(8,128)(2,1)S(1)}, bf16[256,4096]{1,0:T(8,128)(2,1)S(1)}, u32[]{:S(2)}, u32[]{:S(2)}) collective-permute-start(bf16[256,4096]{1,0:T(8,128)(2,1)S(1)} %bitcast.26), channel_id=1, source_target_pairs={{0,8},{8,16},{16,24},{24,32},{32,40},{40,48},{48,56},{56,64},{64,7... | collective-permute-start | bytes 6291464 | tf_op jit(solution)/shard_map/ppermute | solution.py:18
  33.1 1.1 collective-permute-start.6
  34.2 1.6 collective-permute-start.7
  35.9 2.7 %collective-permute-start.5 = (bf16[512,512]{1,0:T(8,128)(2,1)S(1)}, bf16[512,512]{1,0:T(8,128)(2,1)S(1)}, u32[]{:S(2)}, u32[]{:S(2)}) collective-permute-start(bf16[512,512]{1,0:T(8,128)(2,1)S(1)} %slice.13), channel_id=1, source_target_pairs={{0,6},{1,7},{2,0},{3,1},{4,2},{5,3},{6,4},{7,5},{8,14},{9,15},{10,... | collective-permute-start | bytes 1572872 | tf_op jit(solution)/shard_map/ppermute | solution.py:28
  38.7 31.8 %collective-permute-done.4.rest_6_ = bf16[512,512]{1,0:T(8,128)(2,1)S(1)} collective-permute-done((bf16[512,512]{1,0:T(8,128)(2,1)S(1)}, bf16[512,512]{1,0:T(8,128)(2,1)S(1)}, u32[]{:S(2)}, u32[]{:S(2)}) %collective-permute-start.4) | collective-permute-done | bytes 524320 | tf_op jit(solution)/shard_map/ppermute | solution.py:28
  72.1 2.0 %slice.16 = bf16[512,512]{1,0:T(8,128)(2,1)} slice(bf16[1024,512]{1,0:T(8,128)(2,1)} %copy-done.4), slice={[0:512], [0:512]} | slice | bytes 1048576 | tf_op jit(solution)/shard_map/slice | solution.py:276
  74.5 1.9 slice.17
  76.4 2.2 %collective-permute-start.9 = (bf16[512,512]{1,0:T(8,128)(2,1)}, bf16[512,512]{1,0:T(8,128)(2,1)}, u32[]{:S(2)}, u32[]{:S(2)}) collective-permute-start(bf16[512,512]{1,0:T(8,128)(2,1)} %slice.17), channel_id=1, source_target_pairs={{0,6},{1,7},{2,0},{3,1},{4,2},{5,3},{6,4},{7,5},{8,14},{9,15},{10,... | collective-permute-start | bytes 1572872 | tf_op jit(solution)/shard_map/ppermute | solution.py:28
  78.6 1.2 constant_dynamic-slice_fusion.3
  79.8 2.7 %collective-permute-start.11 = (bf16[256,1024]{1,0:T(8,128)(2,1)}, bf16[256,1024]{1,0:T(8,128)(2,1)S(1)}, u32[]{:S(2)}, u32[]{:S(2)}) collective-permute-start(bf16[256,1024]{1,0:T(8,128)(2,1)} %get-tuple-element.71), channel_id=1, source_target_pairs={{0,6},{1,7},{2,0},{3,1},{4,2},{5,3},{6,4},{7,5},{8,14},{9,15},{10,... | collective-permute-start | bytes 1572872 | tf_op jit(solution)/shard_map/ppermute | solution.py:28
  83.1 4.5 %shard_map.83.partial = f32[256,512]{1,0:T(8,128)} custom-call(s32[8]{0:T(128)} %stack.53.starts, bf16[256,4096]{1,0:T(8,128)(2,1)} %copy-done, bf16[1024,512]{1,0:T(8,128)(2,1)} %copy-done.1, bf16[1024,512]{1,0:T(8,128)(2,1)} %copy-done.6, bf16[1024,512]{1,0:T(8,128)(2,1)} %copy-done.2, bf16[1024,512]{1,0:T(8,128)(2,1)} %copy-done.3, ...), custom_call_target="tpu_custom_call" | custom-call | flops 1 | bytes 1 | tf_op jit(solution)/shard_map/pallas_call | solution.py:246
  87.6 0.8 collective-permute-done.8.rest_8_
  88.4 0.8 collective-permute-done.9.rest_9_
  89.2 7.5 %shard_map.84 = (bf16[256,512]{1,0:T(8,128)(2,1)}, f32[256,512]{1,0:T(8,128)}, bf16[256,4096]{1,0:T(8,128)(2,1)}) custom-call(s32[8]{0:T(128)} %stack.53.starts, bf16[256,4096]{1,0:T(8,128)(2,1)} %copy-done, f32[256,512]{1,0:T(8,128)} %shard_map.83.partial, bf16[1024,512]{1,0:T(8,128)(2,1)} %copy-done.1, bf16[1024,512]{1,0:T(8,128)(2,1)} %copy-done.6, ...), custom_call_target="tpu_custom_call" | custom-call | flops 1 | bytes 1 | tf_op jit(solution)/shard_map/pallas_call | solution.py:246
  96.7 2.8 %collective-permute-done.10.rest_0_ = bf16[256,1024]{1,0:T(8,128)(2,1)S(1)} collective-permute-done((bf16[256,1024]{1,0:T(8,128)(2,1)}, bf16[256,1024]{1,0:T(8,128)(2,1)S(1)}, u32[]{:S(2)}, u32[]{:S(2)}) %collective-permute-start.10) | collective-permute-done | bytes 524320 | tf_op jit(solution)/shard_map/ppermute | solution.py:28
  99.5 0.9 collective-permute-done.11.rest_2_
  100.4 2.7 %collective-permute-start.13 = (bf16[256,4096]{1,0:T(8,128)(2,1)}, bf16[256,4096]{1,0:T(8,128)(2,1)S(1)}, u32[]{:S(2)}, u32[]{:S(2)}) collective-permute-start(bf16[256,4096]{1,0:T(8,128)(2,1)} %get-tuple-element.43), channel_id=1, source_target_pairs={{0,8},{8,16},{16,24},{24,32},{32,40},{40,48},{48,56},{56,64},{64,7... | collective-permute-start | bytes 6291464 | tf_op jit(solution)/shard_map/ppermute | solution.py:18
  103.2 1.5 constant_dynamic-slice_fusion
  104.7 1.0 pad_maximum_fusion
  105.7 1.4 collective-permute-start.15
  107.1 2.8 %collective-permute-start.16 = (bf16[256,1536]{1,0:T(8,128)(2,1)S(1)}, bf16[256,1536]{1,0:T(8,128)(2,1)S(1)}, u32[]{:S(2)}, u32[]{:S(2)}) collective-permute-start(bf16[256,1536]{1,0:T(8,128)(2,1)S(1)} %get-tuple-element.74), channel_id=1, source_target_pairs={{0,4},{1,5},{2,6},{3,7},{4,0},{5,1},{6,2},{7,3},{8,12},{9,13},{10,... | collective-permute-start | bytes 2359304 | tf_op jit(solution)/shard_map/ppermute | solution.py:28
  110.0 0.9 collective-permute-start.17
  110.8 8.5 %shard_map.85 = (bf16[256,512]{1,0:T(8,128)(2,1)}, bf16[256,4096]{1,0:T(8,128)(2,1)}) custom-call(s32[8]{0:T(128)} %stack.53.starts, bf16[256,4096]{1,0:T(8,128)(2,1)} %collective-permute-done.12.upstream.whole, f32[256,512]{1,0:T(8,128)} %get-tuple-element.45.slope, bf16[1024,512]{1,0:T(8,128)(2,1)} %copy-done.1, bf16[1024,512]{1,0:T(8,128)(2,1)} %copy-done.6, ...), custom_call_target="tpu_custom_call" | custom-call | flops 1 | bytes 1 | tf_op jit(solution)/shard_map/pallas_call | solution.py:246
  119.3 7.1 %collective-permute-done.13.inputs = bf16[256,4096]{1,0:T(8,128)(2,1)S(1)} collective-permute-done((bf16[256,4096]{1,0:T(8,128)(2,1)}, bf16[256,4096]{1,0:T(8,128)(2,1)S(1)}, u32[]{:S(2)}, u32[]{:S(2)}) %collective-permute-start.13) | collective-permute-done | bytes 2097184 | tf_op jit(solution)/shard_map/ppermute | solution.py:18
  126.5 1.4 copy-done.17
  127.8 7.6 %shard_map.86 = bf16[256,4096]{1,0:T(8,128)(2,1)} custom-call(s32[8]{0:T(128)} %stack.53.starts, bf16[256,4096]{1,0:T(8,128)(2,1)} %copy-done.17, bf16[1024,512]{1,0:T(8,128)(2,1)} %copy-done.1, bf16[1024,512]{1,0:T(8,128)(2,1)} %copy-done.6, bf16[1024,512]{1,0:T(8,128)(2,1)} %copy-done.2, bf16[1024,512]{1,0:T(8,128)(2,1)} %copy-done.3, ...), custom_call_target="tpu_custom_call" | custom-call | flops 1 | bytes 1 | tf_op jit(solution)/shard_map/pallas_call | solution.py:246
  135.5 3.7 %collective-permute-start.14 = (bf16[256,4096]{1,0:T(8,128)(2,1)}, bf16[256,4096]{1,0:T(8,128)(2,1)}, u32[]{:S(2)}, u32[]{:S(2)}) collective-permute-start(bf16[256,4096]{1,0:T(8,128)(2,1)} %shard_map.86), channel_id=1, source_target_pairs={{0,248},{8,0},{16,8},{24,16},{32,24},{40,32},{48,40},{56,48},{64,5... | collective-permute-start | bytes 6291464 | tf_op jit(solution)/shard_map/ppermute | solution.py:18
  139.2 0.9 pad_maximum_fusion.4
  140.1 5.0 %collective-permute-done.16.rest_1_.rest_4_ = bf16[256,1536]{1,0:T(8,128)(2,1)S(1)} collective-permute-done((bf16[256,1536]{1,0:T(8,128)(2,1)S(1)}, bf16[256,1536]{1,0:T(8,128)(2,1)S(1)}, u32[]{:S(2)}, u32[]{:S(2)}) %collective-permute-start.16) | collective-permute-done | bytes 786464 | tf_op jit(solution)/shard_map/ppermute | solution.py:28
  145.1 1.8 collective-permute-start.18
  147.5 3.6 %shard_map.91 = bf16[512,512]{1,0:T(8,128)(2,1)} custom-call(s32[2]{0:T(128)} %pad_add_fusion.starts, bf16[256,4096]{1,0:T(8,128)(2,1)} %collective-permute-done.12.upstream.whole, bf16[256,512]{1,0:T(8,128)(2,1)} %get-tuple-element.50.other, bf16[256,1536]{1,0:T(8,128)(2,1)} %copy-done.7, bf16[256,1536]{1,0:T(8,128)(2,1)} %copy-done.8, ...), custom_call_target="tpu_custom_call" | custom-call | flops 1 | bytes 1 | tf_op jit(solution)/shard_map/pallas_call | solution.py:246
  151.1 0.9 collective-permute-start.22
  152.5 2.1 %collective-permute-start.20 = (bf16[256,512]{1,0:T(8,128)(2,1)S(1)}, bf16[256,512]{1,0:T(8,128)(2,1)S(1)}, u32[]{:S(2)}, u32[]{:S(2)}) collective-permute-start(bf16[256,512]{1,0:T(8,128)(2,1)S(1)} %copy-done.16), channel_id=1, source_target_pairs={{0,6},{1,7},{2,0},{3,1},{4,2},{5,3},{6,4},{7,5},{8,14},{9,15},{10,... | collective-permute-start | bytes 786440 | tf_op jit(solution)/shard_map/ppermute | solution.py:28
  155.3 3.8 %shard_map.88 = f32[512,512]{1,0:T(8,128)} custom-call(s32[2]{0:T(128)} %pad_add_fusion.1.starts, bf16[256,4096]{1,0:T(8,128)(2,1)} %collective-permute-done.12.upstream.whole, bf16[256,512]{1,0:T(8,128)(2,1)} %get-tuple-element.50.other, bf16[256,1536]{1,0:T(8,128)(2,1)} %copy-done.7, bf16[256,1536]{1,0:T(8,128)(2,1)} %copy-done.8, ...), custom_call_target="tpu_custom_call" | custom-call | flops 1 | bytes 1 | tf_op jit(solution)/shard_map/pallas_call | solution.py:246
  159.1 13.1 %collective-permute-done.19.rest_3_ = bf16[256,512]{1,0:T(8,128)(2,1)S(1)} collective-permute-done((bf16[256,512]{1,0:T(8,128)(2,1)S(1)}, bf16[256,512]{1,0:T(8,128)(2,1)S(1)}, u32[]{:S(2)}, u32[]{:S(2)}) %collective-permute-start.19) | collective-permute-done | bytes 262176 | tf_op jit(solution)/shard_map/ppermute | solution.py:28
  173.0 0.9 copy-done.10
  173.9 3.7 %shard_map.89 = bf16[512,512]{1,0:T(8,128)(2,1)} custom-call(s32[2]{0:T(128)} %pad_add_fusion.starts, bf16[256,4096]{1,0:T(8,128)(2,1)} %copy-done, bf16[256,512]{1,0:T(8,128)(2,1)} %get-tuple-element.53.other, bf16[256,1024]{1,0:T(8,128)(2,1)} %copy-done.19, bf16[256,1536]{1,0:T(8,128)(2,1)} %copy-done.10, bf16[256,1024]{1,0:T(8,128)(2,1)} %copy-done.20, ...), custom_call_target="tpu_custom_call" | custom-call | flops 1 | bytes 1 | tf_op jit(solution)/shard_map/pallas_call | solution.py:246
  178.1 3.8 %shard_map.90 = f32[512,512]{1,0:T(8,128)} custom-call(s32[2]{0:T(128)} %pad_add_fusion.1.starts, bf16[256,4096]{1,0:T(8,128)(2,1)} %copy-done, bf16[256,512]{1,0:T(8,128)(2,1)} %get-tuple-element.53.other, bf16[256,1024]{1,0:T(8,128)(2,1)} %copy-done.19, bf16[256,1536]{1,0:T(8,128)(2,1)} %copy-done.10, bf16[256,1024]{1,0:T(8,128)(2,1)} %copy-done.20, ...), custom_call_target="tpu_custom_call" | custom-call | flops 1 | bytes 1 | tf_op jit(solution)/shard_map/pallas_call | solution.py:246
  181.9 1.1 add_bitcast_fusion
  183.0 2.5 %shard_map.87 = bf16[256,4096]{1,0:T(8,128)(2,1)} custom-call(bf16[256,4096]{1,0:T(8,128)(2,1)} %collective-permute-done.14.source), custom_call_target="tpu_custom_call" | custom-call | flops 1 | bytes 1 | tf_op jit(solution)/shard_map/pallas_call | solution.py:246
  185.5 6.8 %collective-permute-done.21 = bf16[512,512]{1,0:T(8,128)(2,1)S(1)} collective-permute-done((bf16[512,512]{1,0:T(8,128)(2,1)}, bf16[512,512]{1,0:T(8,128)(2,1)S(1)}, u32[]{:S(2)}, u32[]{:S(2)}) %collective-permute-start.21) | collective-permute-done | bytes 524320 | tf_op jit(solution)/shard_map/ppermute | solution.py:32
  192.3 1.1 add_bitcast_fusion.1
  (69 shorter events, 5.9 us)
Async XLA Ops:
  0.6 30.2 %copy-start.23 = (bf16[1,256,4096]{2,1,0:T(8,128)(2,1)S(1)}, bf16[1,256,4096]{2,1,0:T(8,128)(2,1)}, u32[]{:S(2)}) copy-start(bf16[1,256,4096]{2,1,0:T(8,128)(2,1)} %param.4) | copy-start | bytes 6291460
  2.1 74.3 %copy-start.1 = (bf16[1024,512]{1,0:T(8,128)(2,1)}, bf16[1024,512]{1,0:T(8,128)(2,1)S(1)}, u32[]{:S(2)}) copy-start(bf16[1024,512]{1,0:T(8,128)(2,1)S(1)} %pad_maximum_fusion.3.rest_0_) | copy-start | bytes 3145732
  2.1 25.7 %collective-permute-start = (bf16[1024,512]{1,0:T(8,128)(2,1)S(1)}, bf16[1024,512]{1,0:T(8,128)(2,1)S(1)}, u32[]{:S(2)}, u32[]{:S(2)}) collective-permute-start(bf16[1024,512]{1,0:T(8,128)(2,1)S(1)} %pad_maximum_fusion.3.rest_0_), channel_id=1, source_target_pairs={{0,1},{1,0},{2,3},{3,2},{4,5},{5,4},{6,7},{7,6},{8,9},{9,8},{10,11... | collective-permute-start | bytes 3145736 | tf_op jit(solution)/shard_map/ppermute | solution.py:32
  5.9 24.9 %collective-permute-start.1 = (bf16[1024,512]{1,0:T(8,128)(2,1)S(1)}, bf16[1024,512]{1,0:T(8,128)(2,1)S(1)}, u32[]{:S(2)}, u32[]{:S(2)}) collective-permute-start(bf16[1024,512]{1,0:T(8,128)(2,1)S(1)} %pad_maximum_fusion.3.rest_0_), channel_id=1, source_target_pairs={{0,2},{1,3},{2,4},{3,5},{4,6},{5,7},{6,0},{7,1},{8,10},{9,11},{10,... | collective-permute-start | bytes 3145736 | tf_op jit(solution)/shard_map/ppermute | solution.py:28
  7.1 23.7 %collective-permute-start.2 = (bf16[1024,512]{1,0:T(8,128)(2,1)S(1)}, bf16[1024,512]{1,0:T(8,128)(2,1)S(1)}, u32[]{:S(2)}, u32[]{:S(2)}) collective-permute-start(bf16[1024,512]{1,0:T(8,128)(2,1)S(1)} %pad_maximum_fusion.3.rest_0_), channel_id=1, source_target_pairs={{0,6},{1,7},{2,0},{3,1},{4,2},{5,3},{6,4},{7,5},{8,14},{9,15},{10,... | collective-permute-start | bytes 3145736 | tf_op jit(solution)/shard_map/ppermute | solution.py:28
  27.7 43.5 %copy-start.6 = (bf16[1024,512]{1,0:T(8,128)(2,1)}, bf16[1024,512]{1,0:T(8,128)(2,1)S(1)}, u32[]{:S(2)}) copy-start(bf16[1024,512]{1,0:T(8,128)(2,1)S(1)} %collective-permute-done.rest_1_) | copy-start | bytes 3145732
  30.8 39.7 %copy-start.2 = (bf16[1024,512]{1,0:T(8,128)(2,1)}, bf16[1024,512]{1,0:T(8,128)(2,1)S(1)}, u32[]{:S(2)}) copy-start(bf16[1024,512]{1,0:T(8,128)(2,1)S(1)} %collective-permute-done.1.rest_2_) | copy-start | bytes 3145732
  30.8 39.7 %copy-start.3 = (bf16[1024,512]{1,0:T(8,128)(2,1)}, bf16[1024,512]{1,0:T(8,128)(2,1)S(1)}, u32[]{:S(2)}) copy-start(bf16[1024,512]{1,0:T(8,128)(2,1)S(1)} %collective-permute-done.2.rest_3_) | copy-start | bytes 3145732
  30.8 39.6 %collective-permute-start.3 = (bf16[256,4096]{1,0:T(8,128)(2,1)S(1)}, bf16[256,4096]{1,0:T(8,128)(2,1)S(1)}, u32[]{:S(2)}, u32[]{:S(2)}) collective-permute-start(bf16[256,4096]{1,0:T(8,128)(2,1)S(1)} %bitcast.26), channel_id=1, source_target_pairs={{0,8},{8,16},{16,24},{24,32},{32,40},{40,48},{48,56},{56,64},{64,7... | collective-permute-start | bytes 6291464 | tf_op jit(solution)/shard_map/ppermute | solution.py:18
  33.1 37.4 %collective-permute-start.6 = (bf16[1024,512]{1,0:T(8,128)(2,1)S(1)}, bf16[1024,512]{1,0:T(8,128)(2,1)S(1)}, u32[]{:S(2)}, u32[]{:S(2)}) collective-permute-start(bf16[1024,512]{1,0:T(8,128)(2,1)S(1)} %collective-permute-done.rest_1_), channel_id=1, source_target_pairs={{0,2},{1,3},{2,4},{3,5},{4,6},{5,7},{6,0},{7,1},{8,10},{9,11},{10,... | collective-permute-start | bytes 3145736 | tf_op jit(solution)/shard_map/ppermute | solution.py:28
  34.2 36.3 %collective-permute-start.7 = (bf16[1024,512]{1,0:T(8,128)(2,1)S(1)}, bf16[1024,512]{1,0:T(8,128)(2,1)S(1)}, u32[]{:S(2)}, u32[]{:S(2)}) collective-permute-start(bf16[1024,512]{1,0:T(8,128)(2,1)S(1)} %collective-permute-done.rest_1_), channel_id=1, source_target_pairs={{0,6},{1,7},{2,0},{3,1},{4,2},{5,3},{6,4},{7,5},{8,14},{9,15},{10,... | collective-permute-start | bytes 3145736 | tf_op jit(solution)/shard_map/ppermute | solution.py:28
  35.8 34.6 %collective-permute-start.4 = (bf16[512,512]{1,0:T(8,128)(2,1)S(1)}, bf16[512,512]{1,0:T(8,128)(2,1)S(1)}, u32[]{:S(2)}, u32[]{:S(2)}) collective-permute-start(bf16[512,512]{1,0:T(8,128)(2,1)S(1)} %slice.12), channel_id=1, source_target_pairs={{0,2},{1,3},{2,4},{3,5},{4,6},{5,7},{6,0},{7,1},{8,10},{9,11},{10,... | collective-permute-start | bytes 1572872 | tf_op jit(solution)/shard_map/ppermute | solution.py:28
  35.9 34.5 %collective-permute-start.5 = (bf16[512,512]{1,0:T(8,128)(2,1)S(1)}, bf16[512,512]{1,0:T(8,128)(2,1)S(1)}, u32[]{:S(2)}, u32[]{:S(2)}) collective-permute-start(bf16[512,512]{1,0:T(8,128)(2,1)S(1)} %slice.13), channel_id=1, source_target_pairs={{0,6},{1,7},{2,0},{3,1},{4,2},{5,3},{6,4},{7,5},{8,14},{9,15},{10,... | collective-permute-start | bytes 1572872 | tf_op jit(solution)/shard_map/ppermute | solution.py:28
  70.4 0.8 copy-start.11
  70.4 1.0 copy-start.12
  70.4 1.3 copy-start.4
  70.5 1.6 copy-start.5
  70.5 9.3 %copy-start = (bf16[256,4096]{1,0:T(8,128)(2,1)}, bf16[256,4096]{1,0:T(8,128)(2,1)S(1)}, u32[]{:S(2)}) copy-start(bf16[256,4096]{1,0:T(8,128)(2,1)S(1)} %collective-permute-done.3.inputs.whole) | copy-start | bytes 6291460
  70.5 29.9 %collective-permute-start.12 = (bf16[256,4096]{1,0:T(8,128)(2,1)}, bf16[256,4096]{1,0:T(8,128)(2,1)}, u32[]{:S(2)}, u32[]{:S(2)}) collective-permute-start(bf16[256,4096]{1,0:T(8,128)(2,1)} %bitcast.12), channel_id=1, source_target_pairs={{0,248},{8,0},{16,8},{24,16},{32,24},{40,32},{48,40},{56,48},{64,5... | collective-permute-start | bytes 6291464 | tf_op jit(solution)/shard_map/ppermute | solution.py:18
  74.0 14.3 %collective-permute-start.8 = (bf16[512,512]{1,0:T(8,128)(2,1)}, bf16[512,512]{1,0:T(8,128)(2,1)}, u32[]{:S(2)}, u32[]{:S(2)}) collective-permute-start(bf16[512,512]{1,0:T(8,128)(2,1)} %slice.16), channel_id=1, source_target_pairs={{0,2},{1,3},{2,4},{3,5},{4,6},{5,7},{6,0},{7,1},{8,10},{9,11},{10,... | collective-permute-start | bytes 1572872 | tf_op jit(solution)/shard_map/ppermute | solution.py:28
  76.4 12.8 %collective-permute-start.9 = (bf16[512,512]{1,0:T(8,128)(2,1)}, bf16[512,512]{1,0:T(8,128)(2,1)}, u32[]{:S(2)}, u32[]{:S(2)}) collective-permute-start(bf16[512,512]{1,0:T(8,128)(2,1)} %slice.17), channel_id=1, source_target_pairs={{0,6},{1,7},{2,0},{3,1},{4,2},{5,3},{6,4},{7,5},{8,14},{9,15},{10,... | collective-permute-start | bytes 1572872 | tf_op jit(solution)/shard_map/ppermute | solution.py:28
  79.8 19.7 %collective-permute-start.10 = (bf16[256,1024]{1,0:T(8,128)(2,1)}, bf16[256,1024]{1,0:T(8,128)(2,1)S(1)}, u32[]{:S(2)}, u32[]{:S(2)}) collective-permute-start(bf16[256,1024]{1,0:T(8,128)(2,1)} %get-tuple-element.72), channel_id=1, source_target_pairs={{0,2},{1,3},{2,4},{3,5},{4,6},{5,7},{6,0},{7,1},{8,10},{9,11},{10,... | collective-permute-start | bytes 1572872 | tf_op jit(solution)/shard_map/ppermute | solution.py:28
  79.8 20.6 %collective-permute-start.11 = (bf16[256,1024]{1,0:T(8,128)(2,1)}, bf16[256,1024]{1,0:T(8,128)(2,1)S(1)}, u32[]{:S(2)}, u32[]{:S(2)}) collective-permute-start(bf16[256,1024]{1,0:T(8,128)(2,1)} %get-tuple-element.71), channel_id=1, source_target_pairs={{0,6},{1,7},{2,0},{3,1},{4,2},{5,3},{6,4},{7,5},{8,14},{9,15},{10,... | collective-permute-start | bytes 1572872 | tf_op jit(solution)/shard_map/ppermute | solution.py:28
  96.7 8.0 %copy-start.15 = (bf16[256,512]{1,0:T(8,128)(2,1)S(1)}, bf16[256,512]{1,0:T(8,128)(2,1)}, u32[]{:S(2)}) copy-start(bf16[256,512]{1,0:T(8,128)(2,1)} %get-tuple-element.50.other) | copy-start | bytes 786436
  99.5 6.2 %copy-start.19 = (bf16[256,1024]{1,0:T(8,128)(2,1)}, bf16[256,1024]{1,0:T(8,128)(2,1)S(1)}, u32[]{:S(2)}) copy-start(bf16[256,1024]{1,0:T(8,128)(2,1)S(1)} %collective-permute-done.10.rest_0_) | copy-start | bytes 1572868
  100.4 5.3 %copy-start.20 = (bf16[256,1024]{1,0:T(8,128)(2,1)}, bf16[256,1024]{1,0:T(8,128)(2,1)S(1)}, u32[]{:S(2)}) copy-start(bf16[256,1024]{1,0:T(8,128)(2,1)S(1)} %collective-permute-done.11.rest_2_) | copy-start | bytes 1572868
  100.4 26.0 %collective-permute-start.13 = (bf16[256,4096]{1,0:T(8,128)(2,1)}, bf16[256,4096]{1,0:T(8,128)(2,1)S(1)}, u32[]{:S(2)}, u32[]{:S(2)}) collective-permute-start(bf16[256,4096]{1,0:T(8,128)(2,1)} %get-tuple-element.43), channel_id=1, source_target_pairs={{0,8},{8,16},{16,24},{24,32},{32,40},{40,48},{48,56},{56,64},{64,7... | collective-permute-start | bytes 6291464 | tf_op jit(solution)/shard_map/ppermute | solution.py:18
  105.7 34.4 %collective-permute-start.15 = (bf16[256,1536]{1,0:T(8,128)(2,1)}, bf16[256,1536]{1,0:T(8,128)(2,1)S(1)}, u32[]{:S(2)}, u32[]{:S(2)}) collective-permute-start(bf16[256,1536]{1,0:T(8,128)(2,1)} %get-tuple-element.75), channel_id=1, source_target_pairs={{0,2},{1,3},{2,4},{3,5},{4,6},{5,7},{6,0},{7,1},{8,10},{9,11},{10,... | collective-permute-start | bytes 2359304 | tf_op jit(solution)/shard_map/ppermute | solution.py:28
  107.1 38.0 %collective-permute-start.16 = (bf16[256,1536]{1,0:T(8,128)(2,1)S(1)}, bf16[256,1536]{1,0:T(8,128)(2,1)S(1)}, u32[]{:S(2)}, u32[]{:S(2)}) collective-permute-start(bf16[256,1536]{1,0:T(8,128)(2,1)S(1)} %get-tuple-element.74), channel_id=1, source_target_pairs={{0,4},{1,5},{2,6},{3,7},{4,0},{5,1},{6,2},{7,3},{8,12},{9,13},{10,... | collective-permute-start | bytes 2359304 | tf_op jit(solution)/shard_map/ppermute | solution.py:28
  110.0 35.1 %collective-permute-start.17 = (bf16[256,1536]{1,0:T(8,128)(2,1)S(1)}, bf16[256,1536]{1,0:T(8,128)(2,1)S(1)}, u32[]{:S(2)}, u32[]{:S(2)}) collective-permute-start(bf16[256,1536]{1,0:T(8,128)(2,1)S(1)} %get-tuple-element.73), channel_id=1, source_target_pairs={{0,6},{1,7},{2,0},{3,1},{4,2},{5,3},{6,4},{7,5},{8,14},{9,15},{10,... | collective-permute-start | bytes 2359304 | tf_op jit(solution)/shard_map/ppermute | solution.py:28
  126.5 1.4 copy-start.17
  127.8 11.3 %copy-start.16 = (bf16[256,512]{1,0:T(8,128)(2,1)S(1)}, bf16[256,512]{1,0:T(8,128)(2,1)}, u32[]{:S(2)}) copy-start(bf16[256,512]{1,0:T(8,128)(2,1)} %get-tuple-element.53.other) | copy-start | bytes 786436
  127.8 11.3 %copy-start.18 = (bf16[256,1024]{1,0:T(8,128)(2,1)S(1)}, bf16[256,1024]{1,0:T(8,128)(2,1)}, u32[]{:S(2)}) copy-start(bf16[256,1024]{1,0:T(8,128)(2,1)} %get-tuple-element.70) | copy-start | bytes 1572868
  135.5 47.5 %collective-permute-start.14 = (bf16[256,4096]{1,0:T(8,128)(2,1)}, bf16[256,4096]{1,0:T(8,128)(2,1)}, u32[]{:S(2)}, u32[]{:S(2)}) collective-permute-start(bf16[256,4096]{1,0:T(8,128)(2,1)} %shard_map.86), channel_id=1, source_target_pairs={{0,248},{8,0},{16,8},{24,16},{32,24},{40,32},{48,40},{56,48},{64,5... | collective-permute-start | bytes 6291464 | tf_op jit(solution)/shard_map/ppermute | solution.py:18
  140.1 7.4 %copy-start.7 = (bf16[256,1536]{1,0:T(8,128)(2,1)}, bf16[256,1536]{1,0:T(8,128)(2,1)S(1)}, u32[]{:S(2)}) copy-start(bf16[256,1536]{1,0:T(8,128)(2,1)S(1)} %collective-permute-done.15.rest_0_.rest_3_) | copy-start | bytes 2359300
  145.1 2.4 %copy-start.8 = (bf16[256,1536]{1,0:T(8,128)(2,1)}, bf16[256,1536]{1,0:T(8,128)(2,1)S(1)}, u32[]{:S(2)}) copy-start(bf16[256,1536]{1,0:T(8,128)(2,1)S(1)} %collective-permute-done.16.rest_1_.rest_4_) | copy-start | bytes 2359300
  145.1 2.4 %copy-start.9 = (bf16[256,1536]{1,0:T(8,128)(2,1)}, bf16[256,1536]{1,0:T(8,128)(2,1)S(1)}, u32[]{:S(2)}) copy-start(bf16[256,1536]{1,0:T(8,128)(2,1)S(1)} %collective-permute-done.17.rest_2_.rest_5_) | copy-start | bytes 2359300
  145.1 27.1 %collective-permute-start.18 = (bf16[256,1536]{1,0:T(8,128)(2,1)}, bf16[256,1536]{1,0:T(8,128)(2,1)S(1)}, u32[]{:S(2)}, u32[]{:S(2)}) collective-permute-start(bf16[256,1536]{1,0:T(8,128)(2,1)} %pad_maximum_fusion.4), channel_id=1, source_target_pairs={{0,4},{1,5},{2,6},{3,7},{4,0},{5,1},{6,2},{7,3},{8,12},{9,13},{10,... | collective-permute-start | bytes 2359304 | tf_op jit(solution)/shard_map/ppermute | solution.py:28
  151.1 30.7 %collective-permute-start.22 = (bf16[512,512]{1,0:T(8,128)(2,1)}, bf16[512,512]{1,0:T(8,128)(2,1)S(1)}, u32[]{:S(2)}, u32[]{:S(2)}) collective-permute-start(bf16[512,512]{1,0:T(8,128)(2,1)} %shard_map.91), channel_id=1, source_target_pairs={{0,1},{1,0},{2,3},{3,2},{4,5},{5,4},{6,7},{7,6},{8,9},{9,8},{10,11... | collective-permute-start | bytes 1572872 | tf_op jit(solution)/shard_map/ppermute | solution.py:32
  152.0 20.2 %collective-permute-start.19 = (bf16[256,512]{1,0:T(8,128)(2,1)S(1)}, bf16[256,512]{1,0:T(8,128)(2,1)S(1)}, u32[]{:S(2)}, u32[]{:S(2)}) collective-permute-start(bf16[256,512]{1,0:T(8,128)(2,1)S(1)} %copy-done.16), channel_id=1, source_target_pairs={{0,2},{1,3},{2,4},{3,5},{4,6},{5,7},{6,0},{7,1},{8,10},{9,11},{10,... | collective-permute-start | bytes 786440 | tf_op jit(solution)/shard_map/ppermute | solution.py:28
  152.5 19.6 %collective-permute-start.20 = (bf16[256,512]{1,0:T(8,128)(2,1)S(1)}, bf16[256,512]{1,0:T(8,128)(2,1)S(1)}, u32[]{:S(2)}, u32[]{:S(2)}) collective-permute-start(bf16[256,512]{1,0:T(8,128)(2,1)S(1)} %copy-done.16), channel_id=1, source_target_pairs={{0,6},{1,7},{2,0},{3,1},{4,2},{5,3},{6,4},{7,5},{8,14},{9,15},{10,... | collective-permute-start | bytes 786440 | tf_op jit(solution)/shard_map/ppermute | solution.py:28
  172.2 0.7 copy-start.21
  172.2 0.8 copy-start.22
  173.0 0.9 copy-start.10
  177.5 4.3 %copy-start.14 = (f32[512,512]{1,0:T(8,128)S(1)}, f32[512,512]{1,0:T(8,128)}, u32[]{:S(2)}) copy-start(f32[512,512]{1,0:T(8,128)} %shard_map.88) | copy-start | bytes 3145732
  177.5 14.8 %collective-permute-start.21 = (bf16[512,512]{1,0:T(8,128)(2,1)}, bf16[512,512]{1,0:T(8,128)(2,1)S(1)}, u32[]{:S(2)}, u32[]{:S(2)}) collective-permute-start(bf16[512,512]{1,0:T(8,128)(2,1)} %shard_map.89), channel_id=1, source_target_pairs={{0,1},{1,0},{2,3},{3,2},{4,5},{5,4},{6,7},{7,6},{8,9},{9,8},{10,11... | collective-permute-start | bytes 1572872 | tf_op jit(solution)/shard_map/ppermute | solution.py:32
  183.0 9.3 %copy-start.13 = (f32[512,512]{1,0:T(8,128)S(1)}, f32[512,512]{1,0:T(8,128)}, u32[]{:S(2)}) copy-start(f32[512,512]{1,0:T(8,128)} %shard_map.90) | copy-start | bytes 3145732

commit v6 on v3

--- a/solution.py
+++ b/solution.py
@@ -374,9 +374,6 @@
 
     received_out = swap_y(part(other, BF16, upstream, hidden, *out_pieces))
     mine_out = part(ours, F32, upstream, hidden, *out_pieces)
-    received_in = swap_y(part(other, BF16, inputs, dpre, *in_pieces))
-    mine_in = part(ours, F32, inputs, dpre, *in_pieces)
-    grad_out = mine_out + received_out.astype(F32)
     shadow = local_call(
         copy_kernel,
         activations,
@@ -386,9 +383,11 @@
         16,
         shadow,
     )
-    shadow, received_in, grad_out = lax.optimization_barrier(
-        (shadow, received_in, grad_out)
-    )
+    in_pieces, mine_out = lax.optimization_barrier((in_pieces, mine_out))
+    received_in = swap_y(part(other, BF16, inputs, dpre, *in_pieces))
+    mine_in = part(ours, F32, inputs, dpre, *in_pieces)
+    grad_out = mine_out + received_out.astype(F32)
+    shadow, received_in = lax.optimization_barrier((shadow, received_in))
     grad_in = mine_in + received_in.astype(F32)
     return (
         layer_out[None],

time: 189 us -> 189 us (level)
    ppermute x14, waiting for transfers between devices: 63.1 us -> 58.8 us  [over_x(): return lax.ppermute(array, 'dp', pairs)]
    ppermute x3, waiting for transfers between devices: 19.2 us -> 23 us  [swap_y(): lax.ppermute(array, 'dp', [(i, i ^ 1) for i in range(X_SIZE * Y_SIZE)])]
    add x1 -> x0, other arithmetic: 2.36 us -> none  [on_device(): grad_out = mine_out + received_out.astype(F32)]
  transfers between devices with their start and end apart: 21 -> 21, of which waited for: 10 -> 11; matrix products, arithmetic and copies ran while one was open for 5% -> 4% of each run, Pallas kernels for 24% -> 24%
where the time goes in v6:
time: 189 us; the launch traced here: 187 us
  waiting for transfers between devices  91.4 us (48%)
  Pallas kernels  45.5 us (24%)
  starting transfers between devices  37.5 us (20%)
  other arithmetic  6.55 us (3%)
  local copies, waits for them, and re-layouts  5.1 us (3%)
    ppermute x14, waiting for transfers between devices, over_x(): return lax.ppermute(array, 'dp', pairs)  58.8 us
    pallas_call x9, Pallas kernels, local_call(): pl.pallas_call(kernel, out_shape=outs, in_specs=in_specs, out_specs=out_s...  45.5 us
    ppermute x3, waiting for transfers between devices, swap_y(): lax.ppermute(array, 'dp', [(i, i ^ 1) for i in range(X_SIZE * Y_SIZE)])  23 us
    ppermute x14, starting transfers between devices, over_x(): return lax.ppermute(array, 'dp', pairs)  19.8 us
    ppermute x4, waiting for transfers between devices, over_section(): lax.ppermute(array, 'section', [(i, (i + by) % devices) for i in range(de...  9.62 us
    ppermute x3, starting transfers between devices, swap_y(): lax.ppermute(array, 'dp', [(i, i ^ 1) for i in range(X_SIZE * Y_SIZE)])  9.43 us
    ppermute x4, starting transfers between devices, over_section(): lax.ppermute(array, 'section', [(i, (i + by) % devices) for i in range(de...  8.26 us
  transfers between devices with their start and end apart: 21, of which 11 were waited for; matrix products, arithmetic and copies ran while one was open for 4% of the time, Pallas kernels for 24%

profile of v6, /device:TPU:1, one launch (start us, length us, event | category | flops | bytes accessed | tf_op | source)
XLA Modules:
  0.0 186.9 jit_solution(14364262755258508761)
XLA Ops:
  0.6 1.4 pad_maximum_fusion.6.rest_0_
  2.1 3.8 %collective-permute-start = (bf16[1024,512]{1,0:T(8,128)(2,1)S(1)}, bf16[1024,512]{1,0:T(8,128)(2,1)S(1)}, u32[]{:S(2)}, u32[]{:S(2)}) collective-permute-start(bf16[1024,512]{1,0:T(8,128)(2,1)S(1)} %pad_maximum_fusion.6.rest_0_), channel_id=1, source_target_pairs={{0,1},{1,0},{2,3},{3,2},{4,5},{5,4},{6,7},{7,6},{8,9},{9,8},{10,11... | collective-permute-start | bytes 3145736 | tf_op jit(solution)/shard_map/ppermute | solution.py:32
  5.9 1.2 collective-permute-start.1
  7.1 1.5 collective-permute-start.2
  8.6 19.1 %collective-permute-done.rest_1_ = bf16[1024,512]{1,0:T(8,128)(2,1)S(1)} collective-permute-done((bf16[1024,512]{1,0:T(8,128)(2,1)S(1)}, bf16[1024,512]{1,0:T(8,128)(2,1)S(1)}, u32[]{:S(2)}, u32[]{:S(2)}) %collective-permute-start) | collective-permute-done | bytes 1048608 | tf_op jit(solution)/shard_map/ppermute | solution.py:32
  27.7 3.1 %collective-permute-done.1.rest_2_ = bf16[1024,512]{1,0:T(8,128)(2,1)S(1)} collective-permute-done((bf16[1024,512]{1,0:T(8,128)(2,1)S(1)}, bf16[1024,512]{1,0:T(8,128)(2,1)S(1)}, u32[]{:S(2)}, u32[]{:S(2)}) %collective-permute-start.1) | collective-permute-done | bytes 1048608 | tf_op jit(solution)/shard_map/ppermute | solution.py:28
  30.8 2.2 %collective-permute-start.3 = (bf16[256,4096]{1,0:T(8,128)(2,1)S(1)}, bf16[256,4096]{1,0:T(8,128)(2,1)S(1)}, u32[]{:S(2)}, u32[]{:S(2)}) collective-permute-start(bf16[256,4096]{1,0:T(8,128)(2,1)S(1)} %bitcast.26), channel_id=1, source_target_pairs={{0,8},{8,16},{16,24},{24,32},{32,40},{40,48},{48,56},{56,64},{64,7... | collective-permute-start | bytes 6291464 | tf_op jit(solution)/shard_map/ppermute | solution.py:18
  33.1 1.1 collective-permute-start.4
  34.2 1.6 collective-permute-start.5
  35.9 2.7 %collective-permute-start.7 = (bf16[512,512]{1,0:T(8,128)(2,1)S(1)}, bf16[512,512]{1,0:T(8,128)(2,1)}, u32[]{:S(2)}, u32[]{:S(2)}) collective-permute-start(bf16[512,512]{1,0:T(8,128)(2,1)S(1)} %slice.13), channel_id=1, source_target_pairs={{0,6},{1,7},{2,0},{3,1},{4,2},{5,3},{6,4},{7,5},{8,14},{9,15},{10,... | collective-permute-start | bytes 1572872 | tf_op jit(solution)/shard_map/ppermute | solution.py:28
  38.7 20.5 %collective-permute-done.4.rest_4_ = bf16[1024,512]{1,0:T(8,128)(2,1)S(1)} collective-permute-done((bf16[1024,512]{1,0:T(8,128)(2,1)S(1)}, bf16[1024,512]{1,0:T(8,128)(2,1)S(1)}, u32[]{:S(2)}, u32[]{:S(2)}) %collective-permute-start.4) | collective-permute-done | bytes 1048608 | tf_op jit(solution)/shard_map/ppermute | solution.py:28
  59.2 0.9 slice.16
  60.1 0.9 slice.17
  61.0 2.7 %collective-permute-start.9 = (bf16[512,512]{1,0:T(8,128)(2,1)}, bf16[512,512]{1,0:T(8,128)(2,1)}, u32[]{:S(2)}, u32[]{:S(2)}) collective-permute-start(bf16[512,512]{1,0:T(8,128)(2,1)} %slice.17), channel_id=1, source_target_pairs={{0,6},{1,7},{2,0},{3,1},{4,2},{5,3},{6,4},{7,5},{8,14},{9,15},{10,... | collective-permute-start | bytes 1572872 | tf_op jit(solution)/shard_map/ppermute | solution.py:28
  63.8 1.6 collective-permute-start.11
  65.3 0.7 stack.53.starts
  66.0 4.5 %collective-permute-done.6.rest_6_ = bf16[512,512]{1,0:T(8,128)(2,1)} collective-permute-done((bf16[512,512]{1,0:T(8,128)(2,1)S(1)}, bf16[512,512]{1,0:T(8,128)(2,1)}, u32[]{:S(2)}, u32[]{:S(2)}) %collective-permute-start.6) | collective-permute-done | bytes 524320 | tf_op jit(solution)/shard_map/ppermute | solution.py:28
  70.5 4.5 %shard_map.83.partial = f32[256,512]{1,0:T(8,128)} custom-call(s32[8]{0:T(128)} %stack.53.starts, bf16[256,4096]{1,0:T(8,128)(2,1)} %copy-done, bf16[1024,512]{1,0:T(8,128)(2,1)} %copy-done.2, bf16[1024,512]{1,0:T(8,128)(2,1)} %copy-done.7, bf16[1024,512]{1,0:T(8,128)(2,1)} %copy-done.3, bf16[1024,512]{1,0:T(8,128)(2,1)} %copy-done.4, ...), custom_call_target="tpu_custom_call" | custom-call | flops 1 | bytes 1 | tf_op jit(solution)/shard_map/pallas_call | solution.py:245
  75.0 6.8 %collective-permute-done.8.rest_8_ = bf16[512,512]{1,0:T(8,128)(2,1)} collective-permute-done((bf16[512,512]{1,0:T(8,128)(2,1)}, bf16[512,512]{1,0:T(8,128)(2,1)}, u32[]{:S(2)}, u32[]{:S(2)}) %collective-permute-start.8) | collective-permute-done | bytes 524320 | tf_op jit(solution)/shard_map/ppermute | solution.py:28
  81.8 7.5 %shard_map.84 = (bf16[256,512]{1,0:T(8,128)(2,1)}, f32[256,512]{1,0:T(8,128)}, bf16[256,4096]{1,0:T(8,128)(2,1)}) custom-call(s32[8]{0:T(128)} %stack.53.starts, bf16[256,4096]{1,0:T(8,128)(2,1)} %copy-done, f32[256,512]{1,0:T(8,128)} %shard_map.83.partial, bf16[1024,512]{1,0:T(8,128)(2,1)} %copy-done.2, bf16[1024,512]{1,0:T(8,128)(2,1)} %copy-done.7, ...), custom_call_target="tpu_custom_call" | custom-call | flops 1 | bytes 1 | tf_op jit(solution)/shard_map/pallas_call | solution.py:245
  89.3 0.3 collective-permute-start.10
  89.6 1.5 constant_dynamic-slice_fusion
  91.3 0.7 collective-permute-start.13
  92.0 3.0 %collective-permute-start.14 = (bf16[256,1536]{1,0:T(8,128)(2,1)S(1)}, bf16[256,1536]{1,0:T(8,128)(2,1)}, u32[]{:S(2)}, u32[]{:S(2)}) collective-permute-start(bf16[256,1536]{1,0:T(8,128)(2,1)S(1)} %get-tuple-element.62), channel_id=1, source_target_pairs={{0,4},{1,5},{2,6},{3,7},{4,0},{5,1},{6,2},{7,3},{8,12},{9,13},{10,... | collective-permute-start | bytes 2359304 | tf_op jit(solution)/shard_map/ppermute | solution.py:28
  95.1 0.8 collective-permute-start.15
  95.8 8.5 %shard_map.85 = (bf16[256,512]{1,0:T(8,128)(2,1)}, bf16[256,4096]{1,0:T(8,128)(2,1)}) custom-call(s32[8]{0:T(128)} %stack.53.starts, bf16[256,4096]{1,0:T(8,128)(2,1)} %collective-permute-done.11.upstream.whole, f32[256,512]{1,0:T(8,128)} %get-tuple-element.37.slope, bf16[1024,512]{1,0:T(8,128)(2,1)} %copy-done.2, bf16[1024,512]{1,0:T(8,128)(2,1)} %copy-done.7, ...), custom_call_target="tpu_custom_call" | custom-call | flops 1 | bytes 1 | tf_op jit(solution)/shard_map/pallas_call | solution.py:245
  104.4 9.6 %collective-permute-done.10.inputs = bf16[256,4096]{1,0:T(8,128)(2,1)} collective-permute-done((bf16[256,4096]{1,0:T(8,128)(2,1)}, bf16[256,4096]{1,0:T(8,128)(2,1)}, u32[]{:S(2)}, u32[]{:S(2)}) %collective-permute-start.10) | collective-permute-done | bytes 2097184 | tf_op jit(solution)/shard_map/ppermute | solution.py:18
  114.0 7.6 %shard_map.86 = bf16[256,4096]{1,0:T(8,128)(2,1)} custom-call(s32[8]{0:T(128)} %stack.53.starts, bf16[256,4096]{1,0:T(8,128)(2,1)} %collective-permute-done.10.inputs, bf16[1024,512]{1,0:T(8,128)(2,1)} %copy-done.2, bf16[1024,512]{1,0:T(8,128)(2,1)} %copy-done.7, bf16[1024,512]{1,0:T(8,128)(2,1)} %copy-done.3, bf16[1024,512]{1,0:T(8,128)(2,1)} %copy-done.4, ...), custom_call_target="tpu_custom_call" | custom-call | flops 1 | bytes 1 | tf_op jit(solution)/shard_map/pallas_call | solution.py:245
  121.6 4.2 %collective-permute-start.12 = (bf16[256,4096]{1,0:T(8,128)(2,1)}, bf16[256,4096]{1,0:T(8,128)(2,1)}, u32[]{:S(2)}, u32[]{:S(2)}) collective-permute-start(bf16[256,4096]{1,0:T(8,128)(2,1)} %shard_map.86), channel_id=1, source_target_pairs={{0,248},{8,0},{16,8},{24,16},{32,24},{40,32},{48,40},{56,48},{64,5... | collective-permute-start | bytes 6291464 | tf_op jit(solution)/shard_map/ppermute | solution.py:18
  126.0 1.6 pad_maximum_fusion
  127.5 1.3 collective-permute-done.14.rest_1_
  128.8 1.8 collective-permute-start.16
  130.7 2.5 %collective-permute-start.17 = (bf16[256,1536]{1,0:T(8,128)(2,1)}, bf16[256,1536]{1,0:T(8,128)(2,1)S(1)}, u32[]{:S(2)}, u32[]{:S(2)}) collective-permute-start(bf16[256,1536]{1,0:T(8,128)(2,1)} %get-tuple-element.43), channel_id=1, source_target_pairs={{0,4},{1,5},{2,6},{3,7},{4,0},{5,1},{6,2},{7,3},{8,12},{9,13},{10,... | collective-permute-start | bytes 2359304 | tf_op jit(solution)/shard_map/ppermute | solution.py:28
  133.2 0.6 pad_add_fusion.starts
  133.8 3.6 %shard_map.91 = bf16[512,512]{1,0:T(8,128)(2,1)} custom-call(s32[2]{0:T(128)} %pad_add_fusion.starts, bf16[256,4096]{1,0:T(8,128)(2,1)} %collective-permute-done.11.upstream.whole, bf16[256,512]{1,0:T(8,128)(2,1)} %get-tuple-element.41.other, bf16[256,1536]{1,0:T(8,128)(2,1)} %copy-done.10, bf16[256,1536]{1,0:T(8,128)(2,1)} %collective-permute-done.14.rest_1_, ...), custom_call_target="tpu_custom_call" | custom-call | flops 1 | bytes 1 | tf_op jit(solution)/shard_map/pallas_call | solution.py:245
  137.4 3.1 %collective-permute-start.20 = (bf16[512,512]{1,0:T(8,128)(2,1)}, bf16[512,512]{1,0:T(8,128)(2,1)S(1)}, u32[]{:S(2)}, u32[]{:S(2)}) collective-permute-start(bf16[512,512]{1,0:T(8,128)(2,1)} %shard_map.91), channel_id=1, source_target_pairs={{0,1},{1,0},{2,3},{3,2},{4,5},{5,4},{6,7},{7,6},{8,9},{9,8},{10,11... | collective-permute-start | bytes 1572872 | tf_op jit(solution)/shard_map/ppermute | solution.py:32
  140.5 0.6 pad_add_fusion.1.starts
  141.0 3.8 %shard_map.88 = f32[512,512]{1,0:T(8,128)} custom-call(s32[2]{0:T(128)} %pad_add_fusion.1.starts, bf16[256,4096]{1,0:T(8,128)(2,1)} %collective-permute-done.11.upstream.whole, bf16[256,512]{1,0:T(8,128)(2,1)} %get-tuple-element.41.other, bf16[256,1536]{1,0:T(8,128)(2,1)} %copy-done.10, bf16[256,1536]{1,0:T(8,128)(2,1)} %collective-permute-done.14.rest_1_, ...), custom_call_target="tpu_custom_call" | custom-call | flops 1 | bytes 1 | tf_op jit(solution)/shard_map/pallas_call | solution.py:245
  144.8 3.7 %collective-permute-done.16.rest_0_ = bf16[256,1536]{1,0:T(8,128)(2,1)S(1)} collective-permute-done((bf16[256,1536]{1,0:T(8,128)(2,1)}, bf16[256,1536]{1,0:T(8,128)(2,1)S(1)}, u32[]{:S(2)}, u32[]{:S(2)}) %collective-permute-start.16) | collective-permute-done | bytes 786464 | tf_op jit(solution)/shard_map/ppermute | solution.py:28
  148.5 18.8 %collective-permute-done.17.rest_1_ = bf16[256,1536]{1,0:T(8,128)(2,1)S(1)} collective-permute-done((bf16[256,1536]{1,0:T(8,128)(2,1)}, bf16[256,1536]{1,0:T(8,128)(2,1)S(1)}, u32[]{:S(2)}, u32[]{:S(2)}) %collective-permute-start.17) | collective-permute-done | bytes 786464 | tf_op jit(solution)/shard_map/ppermute | solution.py:28
  167.4 0.9 copy-done.12
  168.3 3.6 %shard_map.89 = bf16[512,512]{1,0:T(8,128)(2,1)} custom-call(s32[2]{0:T(128)} %pad_add_fusion.starts, bf16[256,4096]{1,0:T(8,128)(2,1)} %copy-done, bf16[256,512]{1,0:T(8,128)(2,1)} %get-tuple-element.40.other, bf16[256,1536]{1,0:T(8,128)(2,1)} %copy-done.11, bf16[256,1536]{1,0:T(8,128)(2,1)} %copy-done.12, bf16[256,1536]{1,0:T(8,128)(2,1)} %collective-permute-done.18.rest_2_), custom_call_target="tpu_custom_call" | custom-call | flops 1 | bytes 1 | tf_op jit(solution)/shard_map/pallas_call | solution.py:245
  171.9 2.5 %collective-permute-start.19 = (bf16[512,512]{1,0:T(8,128)(2,1)}, bf16[512,512]{1,0:T(8,128)(2,1)S(1)}, u32[]{:S(2)}, u32[]{:S(2)}) collective-permute-start(bf16[512,512]{1,0:T(8,128)(2,1)} %shard_map.89), channel_id=1, source_target_pairs={{0,1},{1,0},{2,3},{3,2},{4,5},{5,4},{6,7},{7,6},{8,9},{9,8},{10,11... | collective-permute-start | bytes 1572872 | tf_op jit(solution)/shard_map/ppermute | solution.py:32
  174.4 3.8 %shard_map.90 = f32[512,512]{1,0:T(8,128)} custom-call(s32[2]{0:T(128)} %pad_add_fusion.1.starts, bf16[256,4096]{1,0:T(8,128)(2,1)} %copy-done, bf16[256,512]{1,0:T(8,128)(2,1)} %get-tuple-element.40.other, bf16[256,1536]{1,0:T(8,128)(2,1)} %copy-done.11, bf16[256,1536]{1,0:T(8,128)(2,1)} %copy-done.12, bf16[256,1536]{1,0:T(8,128)(2,1)} %collective-permute-done.18.rest_2_), custom_call_target="tpu_custom_call" | custom-call | flops 1 | bytes 1 | tf_op jit(solution)/shard_map/pallas_call | solution.py:245
  178.3 1.1 add_bitcast_fusion
  179.4 2.5 %shard_map.87 = bf16[256,4096]{1,0:T(8,128)(2,1)} custom-call(bf16[256,4096]{1,0:T(8,128)(2,1)} %collective-permute-done.12.source), custom_call_target="tpu_custom_call" | custom-call | flops 1 | bytes 1 | tf_op jit(solution)/shard_map/pallas_call | solution.py:245
  181.9 3.9 %collective-permute-done.19 = bf16[512,512]{1,0:T(8,128)(2,1)S(1)} collective-permute-done((bf16[512,512]{1,0:T(8,128)(2,1)}, bf16[512,512]{1,0:T(8,128)(2,1)S(1)}, u32[]{:S(2)}, u32[]{:S(2)}) %collective-permute-start.19) | collective-permute-done | bytes 524320 | tf_op jit(solution)/shard_map/ppermute | solution.py:32
  185.8 1.1 add_bitcast_fusion.1
  (49 shorter events, 0.6 us)
Async XLA Ops:
  0.6 30.2 %copy-start.15 = (bf16[1,256,4096]{2,1,0:T(8,128)(2,1)S(1)}, bf16[1,256,4096]{2,1,0:T(8,128)(2,1)}, u32[]{:S(2)}) copy-start(bf16[1,256,4096]{2,1,0:T(8,128)(2,1)} %param.4) | copy-start | bytes 6291460
  2.1 58.9 %copy-start.2 = (bf16[1024,512]{1,0:T(8,128)(2,1)}, bf16[1024,512]{1,0:T(8,128)(2,1)S(1)}, u32[]{:S(2)}) copy-start(bf16[1024,512]{1,0:T(8,128)(2,1)S(1)} %pad_maximum_fusion.6.rest_0_) | copy-start | bytes 3145732
  2.1 25.7 %collective-permute-start = (bf16[1024,512]{1,0:T(8,128)(2,1)S(1)}, bf16[1024,512]{1,0:T(8,128)(2,1)S(1)}, u32[]{:S(2)}, u32[]{:S(2)}) collective-permute-start(bf16[1024,512]{1,0:T(8,128)(2,1)S(1)} %pad_maximum_fusion.6.rest_0_), channel_id=1, source_target_pairs={{0,1},{1,0},{2,3},{3,2},{4,5},{5,4},{6,7},{7,6},{8,9},{9,8},{10,11... | collective-permute-start | bytes 3145736 | tf_op jit(solution)/shard_map/ppermute | solution.py:32
  5.9 24.9 %collective-permute-start.1 = (bf16[1024,512]{1,0:T(8,128)(2,1)S(1)}, bf16[1024,512]{1,0:T(8,128)(2,1)S(1)}, u32[]{:S(2)}, u32[]{:S(2)}) collective-permute-start(bf16[1024,512]{1,0:T(8,128)(2,1)S(1)} %pad_maximum_fusion.6.rest_0_), channel_id=1, source_target_pairs={{0,2},{1,3},{2,4},{3,5},{4,6},{5,7},{6,0},{7,1},{8,10},{9,11},{10,... | collective-permute-start | bytes 3145736 | tf_op jit(solution)/shard_map/ppermute | solution.py:28
  7.1 23.7 %collective-permute-start.2 = (bf16[1024,512]{1,0:T(8,128)(2,1)S(1)}, bf16[1024,512]{1,0:T(8,128)(2,1)S(1)}, u32[]{:S(2)}, u32[]{:S(2)}) collective-permute-start(bf16[1024,512]{1,0:T(8,128)(2,1)S(1)} %pad_maximum_fusion.6.rest_0_), channel_id=1, source_target_pairs={{0,6},{1,7},{2,0},{3,1},{4,2},{5,3},{6,4},{7,5},{8,14},{9,15},{10,... | collective-permute-start | bytes 3145736 | tf_op jit(solution)/shard_map/ppermute | solution.py:28
  27.7 37.6 %copy-start.7 = (bf16[1024,512]{1,0:T(8,128)(2,1)}, bf16[1024,512]{1,0:T(8,128)(2,1)S(1)}, u32[]{:S(2)}) copy-start(bf16[1024,512]{1,0:T(8,128)(2,1)S(1)} %collective-permute-done.rest_1_) | copy-start | bytes 3145732
  30.8 30.2 %copy-start.3 = (bf16[1024,512]{1,0:T(8,128)(2,1)}, bf16[1024,512]{1,0:T(8,128)(2,1)S(1)}, u32[]{:S(2)}) copy-start(bf16[1024,512]{1,0:T(8,128)(2,1)S(1)} %collective-permute-done.1.rest_2_) | copy-start | bytes 3145732
  30.8 30.2 %copy-start.4 = (bf16[1024,512]{1,0:T(8,128)(2,1)}, bf16[1024,512]{1,0:T(8,128)(2,1)S(1)}, u32[]{:S(2)}) copy-start(bf16[1024,512]{1,0:T(8,128)(2,1)S(1)} %collective-permute-done.2.rest_3_) | copy-start | bytes 3145732
  30.8 32.9 %collective-permute-start.3 = (bf16[256,4096]{1,0:T(8,128)(2,1)S(1)}, bf16[256,4096]{1,0:T(8,128)(2,1)S(1)}, u32[]{:S(2)}, u32[]{:S(2)}) collective-permute-start(bf16[256,4096]{1,0:T(8,128)(2,1)S(1)} %bitcast.26), channel_id=1, source_target_pairs={{0,8},{8,16},{16,24},{24,32},{32,40},{40,48},{48,56},{56,64},{64,7... | collective-permute-start | bytes 6291464 | tf_op jit(solution)/shard_map/ppermute | solution.py:18
  33.1 26.1 %collective-permute-start.4 = (bf16[1024,512]{1,0:T(8,128)(2,1)S(1)}, bf16[1024,512]{1,0:T(8,128)(2,1)S(1)}, u32[]{:S(2)}, u32[]{:S(2)}) collective-permute-start(bf16[1024,512]{1,0:T(8,128)(2,1)S(1)} %collective-permute-done.rest_1_), channel_id=1, source_target_pairs={{0,2},{1,3},{2,4},{3,5},{4,6},{5,7},{6,0},{7,1},{8,10},{9,11},{10,... | collective-permute-start | bytes 3145736 | tf_op jit(solution)/shard_map/ppermute | solution.py:28
  34.2 25.9 %collective-permute-start.5 = (bf16[1024,512]{1,0:T(8,128)(2,1)S(1)}, bf16[1024,512]{1,0:T(8,128)(2,1)S(1)}, u32[]{:S(2)}, u32[]{:S(2)}) collective-permute-start(bf16[1024,512]{1,0:T(8,128)(2,1)S(1)} %collective-permute-done.rest_1_), channel_id=1, source_target_pairs={{0,6},{1,7},{2,0},{3,1},{4,2},{5,3},{6,4},{7,5},{8,14},{9,15},{10,... | collective-permute-start | bytes 3145736 | tf_op jit(solution)/shard_map/ppermute | solution.py:28
  35.8 34.7 %collective-permute-start.6 = (bf16[512,512]{1,0:T(8,128)(2,1)S(1)}, bf16[512,512]{1,0:T(8,128)(2,1)}, u32[]{:S(2)}, u32[]{:S(2)}) collective-permute-start(bf16[512,512]{1,0:T(8,128)(2,1)S(1)} %slice.12), channel_id=1, source_target_pairs={{0,2},{1,3},{2,4},{3,5},{4,6},{5,7},{6,0},{7,1},{8,10},{9,11},{10,... | collective-permute-start | bytes 1572872 | tf_op jit(solution)/shard_map/ppermute | solution.py:28
  35.9 34.6 %collective-permute-start.7 = (bf16[512,512]{1,0:T(8,128)(2,1)S(1)}, bf16[512,512]{1,0:T(8,128)(2,1)}, u32[]{:S(2)}, u32[]{:S(2)}) collective-permute-start(bf16[512,512]{1,0:T(8,128)(2,1)S(1)} %slice.13), channel_id=1, source_target_pairs={{0,6},{1,7},{2,0},{3,1},{4,2},{5,3},{6,4},{7,5},{8,14},{9,15},{10,... | collective-permute-start | bytes 1572872 | tf_op jit(solution)/shard_map/ppermute | solution.py:28
  59.2 4.6 %copy-start.5 = (bf16[1024,512]{1,0:T(8,128)(2,1)}, bf16[1024,512]{1,0:T(8,128)(2,1)S(1)}, u32[]{:S(2)}) copy-start(bf16[1024,512]{1,0:T(8,128)(2,1)S(1)} %collective-permute-done.4.rest_4_) | copy-start | bytes 3145732
  60.1 21.7 %collective-permute-start.8 = (bf16[512,512]{1,0:T(8,128)(2,1)}, bf16[512,512]{1,0:T(8,128)(2,1)}, u32[]{:S(2)}, u32[]{:S(2)}) collective-permute-start(bf16[512,512]{1,0:T(8,128)(2,1)} %slice.16), channel_id=1, source_target_pairs={{0,2},{1,3},{2,4},{3,5},{4,6},{5,7},{6,0},{7,1},{8,10},{9,11},{10,... | collective-permute-start | bytes 1572872 | tf_op jit(solution)/shard_map/ppermute | solution.py:28
  60.1 3.7 %copy-start.6 = (bf16[1024,512]{1,0:T(8,128)(2,1)}, bf16[1024,512]{1,0:T(8,128)(2,1)S(1)}, u32[]{:S(2)}) copy-start(bf16[1024,512]{1,0:T(8,128)(2,1)S(1)} %collective-permute-done.5.rest_5_) | copy-start | bytes 3145732
  61.0 20.8 %collective-permute-start.9 = (bf16[512,512]{1,0:T(8,128)(2,1)}, bf16[512,512]{1,0:T(8,128)(2,1)}, u32[]{:S(2)}, u32[]{:S(2)}) collective-permute-start(bf16[512,512]{1,0:T(8,128)(2,1)} %slice.17), channel_id=1, source_target_pairs={{0,6},{1,7},{2,0},{3,1},{4,2},{5,3},{6,4},{7,5},{8,14},{9,15},{10,... | collective-permute-start | bytes 1572872 | tf_op jit(solution)/shard_map/ppermute | solution.py:28
  63.8 6.8 %copy-start = (bf16[256,4096]{1,0:T(8,128)(2,1)}, bf16[256,4096]{1,0:T(8,128)(2,1)S(1)}, u32[]{:S(2)}) copy-start(bf16[256,4096]{1,0:T(8,128)(2,1)S(1)} %collective-permute-done.3.inputs.whole) | copy-start | bytes 6291460
  63.8 25.9 %collective-permute-start.11 = (bf16[256,4096]{1,0:T(8,128)(2,1)}, bf16[256,4096]{1,0:T(8,128)(2,1)}, u32[]{:S(2)}, u32[]{:S(2)}) collective-permute-start(bf16[256,4096]{1,0:T(8,128)(2,1)} %bitcast.12), channel_id=1, source_target_pairs={{0,248},{8,0},{16,8},{24,16},{32,24},{40,32},{48,40},{56,48},{64,5... | collective-permute-start | bytes 6291464 | tf_op jit(solution)/shard_map/ppermute | solution.py:18
  89.3 1.9 copy-start.13
  89.3 24.7 %collective-permute-start.10 = (bf16[256,4096]{1,0:T(8,128)(2,1)}, bf16[256,4096]{1,0:T(8,128)(2,1)}, u32[]{:S(2)}, u32[]{:S(2)}) collective-permute-start(bf16[256,4096]{1,0:T(8,128)(2,1)} %get-tuple-element.35), channel_id=1, source_target_pairs={{0,8},{8,16},{16,24},{24,32},{32,40},{40,48},{48,56},{56,64},{64,7... | collective-permute-start | bytes 6291464 | tf_op jit(solution)/shard_map/ppermute | solution.py:18
  91.3 36.2 %collective-permute-start.13 = (bf16[256,1536]{1,0:T(8,128)(2,1)S(1)}, bf16[256,1536]{1,0:T(8,128)(2,1)S(1)}, u32[]{:S(2)}, u32[]{:S(2)}) collective-permute-start(bf16[256,1536]{1,0:T(8,128)(2,1)S(1)} %get-tuple-element.63), channel_id=1, source_target_pairs={{0,2},{1,3},{2,4},{3,5},{4,6},{5,7},{6,0},{7,1},{8,10},{9,11},{10,... | collective-permute-start | bytes 2359304 | tf_op jit(solution)/shard_map/ppermute | solution.py:28
  92.0 36.8 %collective-permute-start.14 = (bf16[256,1536]{1,0:T(8,128)(2,1)S(1)}, bf16[256,1536]{1,0:T(8,128)(2,1)}, u32[]{:S(2)}, u32[]{:S(2)}) collective-permute-start(bf16[256,1536]{1,0:T(8,128)(2,1)S(1)} %get-tuple-element.62), channel_id=1, source_target_pairs={{0,4},{1,5},{2,6},{3,7},{4,0},{5,1},{6,2},{7,3},{8,12},{9,13},{10,... | collective-permute-start | bytes 2359304 | tf_op jit(solution)/shard_map/ppermute | solution.py:28
  95.1 33.8 %collective-permute-start.15 = (bf16[256,1536]{1,0:T(8,128)(2,1)S(1)}, bf16[256,1536]{1,0:T(8,128)(2,1)}, u32[]{:S(2)}, u32[]{:S(2)}) collective-permute-start(bf16[256,1536]{1,0:T(8,128)(2,1)S(1)} %get-tuple-element.61), channel_id=1, source_target_pairs={{0,6},{1,7},{2,0},{3,1},{4,2},{5,3},{6,4},{7,5},{8,14},{9,15},{10,... | collective-permute-start | bytes 2359304 | tf_op jit(solution)/shard_map/ppermute | solution.py:28
  113.9 11.9 %copy-start.1 = (bf16[256,4096]{1,0:T(8,128)(2,1)S(1)}, bf16[256,4096]{1,0:T(8,128)(2,1)}, u32[]{:S(2)}) copy-start(bf16[256,4096]{1,0:T(8,128)(2,1)} %copy-done) | copy-start | bytes 6291460
  121.6 4.3 %copy-start.14 = (bf16[256,512]{1,0:T(8,128)(2,1)S(1)}, bf16[256,512]{1,0:T(8,128)(2,1)}, u32[]{:S(2)}) copy-start(bf16[256,512]{1,0:T(8,128)(2,1)} %get-tuple-element.40.other) | copy-start | bytes 786436
  121.6 57.8 %collective-permute-start.12 = (bf16[256,4096]{1,0:T(8,128)(2,1)}, bf16[256,4096]{1,0:T(8,128)(2,1)}, u32[]{:S(2)}, u32[]{:S(2)}) collective-permute-start(bf16[256,4096]{1,0:T(8,128)(2,1)} %shard_map.86), channel_id=1, source_target_pairs={{0,248},{8,0},{16,8},{24,16},{32,24},{40,32},{48,40},{56,48},{64,5... | collective-permute-start | bytes 6291464 | tf_op jit(solution)/shard_map/ppermute | solution.py:18
  127.5 6.2 %copy-start.10 = (bf16[256,1536]{1,0:T(8,128)(2,1)}, bf16[256,1536]{1,0:T(8,128)(2,1)S(1)}, u32[]{:S(2)}) copy-start(bf16[256,1536]{1,0:T(8,128)(2,1)S(1)} %collective-permute-done.13.rest_0_) | copy-start | bytes 2359300
  128.8 19.7 %collective-permute-start.16 = (bf16[256,1536]{1,0:T(8,128)(2,1)}, bf16[256,1536]{1,0:T(8,128)(2,1)S(1)}, u32[]{:S(2)}, u32[]{:S(2)}) collective-permute-start(bf16[256,1536]{1,0:T(8,128)(2,1)} %get-tuple-element.42), channel_id=1, source_target_pairs={{0,2},{1,3},{2,4},{3,5},{4,6},{5,7},{6,0},{7,1},{8,10},{9,11},{10,... | collective-permute-start | bytes 2359304 | tf_op jit(solution)/shard_map/ppermute | solution.py:28
  130.7 36.7 %collective-permute-start.17 = (bf16[256,1536]{1,0:T(8,128)(2,1)}, bf16[256,1536]{1,0:T(8,128)(2,1)S(1)}, u32[]{:S(2)}, u32[]{:S(2)}) collective-permute-start(bf16[256,1536]{1,0:T(8,128)(2,1)} %get-tuple-element.43), channel_id=1, source_target_pairs={{0,4},{1,5},{2,6},{3,7},{4,0},{5,1},{6,2},{7,3},{8,12},{9,13},{10,... | collective-permute-start | bytes 2359304 | tf_op jit(solution)/shard_map/ppermute | solution.py:28
  133.2 34.2 %collective-permute-start.18 = (bf16[256,1536]{1,0:T(8,128)(2,1)}, bf16[256,1536]{1,0:T(8,128)(2,1)}, u32[]{:S(2)}, u32[]{:S(2)}) collective-permute-start(bf16[256,1536]{1,0:T(8,128)(2,1)} %get-tuple-element.44), channel_id=1, source_target_pairs={{0,6},{1,7},{2,0},{3,1},{4,2},{5,3},{6,4},{7,5},{8,14},{9,15},{10,... | collective-permute-start | bytes 2359304 | tf_op jit(solution)/shard_map/ppermute | solution.py:28
  137.4 40.9 %collective-permute-start.20 = (bf16[512,512]{1,0:T(8,128)(2,1)}, bf16[512,512]{1,0:T(8,128)(2,1)S(1)}, u32[]{:S(2)}, u32[]{:S(2)}) collective-permute-start(bf16[512,512]{1,0:T(8,128)(2,1)} %shard_map.91), channel_id=1, source_target_pairs={{0,1},{1,0},{2,3},{3,2},{4,5},{5,4},{6,7},{7,6},{8,9},{9,8},{10,11... | collective-permute-start | bytes 1572872 | tf_op jit(solution)/shard_map/ppermute | solution.py:32
  148.5 18.8 %copy-start.11 = (bf16[256,1536]{1,0:T(8,128)(2,1)}, bf16[256,1536]{1,0:T(8,128)(2,1)S(1)}, u32[]{:S(2)}) copy-start(bf16[256,1536]{1,0:T(8,128)(2,1)S(1)} %collective-permute-done.16.rest_0_) | copy-start | bytes 2359300
  167.4 0.9 copy-start.12
  171.9 6.4 %copy-start.8 = (f32[512,512]{1,0:T(8,128)S(1)}, f32[512,512]{1,0:T(8,128)}, u32[]{:S(2)}) copy-start(f32[512,512]{1,0:T(8,128)} %shard_map.88) | copy-start | bytes 3145732
  171.9 13.9 %collective-permute-start.19 = (bf16[512,512]{1,0:T(8,128)(2,1)}, bf16[512,512]{1,0:T(8,128)(2,1)S(1)}, u32[]{:S(2)}, u32[]{:S(2)}) collective-permute-start(bf16[512,512]{1,0:T(8,128)(2,1)} %shard_map.89), channel_id=1, source_target_pairs={{0,1},{1,0},{2,3},{3,2},{4,5},{5,4},{6,7},{7,6},{8,9},{9,8},{10,11... | collective-permute-start | bytes 1572872 | tf_op jit(solution)/shard_map/ppermute | solution.py:32
  179.4 6.4 %copy-start.9 = (f32[512,512]{1,0:T(8,128)S(1)}, f32[512,512]{1,0:T(8,128)}, u32[]{:S(2)}) copy-start(f32[512,512]{1,0:T(8,128)} %shard_map.90) | copy-start | bytes 3145732
